TPU v7x, 32 devices: a whole 2x2x4 slice. The times are simulated.
32 devices in a mesh: grp: 2 (over x), aux: 16 (over z, y, core).
Axes of the slice: x: 2, y: 2, z: 4, core: 2. Of those that a mesh axis runs over, the one named last changes fastest.
Arguments:
- raw_tiles: bfloat16 [32, 32, 32, 6, 128], P(('grp', 'aux')), parts along dimension 0, may hold values from -1.25 to 1.25
- metric: bfloat16 [32, 16], P('grp'), parts along dimension 0, may hold values from -2 to 2
- owner_map: int32 [64], P('grp'), parts along dimension 0, may hold values from 0 to 31, as said below
- counts: int32 [64], P(('grp', 'aux')), parts along dimension 0, may hold values from 1 to 5, as said below
Outputs:
- exchange_blocks: float32 [64, 768, 768], P(('grp', 'aux')), parts along dimension 0
There are 2 independent parts, one for each index of `grp`. A program takes and returns all parts, laid end to end along the dimension named above; each array names one. Nothing has to cross between parts.
Inputs may be any that keep to these rules, and one draw needn't show every extreme that they name: Slots at or beyond counts[o] are ignored; for every d, the two blocks whose positions are 2 d and 2 d + 1 have counts summing to at most 6, and some such pair reaches 6; 5 is reached by some block. `owner_map`: every position 0 to 31 once.
All inputs are finite; a program needn't handle non-finite values.
Results may differ from a plain program's by a relative error of at most 0.0027.
Values may be sent and summed in bfloat16 or wider, within the bound.
No kernel may reach another device: no remote copies, remote signals or barrier semaphores. Data moves between devices by JAX's collectives and lax.ppermute only.
A program may use at most 64 MiB of HBM per device.

v0:
```python
import jax
import jax.numpy as jnp
from jax import lax
from jax.sharding import PartitionSpec as P


def block_exchange(arrived_block, metric, live_slots):
    aux_total, orbitals, domain, tile_width = arrived_block.shape
    slot_ids = jnp.arange(domain, dtype=jnp.int32)
    masked = jnp.where(
        (slot_ids < live_slots)[None, None, :, None], arrived_block, jnp.zeros_like(arrived_block)
    )
    fitted = jnp.dot(
        metric,
        masked.reshape(aux_total, orbitals * domain * tile_width),
        preferred_element_type=jnp.float32,
    )
    fitted = fitted.astype(jnp.bfloat16).reshape(aux_total * orbitals, domain * tile_width)

    def row_tile(tile_index, stored):
        row_part = lax.dynamic_slice_in_dim(fitted, tile_index * tile_width, tile_width, 1)
        product = lax.dot_general(
            row_part, fitted, (((0,), (0,)), ((), ())), preferred_element_type=jnp.float32
        )
        return lax.dynamic_update_slice_in_dim(stored, product, tile_index * tile_width, 0)

    initial = jnp.zeros((domain * tile_width, domain * tile_width), jnp.float32)
    return lax.fori_loop(0, live_slots, row_tile, initial)


def shards(raw_tiles, metric, owner_map, counts):
    my_index = lax.axis_index("aux")
    per_device = counts.shape[0]
    aux_local, block_total, orbitals, domain, tile_width = raw_tiles.shape
    all_counts = lax.all_gather(counts, "aux", axis=0, tiled=True)
    block_ids = jnp.arange(block_total, dtype=jnp.int32)
    held_at = jnp.zeros((block_total,), jnp.int32).at[owner_map].set(block_ids)
    my_positions = my_index * per_device + jnp.arange(per_device, dtype=jnp.int32)
    my_blocks = held_at[my_positions]
    finished = []
    outgoing = jnp.take(raw_tiles, held_at, axis=1)
    arrived = lax.all_to_all(outgoing, "aux", split_axis=1, concat_axis=0, tiled=True)
    for within in range(per_device):
        finished.append(block_exchange(arrived[:, within], metric, all_counts[my_blocks[within]]))
    return jnp.stack(finished)


def solution(mesh):
    in_specs = (
        P(("grp", "aux"), None, None, None, None),
        P("grp", None),
        P("grp"),
        P(("grp", "aux")),
    )
    out_specs = P(("grp", "aux"), None, None)
    return jax.shard_map(shards, mesh=mesh, in_specs=in_specs, out_specs=out_specs, check_vma=False)
```

profile of v0, /device:TPU:0, one launch (start us, length us, event | category | flops | bytes accessed | tf_op | source)
XLA Modules:
  0.0 83.2 jit_solution(18311362938140064738)
XLA Ops:
  0.0 0.8 compare_select_fusion.2
  0.8 0.7 scatter_custom_fusion
  1.5 0.9 %gather_fusion.1 = bf16[32,32,6,128]{3,1,2,0:T(8,128)(2,1)S(1)} fusion(bf16[32,32,6,128]{3,1,2,0:T(8,128)(2,1)S(1)} %bitcast.30, s32[1024]{0:T(1024)S(1)} %pad_clamp_fusion), kind=kCustom, calls=%fused_computation.1 | custom fusion | bytes 3145856 | tf_op jit(solution)/shard_map/jit(_take)/gather | solution.py:41
  2.4 1.4 %bitcast_select_fusion = bf16[1,32,32,6,128]{4,2,3,0,1:T(8,128)(2,1)} fusion(bf16[32,32,6,128]{3,1,2,0:T(8,128)(2,1)S(1)} %gather_fusion.1, pred[32]{0:T(512)(128)(4,1)S(1)} %compare_and_fusion), kind=kLoop, calls=%fused_computation.14 | loop fusion | flops 786432 | bytes 3145760 | tf_op jit(solution)/shard_map/jit(_take)/select_n | solution.py:41
  3.7 7.5 %all-to-all-start = ((bf16[1,32,32,6,128]{4,2,3,0,1:T(8,128)(2,1)}), bf16[1,32,32,6,128]{4,2,3,0,1:T(8,128)(2,1)S(1)}, u32[]{:S(2)}, u32[]{:S(2)}) async-start(bf16[1,32,32,6,128]{4,2,3,0,1:T(8,128)(2,1)} %bitcast_select_fusion), calls=%async_computation | async-start | bytes 3145728 | tf_op jit(solution)/shard_map/all_to_all | solution.py:42
  11.3 0.6 gather_fusion
  11.9 0.6 fusion.19
  15.2 0.6 dynamic-slice
  18.0 31.2 %all-reduce = s32[32]{0:T(128)S(1)} all-reduce(s32[32]{0:T(128)S(1)} %dynamic-update-slice), channel_id=1, replica_groups=mesh['grp'=2,'aux'=16] {'aux'}, use_global_device_ids=true, to_apply=%add | all-reduce | flops 32 | bytes 256
  49.3 0.7 fusion.18
  49.9 0.6 iota_compare_fusion
  50.7 0.6 iota_compare_fusion.1
  51.4 1.2 %fusion.17 = (bf16[16,1,32,6,128]{4,2,3,1,0:T(8,128)(2,1)S(1)}, bf16[16,1,32,6,128]{4,2,3,1,0:T(8,128)(2,1)}) fusion(bf16[16,2,32,6,128]{4,2,3,1,0:T(8,128)(2,1)S(1)} %bitcast.33), kind=kLoop, calls=%fused_computation.34 | loop fusion | bytes 3145728 | tf_op jit(solution)/shard_map/slice | solution.py:44
  52.6 0.3 copy.9
  52.9 0.8 %squeeze.20 = bf16[16,24576]{1,0:T(8,128)(2,1)S(1)} reshape(bf16[16,1,32,6,128]{4,3,2,0,1:T(8,128)(2,1)S(1)} %copy.9) | data formatting | bytes 1572864 | tf_op jit(solution)/shard_map/squeeze | solution.py:44
  53.8 1.3 %fusion.4 = bf16[16,24576]{1,0:T(8,128)(2,1)} fusion(bf16[16,16]{1,0:T(8,128)(2,1)S(1)} %copy-done.1, bf16[16,24576]{1,0:T(8,128)(2,1)S(1)} %squeeze.20, pred[24576]{0:T(1024)(128)(4,1)S(1)} %broadcast_in_dim.41), kind=kOutput, calls=%fused_computation.11 | convolution fusion | flops 13369344 | bytes 1597952 | tf_op jit(solution)/shard_map/dot_general | solution.py:13
  55.1 1.5 %reshape.52 = bf16[512,768]{1,0:T(8,128)(2,1)S(1)} reshape(bf16[16,24576]{1,0:T(8,128)(2,1)} %fusion.4) | data formatting | bytes 1572864 | tf_op jit(solution)/shard_map/reshape | solution.py:18
  56.6 1.5 %copy.10 = bf16[16,1,32,6,128]{4,3,2,0,1:T(8,128)(2,1)S(1)} copy(bf16[16,1,32,6,128]{4,2,3,1,0:T(8,128)(2,1)} %get-tuple-element.70) | data formatting | bytes 1572864
  58.0 1.7 %squeeze.23 = bf16[16,24576]{1,0:T(8,128)(2,1)} reshape(bf16[16,1,32,6,128]{4,3,2,0,1:T(8,128)(2,1)S(1)} %copy.10) | data formatting | bytes 1572864 | tf_op jit(solution)/shard_map/squeeze | solution.py:44
  59.8 2.4 %fusion.5 = bf16[16,24576]{1,0:T(8,128)(2,1)} fusion(bf16[16,16]{1,0:T(8,128)(2,1)S(1)} %copy-done.1, bf16[16,24576]{1,0:T(8,128)(2,1)} %squeeze.23, pred[24576]{0:T(1024)(128)(4,1)S(1)} %broadcast_in_dim.47), kind=kOutput, calls=%fused_computation.12 | convolution fusion | flops 13369344 | bytes 1597952 | tf_op jit(solution)/shard_map/dot_general | solution.py:13
  62.2 1.5 %reshape.53 = bf16[512,768]{1,0:T(8,128)(2,1)S(1)} reshape(bf16[16,24576]{1,0:T(8,128)(2,1)} %fusion.5) | data formatting | bytes 1572864 | tf_op jit(solution)/shard_map/reshape | solution.py:18
  63.7 1.6 %broadcast.69.clone = f32[768,768]{1,0:T(8,128)} broadcast(f32[]{:T(128)} %constant.25.clone.1), dimensions={} | broadcast | bytes 2359300 | tf_op jit(solution)/shard_map/broadcast.5
  65.2 4.0 %while.21 = (s32[]{:T(128)}, f32[768,768]{1,0:T(8,128)}, s32[]{:T(128)}, bf16[512,768]{1,0:T(8,128)(2,1)S(1)}, s32[]{:T(128)}, /*index=5*/s32[]{:T(128)}, s32[]{:T(128)}, s32[]{:T(128)}) while((s32[]{:T(128)}, f32[768,768]{1,0:T(8,128)}, s32[]{:T(128)}, bf16[512,768]{1,0:T(8,128)(2,1)S(1)}, s32[]{:T(128)}, /*index=5*/s32[]{:T(128)}, ...), condition=%wide.region_4.5_spmd, body=%wide.region_3.4_spmd.sunk | while | flops 100663304 | bytes 1311875 | solution.py:28
  65.9 1.1 %convolution_dynamic-update-slice_fusion.5 = f32[768,768]{1,0:T(8,128)} fusion(f32[768,768]{1,0:T(8,128)} %get-tuple-element.136, s32[]{:T(128)S(6)} %select_n.76, bf16[512,768]{1,0:T(8,128)(2,1)S(1)} %get-tuple-element.146), kind=kOutput, calls=%fused_computation.6.clone.1 | convolution fusion | flops 100663296 | bytes 1311744 | tf_op jit(solution)/shard_map/while/body/dot_general | solution.py:22
  67.6 1.1 %convolution_dynamic-update-slice_fusion.5 = f32[768,768]{1,0:T(8,128)} fusion(f32[768,768]{1,0:T(8,128)} %get-tuple-element.136, s32[]{:T(128)S(6)} %select_n.76, bf16[512,768]{1,0:T(8,128)(2,1)S(1)} %get-tuple-element.146), kind=kOutput, calls=%fused_computation.6.clone.1 | convolution fusion | flops 100663296 | bytes 1311744 | tf_op jit(solution)/shard_map/while/body/dot_general | solution.py:22
  69.3 1.6 %broadcast.69.clone.1 = f32[768,768]{1,0:T(8,128)} broadcast(f32[]{:T(128)} %constant.25.clone.1), dimensions={} | broadcast | bytes 2359300 | tf_op jit(solution)/shard_map/broadcast.5
  70.8 7.5 %while.20 = (s32[]{:T(128)}, f32[768,768]{1,0:T(8,128)}, s32[]{:T(128)}, bf16[512,768]{1,0:T(8,128)(2,1)S(1)}, s32[]{:T(128)}, /*index=5*/s32[]{:T(128)}, s32[]{:T(128)}, s32[]{:T(128)}) while((s32[]{:T(128)}, f32[768,768]{1,0:T(8,128)}, s32[]{:T(128)}, bf16[512,768]{1,0:T(8,128)(2,1)S(1)}, s32[]{:T(128)}, /*index=5*/s32[]{:T(128)}, ...), condition=%wide.region_2.3_spmd, body=%wide.region_1.2_spmd.sunk | while | flops 100663304 | bytes 1311875 | solution.py:28
  71.5 1.0 %convolution_dynamic-update-slice_fusion.4 = f32[768,768]{1,0:T(8,128)} fusion(f32[768,768]{1,0:T(8,128)} %get-tuple-element.160, s32[]{:T(128)S(6)} %select_n.75, bf16[512,768]{1,0:T(8,128)(2,1)S(1)} %get-tuple-element.170), kind=kOutput, calls=%fused_computation.3.clone.1 | convolution fusion | flops 100663296 | bytes 1311744 | tf_op jit(solution)/shard_map/while/body/dot_general | solution.py:22
  73.2 1.1 %convolution_dynamic-update-slice_fusion.4 = f32[768,768]{1,0:T(8,128)} fusion(f32[768,768]{1,0:T(8,128)} %get-tuple-element.160, s32[]{:T(128)S(6)} %select_n.75, bf16[512,768]{1,0:T(8,128)(2,1)S(1)} %get-tuple-element.170), kind=kOutput, calls=%fused_computation.3.clone.1 | convolution fusion | flops 100663296 | bytes 1311744 | tf_op jit(solution)/shard_map/while/body/dot_general | solution.py:22
  74.9 1.0 %convolution_dynamic-update-slice_fusion.4 = f32[768,768]{1,0:T(8,128)} fusion(f32[768,768]{1,0:T(8,128)} %get-tuple-element.160, s32[]{:T(128)S(6)} %select_n.75, bf16[512,768]{1,0:T(8,128)(2,1)S(1)} %get-tuple-element.170), kind=kOutput, calls=%fused_computation.3.clone.1 | convolution fusion | flops 100663296 | bytes 1311744 | tf_op jit(solution)/shard_map/while/body/dot_general | solution.py:22
  76.6 1.1 %convolution_dynamic-update-slice_fusion.4 = f32[768,768]{1,0:T(8,128)} fusion(f32[768,768]{1,0:T(8,128)} %get-tuple-element.160, s32[]{:T(128)S(6)} %select_n.75, bf16[512,768]{1,0:T(8,128)(2,1)S(1)} %get-tuple-element.170), kind=kOutput, calls=%fused_computation.3.clone.1 | convolution fusion | flops 100663296 | bytes 1311744 | tf_op jit(solution)/shard_map/while/body/dot_general | solution.py:22
  78.3 4.9 %pad_maximum_fusion = f32[2,768,768]{2,1,0:T(8,128)} fusion(f32[1,768,768]{2,1,0:T(8,128)} %bitcast.32, f32[1,768,768]{2,1,0:T(8,128)} %bitcast.31), kind=kLoop, calls=%fused_computation.13 | loop fusion | flops 1179648 | bytes 9437184 | tf_op jit(solution)/shard_map/stack | solution.py:45
  (21 shorter events, 0.5 us)
Async XLA Ops:
  0.0 1.5 %copy-start = (bf16[1,32,32,6,128]{4,2,3,1,0:T(8,128)(2,1)S(1)}, bf16[1,32,32,6,128]{4,2,3,1,0:T(8,128)(2,1)}, u32[]{:S(2)}) copy-start(bf16[1,32,32,6,128]{4,2,3,1,0:T(8,128)(2,1)} %param.8) | copy-start | bytes 4718596
  3.7 11.5 %copy-start.3 = (u32[32]{0:T(128)S(1)}, u32[32]{0:T(128)}, u32[]{:S(2)}) copy-start(u32[32]{0:T(128)} %constant.52) | copy-start | bytes 388
  3.7 14.1 %copy-start.2 = (s32[2]{0:T(128)S(1)}, s32[2]{0:T(128)}, u32[]{:S(2)}) copy-start(s32[2]{0:T(128)} %param.11) | copy-start | bytes 28
  3.7 47.7 %all-to-all-start = ((bf16[1,32,32,6,128]{4,2,3,0,1:T(8,128)(2,1)}), bf16[1,32,32,6,128]{4,2,3,0,1:T(8,128)(2,1)S(1)}, u32[]{:S(2)}, u32[]{:S(2)}) async-start(bf16[1,32,32,6,128]{4,2,3,0,1:T(8,128)(2,1)} %bitcast_select_fusion), calls=%async_computation | async-start | bytes 3145728 | tf_op jit(solution)/shard_map/all_to_all | solution.py:42
  52.6 1.2 %copy-start.1 = (bf16[16,16]{1,0:T(8,128)(2,1)S(1)}, bf16[16,16]{1,0:T(8,128)(2,1)}, u32[]{:S(2)}) copy-start(bf16[16,16]{1,0:T(8,128)(2,1)} %param.9) | copy-start | bytes 1540
where the time goes:
time: 83.7 us; the launch traced here: 83.2 us
  blocking collectives  31.2 us (37%)
  local copies, waits for them, and re-layouts  16.2 us (19%)
  matrix products  10 us (12%)
  other arithmetic  8.29 us (10%)
  starting transfers between devices  7.52 us (9%)
  loops' own time  5.16 us (6%)
  between operations  4.82 us (6%)
    unnamed x1, blocking collectives  31.2 us
    all_to_all x1, starting transfers between devices, shards(): lax.all_to_all(outgoing, 'aux', split_axis=1, concat_axis=0, tiled=True)  7.52 us
    dot_general x6, matrix products, row_tile(): lax.dot_general(row_part, fitted, (((0,), (0,)), ((), ())), preferred_ele...  6.35 us
    another operation x2, loops' own time, block_exchange(): return lax.fori_loop(0, live_slots, row_tile, initial)  5.16 us
    another operation x1, other arithmetic, shards(): return jnp.stack(finished)  4.87 us
    dot_general x2, matrix products, block_exchange(): jnp.dot(metric, masked.reshape(aux_total, orbitals * domain * tile_width)...  3.65 us
    another operation x2, local copies, waits for them, and re-layouts  3.13 us
    reshape x2, local copies, waits for them, and re-layouts, block_exchange(): fitted.astype(jnp.bfloat16)  2.98 us
  transfers between devices with their start and end apart: 1, of which 0 were waited for; matrix products, arithmetic and copies ran while one was open for 5% of the time, Pallas kernels for 0%

commit v1 on v0

v1 whole, which is shorter than its diff:
```python
import functools

import jax
import jax.numpy as jnp
from jax import lax
from jax.experimental import pallas as pl
from jax.experimental.pallas import tpu as pltpu
from jax.sharding import PartitionSpec as P

ANY = pl.BlockSpec(memory_space=pl.ANY)
SMEM = pl.BlockSpec(memory_space=pltpu.SMEM)


def pack_kernel(chips, owner_ref, mine_ref, side_ref, *refs):
    half = chips // 2
    own_raw, peer_raw = refs[2 * (half - 1) : 2 * half]
    got, swapped = refs[: half - 1], refs[half - 1 : 2 * half - 2]
    outs = refs[2 * half : 3 * half]
    info_ref = refs[3 * half]
    held, table, small_sem, sems = refs[3 * half + 1 :]
    blocks, slots = own_raw.shape[0], own_raw.shape[1]
    me = lax.axis_index("aux")
    chip, core = me // 2, lax.rem(me, 2)

    rows = [(mine_ref, 0), (side_ref, 1)]
    for k in range(1, half):
        rows += [(got[k - 1], 2 * k), (swapped[k - 1], 2 * k + 1)]
    for n, (ref, row) in enumerate(rows):
        pltpu.make_async_copy(ref, table.at[row], small_sem.at[n]).start()

    def place(o, carry):
        held[owner_ref[o]] = o
        return carry

    lax.fori_loop(0, blocks, place, 0)
    for n, (ref, row) in enumerate(rows):
        pltpu.make_async_copy(ref, table.at[row], small_sem.at[n]).wait()

    def live(block):
        m = lax.bitwise_xor(block // 4, chip)
        parity = jnp.where(m >= 2, lax.bitwise_xor(lax.rem(m, 2), core), lax.rem(m, 2))
        return table[(m // 2) * 2 + parity, lax.rem(block, 4)]

    def pair(dest):
        first, second = held[2 * dest], held[2 * dest + 1]
        return first, second, live(first)

    def send(dest, target, sem):
        first, second, count = pair(dest)
        for j in range(slots):
            from_first = j < count
            block = jnp.where(from_first, first, second)
            slot = jnp.where(from_first, j, slots - 1 - j)
            pltpu.make_async_copy(own_raw.at[block, slot], target.at[core, j], sem).start()
            pltpu.make_async_copy(peer_raw.at[block, slot], target.at[1 - core, j], sem).start()

    for k in range(half - 1, 0, -1):
        there = lax.bitwise_xor(chip, 2 * k + core)
        for f in range(2):
            dest = 2 * there + (core if f == 0 else 1 - core)
            send(dest, outs[k].at[f], sems.at[k])
    send(2 * lax.bitwise_xor(chip, 1) + core, outs[0], sems.at[0])

    first, second, count = pair(me)
    info_ref[0] = first
    info_ref[1] = second
    info_ref[2] = count
    info_ref[3] = live(second)
    for k in range(half):
        pltpu.make_async_copy(outs[k], outs[k], sems.at[k]).wait()


def exchange_kernel(chips, info_ref, metric_ref, *refs):
    half = chips // 2
    own_raw, peer_raw, side = refs[:3]
    got, swapped = refs[3 : half + 2], refs[half + 2 : 2 * half + 1]
    out_ref, gathered, rows, stage, in_sems, out_sems = refs[2 * half + 1 :]
    aux, slots, orbitals, width = gathered.shape
    me = lax.axis_index("aux")
    chip, core = me // 2, lax.rem(me, 2)
    first, second, first_live, second_live = (info_ref[n] for n in range(4))

    def chip_rows(m):
        return gathered.at[pl.ds(2 * lax.bitwise_xor(chip, m), 2)]

    copies = [pltpu.make_async_copy(side, chip_rows(1), in_sems.at[0])]
    for k in range(1, half):
        copies.append(pltpu.make_async_copy(got[k - 1].at[0], chip_rows(2 * k + core), in_sems.at[2 * k]))
        copies.append(pltpu.make_async_copy(swapped[k - 1].at[1], chip_rows(2 * k + 1 - core), in_sems.at[2 * k + 1]))
    for copy in copies:
        copy.start()
    for j in range(slots):
        from_first = j < first_live
        block = jnp.where(from_first, first, second)
        slot = jnp.where(from_first, j, slots - 1 - j)
        pltpu.make_async_copy(own_raw.at[block, slot], gathered.at[2 * chip + core, j], in_sems.at[1]).start()
        pltpu.make_async_copy(peer_raw.at[block, slot], gathered.at[2 * chip + 1 - core, j], in_sems.at[1]).start()

    group = 16
    wide = aux * group
    pick = (lax.broadcasted_iota(jnp.int32, (wide, aux), 0) // group == lax.broadcasted_iota(jnp.int32, (wide, aux), 1)).astype(jnp.bfloat16)
    tall = jnp.dot(pick, metric_ref[...], preferred_element_type=jnp.float32).astype(jnp.bfloat16)
    spread = lax.dot_general(tall, pick, (((1,), (1,)), ((), ())), preferred_element_type=jnp.float32)
    same = lax.rem(lax.broadcasted_iota(jnp.int32, (wide, wide), 0), group) == lax.rem(lax.broadcasted_iota(jnp.int32, (wide, wide), 1), group)
    factor = jnp.where(same, spread, 0.0).astype(jnp.bfloat16)

    for copy in copies:
        copy.wait()
    pltpu.make_async_copy(chip_rows(0), chip_rows(0), in_sems.at[1]).wait()

    for part in range(orbitals // group):
        columns = [gathered[:, s, part * group : (part + 1) * group, :].reshape(wide, width) for s in range(slots)]
        fitted = jnp.dot(factor, jnp.concatenate(columns, axis=1), preferred_element_type=jnp.float32)
        rows[part * wide : (part + 1) * wide, :] = fitted.astype(jnp.bfloat16)

    def span(n):
        return slice(n * width, (n + 1) * width)

    for s in range(slots):
        product = lax.dot_general(rows[:, span(s)], rows[...], (((0,), (0,)), ((), ())), preferred_element_type=jnp.float32)
        for which, count in ((0, first_live), (1, second_live)):
            row = s if which == 0 else slots - 1 - s
            for t in range(slots):
                column = t if which == 0 else slots - 1 - t
                stage[which, span(row), span(column)] = jnp.where(max(row, column) < count, product[:, span(t)], 0.0)
            pltpu.make_async_copy(stage.at[which, span(row)], out_ref.at[which, span(row)], out_sems.at[which, row]).start()
    for which in range(2):
        for row in range(slots):
            pltpu.make_async_copy(stage.at[which, span(row)], out_ref.at[which, span(row)], out_sems.at[which, row]).wait()


def shards(devices, raw_tiles, metric, owner_map, counts):
    chips = devices // 2
    half = chips // 2
    _, blocks, orbitals, slots, width = raw_tiles.shape
    core = lax.rem(lax.axis_index("aux"), 2)
    raw = raw_tiles[0].transpose(0, 2, 1, 3)

    def swap(x):
        return lax.ppermute(x, "aux", [(i, i ^ 1) for i in range(devices)])

    def hop(x, k):
        def target(i):
            away = 1 if k == 0 else 2 * k + i % 2
            return (i // 2 ^ away) * 2 + i % 2

        return lax.ppermute(x, "aux", [(i, target(i)) for i in range(devices)])

    other = swap(counts)
    lane = lax.broadcasted_iota(jnp.int32, (128,), 0)
    mine = jnp.where(lane // 2 == core, jnp.where(lane % 2 == 0, counts[0], counts[1]), jnp.where(lane % 2 == 0, other[0], other[1]))
    peer_raw = swap(raw)
    got = [hop(mine, k) for k in range(half)]
    swapped = [swap(x) for x in got[1:]]

    packed = [jax.ShapeDtypeStruct((2, slots, orbitals, width), raw.dtype)]
    packed += [jax.ShapeDtypeStruct((2, 2, slots, orbitals, width), raw.dtype)] * (half - 1)
    *outgoing, info = pl.pallas_call(
        functools.partial(pack_kernel, chips),
        out_shape=packed + [jax.ShapeDtypeStruct((4,), jnp.int32)],
        in_specs=[SMEM] + [ANY] * (2 * half + 2),
        out_specs=[ANY] * half + [SMEM],
        scratch_shapes=[
            pltpu.SMEM((blocks,), jnp.int32),
            pltpu.SMEM((chips, 128), jnp.int32),
            pltpu.SemaphoreType.DMA((chips,)),
            pltpu.SemaphoreType.DMA((half,)),
        ],
        name="pack",
    )(owner_map, mine, got[0], *got[1:], *swapped, raw, peer_raw)

    arrived = [hop(x, k) for k, x in enumerate(outgoing)]
    crossed = [swap(x) for x in arrived[1:]]

    return pl.pallas_call(
        functools.partial(exchange_kernel, chips),
        out_shape=jax.ShapeDtypeStruct((2, slots * width, slots * width), jnp.float32),
        in_specs=[SMEM, pl.BlockSpec(memory_space=pltpu.VMEM)] + [ANY] * (2 * half + 1),
        out_specs=ANY,
        scratch_shapes=[
            pltpu.VMEM((devices, slots, orbitals, width), raw.dtype),
            pltpu.VMEM((devices * orbitals, slots * width), raw.dtype),
            pltpu.VMEM((2, slots * width, slots * width), jnp.float32),
            pltpu.SemaphoreType.DMA((chips,)),
            pltpu.SemaphoreType.DMA((2, slots)),
        ],
        compiler_params=pltpu.CompilerParams(vmem_limit_bytes=40 * 1024 * 1024),
        name="exchange",
    )(info, metric, raw, peer_raw, arrived[0], *arrived[1:], *crossed)


def solution(mesh):
    in_specs = (
        P(("grp", "aux"), None, None, None, None),
        P("grp", None),
        P("grp"),
        P(("grp", "aux")),
    )
    out_specs = P(("grp", "aux"), None, None)
    body = functools.partial(shards, mesh.shape["aux"])
    return jax.shard_map(body, mesh=mesh, in_specs=in_specs, out_specs=out_specs, check_vma=False)
```

time: 83.7 us -> 76.2 us (0.910)
  the two profiles are of different devices: /device:TPU:0 before, /device:TPU:16 now
where the time goes in v1:
time: 76.2 us; the launch traced here: 76 us
  Pallas kernels  28.9 us (38%)
  waiting for transfers between devices  26.7 us (35%)
  starting transfers between devices  11.9 us (16%)
  local copies, waits for them, and re-layouts  5.82 us (8%)
  other arithmetic  2.54 us (3%)
    ppermute x8, waiting for transfers between devices, hop(): return lax.ppermute(x, 'aux', [(i, target(i)) for i in range(devices)])  24.1 us
    pallas_call x1, Pallas kernels, shards(): pl.pallas_call(functools.partial(pack_kernel, chips), out_shape=packed +...  24 us
    ppermute x8, starting transfers between devices, hop(): return lax.ppermute(x, 'aux', [(i, target(i)) for i in range(devices)])  9.95 us
    pallas_call x1, Pallas kernels, shards(): pl.pallas_call(functools.partial(exchange_kernel, chips), out_shape=jax.S...  4.94 us
    unnamed x26, local copies, waits for them, and re-layouts  3.77 us
    ppermute x8, waiting for transfers between devices, swap(): return lax.ppermute(x, 'aux', [(i, i ^ 1) for i in range(devices)])  2.6 us
    select_n x1, other arithmetic, shards(): jnp.where(lane // 2 == core, jnp.where(lane % 2 == 0, counts[0], counts[1...  2.54 us
    ppermute x8, starting transfers between devices, swap(): return lax.ppermute(x, 'aux', [(i, i ^ 1) for i in range(devices)])  1.9 us
  transfers between devices with their start and end apart: 16, of which 7 were waited for; matrix products, arithmetic and copies ran while one was open for 6% of the time, Pallas kernels for 0%

profile of v1, /device:TPU:16, one launch (start us, length us, event | category | flops | bytes accessed | tf_op | source)
XLA Modules:
  0.0 76.0 jit_solution(8009748412383387396)
XLA Ops:
  0.0 0.0 collective-permute-start.8
  0.0 0.5 collective-permute-start
  0.5 1.4 %fusion = (s32[1]{0:T(128)}, s32[1]{0:T(128)}) fusion(s32[2]{0:T(128)} %param.7), kind=kLoop, calls=%fused_computation.8 | loop fusion | bytes 16 | tf_op jit(solution)/shard_map/slice | solution.py:151
  1.9 1.7 %collective-permute-done = s32[2]{0:T(128)S(1)} collective-permute-done((s32[2]{0:T(128)}, s32[2]{0:T(128)S(1)}, u32[]{:S(2)}, u32[]{:S(2)}) %collective-permute-start) | collective-permute-done | bytes 40 | tf_op jit(solution)/shard_map/ppermute | solution.py:140
  3.6 0.7 fusion.1
  4.3 2.5 %compare_select_fusion.mine_ref = s32[128]{0:T(128)S(1)} fusion(s32[]{:T(128)} %bitcast.3, s32[]{:T(128)} %bitcast.2, s32[]{:T(128)} %bitcast.1, s32[]{:T(128)} %bitcast, s32[]{:T(128)S(6)} %rem.37), kind=kLoop, calls=%fused_computation.1 | loop fusion | flops 2176 | bytes 532 | tf_op jit(solution)/shard_map/jit(_where)/select_n | solution.py:151
  6.8 0.0 copy-start
  6.9 0.0 copy-start.3
  6.9 0.5 collective-permute-start.4
  7.4 3.5 %collective-permute-start.3 = (s32[128]{0:T(128)S(1)}, s32[128]{0:T(128)S(1)}, u32[]{:S(2)}, u32[]{:S(2)}) collective-permute-start(s32[128]{0:T(128)S(1)} %compare_select_fusion.mine_ref), channel_id=1, source_target_pairs={{0,8},{1,11},{2,10},{3,9},{4,12},{5,15},{6,14},{7,13},{8,0},{9,3},... | collective-permute-start | bytes 1544 | tf_op jit(solution)/shard_map/ppermute | solution.py:147
  10.9 1.5 %collective-permute-start.1 = (s32[128]{0:T(128)S(1)}, s32[128]{0:T(128)S(1)}, u32[]{:S(2)}, u32[]{:S(2)}) collective-permute-start(s32[128]{0:T(128)S(1)} %compare_select_fusion.mine_ref), channel_id=1, source_target_pairs={{0,2},{1,3},{2,0},{3,1},{4,6},{5,7},{6,4},{7,5},{8,10},{9,11},{10,... | collective-permute-start | bytes 1544 | tf_op jit(solution)/shard_map/ppermute | solution.py:147
  12.4 0.2 collective-permute-start.7
  12.6 0.3 collective-permute-start.6
  12.9 1.5 %collective-permute-done.2.refs_0_ = s32[128]{0:T(128)S(1)} collective-permute-done((s32[128]{0:T(128)S(1)}, s32[128]{0:T(128)S(1)}, u32[]{:S(2)}, u32[]{:S(2)}) %collective-permute-start.2) | collective-permute-done | bytes 544 | tf_op jit(solution)/shard_map/ppermute | solution.py:147
  14.4 0.2 collective-permute-start.5
  14.7 0.9 %collective-permute-done.5.refs_3_ = s32[128]{0:T(128)S(1)} collective-permute-done((s32[128]{0:T(128)S(1)}, s32[128]{0:T(128)S(1)}, u32[]{:S(2)}, u32[]{:S(2)}) %collective-permute-start.5) | collective-permute-done | bytes 544 | tf_op jit(solution)/shard_map/ppermute | solution.py:140
  15.6 0.5 copy-done.12
  16.1 1.1 %copy-done.1 = bf16[32,6,32,128]{3,2,1,0:T(8,128)(2,1)} copy-done((bf16[32,6,32,128]{3,2,1,0:T(8,128)(2,1)}, bf16[32,6,32,128]{3,2,1,0:T(8,128)(2,1)S(1)}, u32[]{:S(2)}) %copy-start.1) | copy-done | bytes 1572888
  17.3 24.0 %pack.1 = (bf16[2,6,32,128]{3,2,1,0:T(8,128)(2,1)}, bf16[2,2,6,32,128]{4,3,2,1,0:T(8,128)(2,1)}, bf16[2,2,6,32,128]{4,3,2,1,0:T(8,128)(2,1)}, bf16[2,2,6,32,128]{4,3,2,1,0:T(8,128)(2,1)}, s32[4]{0:T(128)}) custom-call(s32[32]{0:T(128)} %owner_ref.1, s32[128]{0:T(128)} %copy-done.5, s32[128]{0:T(128)} %copy-done.9, s32[128]{0:T(128)} %copy-done.8, ...), custom_call_target="tpu_custom_call" | custom-call | tf_op jit(solution)/shard_map/pack/pallas_call | solution.py:158
  41.3 1.0 %collective-permute-start.10 = (bf16[2,2,6,32,128]{4,3,2,1,0:T(8,128)(2,1)}, bf16[2,2,6,32,128]{4,3,2,1,0:T(8,128)(2,1)S(1)}, u32[]{:S(2)}, u32[]{:S(2)}) collective-permute-start(bf16[2,2,6,32,128]{4,3,2,1,0:T(8,128)(2,1)} %get-tuple-element.12), channel_id=1, source_target_pairs={{0,4},{1,7},{2,6},{3,5},{4,0},{5,3},{6,2},{7,1},{8,12},{9,15},{10,... | collective-permute-start | bytes 589832 | tf_op jit(solution)/shard_map/ppermute | solution.py:147
  42.3 0.6 collective-permute-start.11
  42.9 1.9 %collective-permute-start.12 = (bf16[2,2,6,32,128]{4,3,2,1,0:T(8,128)(2,1)}, bf16[2,2,6,32,128]{4,3,2,1,0:T(8,128)(2,1)S(1)}, u32[]{:S(2)}, u32[]{:S(2)}) collective-permute-start(bf16[2,2,6,32,128]{4,3,2,1,0:T(8,128)(2,1)} %get-tuple-element.14), channel_id=1, source_target_pairs={{0,12},{1,15},{2,14},{3,13},{4,8},{5,11},{6,10},{7,9},{8,4},{9,7},... | collective-permute-start | bytes 589832 | tf_op jit(solution)/shard_map/ppermute | solution.py:147
  44.8 4.4 %collective-permute-done.10.refs_3_ = bf16[2,2,6,32,128]{4,3,2,1,0:T(8,128)(2,1)S(1)} collective-permute-done((bf16[2,2,6,32,128]{4,3,2,1,0:T(8,128)(2,1)}, bf16[2,2,6,32,128]{4,3,2,1,0:T(8,128)(2,1)S(1)}, u32[]{:S(2)}, u32[]{:S(2)}) %collective-permute-start.10) | collective-permute-done | bytes 196640 | tf_op jit(solution)/shard_map/ppermute | solution.py:147
  49.2 3.8 %collective-permute-done.11.refs_4_ = bf16[2,2,6,32,128]{4,3,2,1,0:T(8,128)(2,1)S(1)} collective-permute-done((bf16[2,2,6,32,128]{4,3,2,1,0:T(8,128)(2,1)}, bf16[2,2,6,32,128]{4,3,2,1,0:T(8,128)(2,1)S(1)}, u32[]{:S(2)}, u32[]{:S(2)}) %collective-permute-start.11) | collective-permute-done | bytes 196640 | tf_op jit(solution)/shard_map/ppermute | solution.py:147
  53.0 10.3 %collective-permute-done.12.refs_5_ = bf16[2,2,6,32,128]{4,3,2,1,0:T(8,128)(2,1)S(1)} collective-permute-done((bf16[2,2,6,32,128]{4,3,2,1,0:T(8,128)(2,1)}, bf16[2,2,6,32,128]{4,3,2,1,0:T(8,128)(2,1)S(1)}, u32[]{:S(2)}, u32[]{:S(2)}) %collective-permute-start.12) | collective-permute-done | bytes 196640 | tf_op jit(solution)/shard_map/ppermute | solution.py:147
  63.4 0.7 collective-permute-start.15
  64.0 0.9 %collective-permute-start.9 = (bf16[2,6,32,128]{3,2,1,0:T(8,128)(2,1)}, bf16[2,6,32,128]{3,2,1,0:T(8,128)(2,1)S(1)}, u32[]{:S(2)}, u32[]{:S(2)}) collective-permute-start(bf16[2,6,32,128]{3,2,1,0:T(8,128)(2,1)} %get-tuple-element.11), channel_id=1, source_target_pairs={{0,2},{1,3},{2,0},{3,1},{4,6},{5,7},{6,4},{7,5},{8,10},{9,11},{10,... | collective-permute-start | bytes 294920 | tf_op jit(solution)/shard_map/ppermute | solution.py:147
  64.9 4.0 %collective-permute-done.9.refs_2_ = bf16[2,6,32,128]{3,2,1,0:T(8,128)(2,1)S(1)} collective-permute-done((bf16[2,6,32,128]{3,2,1,0:T(8,128)(2,1)}, bf16[2,6,32,128]{3,2,1,0:T(8,128)(2,1)S(1)}, u32[]{:S(2)}, u32[]{:S(2)}) %collective-permute-start.9) | collective-permute-done | bytes 98336 | tf_op jit(solution)/shard_map/ppermute | solution.py:147
  69.0 0.0 copy-start.2
  69.0 1.4 %copy-done.2 = bf16[32,6,32,128]{3,2,1,0:T(8,128)(2,1)S(1)} copy-done((bf16[32,6,32,128]{3,2,1,0:T(8,128)(2,1)S(1)}, bf16[32,6,32,128]{3,2,1,0:T(8,128)(2,1)}, u32[]{:S(2)}) %copy-start.2) | copy-done | bytes 1572888
  70.4 0.7 copy-done.4
  71.0 4.9 %exchange.1 = f32[2,768,768]{2,1,0:T(8,128)} custom-call(s32[4]{0:T(128)S(1)} %copy-done.4, bf16[16,16]{1,0:T(8,128)(2,1)S(1)} %copy-done.3, bf16[32,6,32,128]{3,2,1,0:T(8,128)(2,1)S(1)} %bitcast.9, bf16[32,6,32,128]{3,2,1,0:T(8,128)(2,1)S(1)} %copy-done.2, bf16[2,6,32,128]{3,2,1,0:T(8,128)(2,1)S(1)} %collective-permute-done.9.refs_2_, ...), custom_call_target="tpu_custom_call" | custom-call | tf_op jit(solution)/shard_map/exchange/pallas_call | solution.py:175
  (31 shorter events, 0.1 us)
Async XLA Ops:
  0.0 15.5 %collective-permute-start.8 = (bf16[32,6,32,128]{3,2,1,0:T(8,128)(2,1)}, bf16[32,6,32,128]{3,2,1,0:T(8,128)(2,1)S(1)}, u32[]{:S(2)}, u32[]{:S(2)}) collective-permute-start(bf16[32,6,32,128]{3,2,1,0:T(8,128)(2,1)} %bitcast.7), channel_id=1, source_target_pairs={{0,1},{1,0},{2,3},{3,2},{4,5},{5,4},{6,7},{7,6},{8,9},{9,8},{10,11... | collective-permute-start | bytes 4718600 | tf_op jit(solution)/shard_map/ppermute | solution.py:140
  0.0 3.6 %collective-permute-start = (s32[2]{0:T(128)}, s32[2]{0:T(128)S(1)}, u32[]{:S(2)}, u32[]{:S(2)}) collective-permute-start(s32[2]{0:T(128)} %param.7), channel_id=1, source_target_pairs={{0,1},{1,0},{2,3},{3,2},{4,5},{5,4},{6,7},{7,6},{8,9},{9,8},{10,11... | collective-permute-start | bytes 32 | tf_op jit(solution)/shard_map/ppermute | solution.py:140
  6.8 8.7 %copy-start.5 = (s32[128]{0:T(128)}, s32[128]{0:T(128)S(1)}, u32[]{:S(2)}) copy-start(s32[128]{0:T(128)S(1)} %compare_select_fusion.mine_ref) | copy-start | bytes 1540
  6.8 62.1 %copy-start = (bf16[1,32,32,6,128]{4,2,3,1,0:T(8,128)(2,1)S(1)}, bf16[1,32,32,6,128]{4,2,3,1,0:T(8,128)(2,1)}, u32[]{:S(2)}) copy-start(bf16[1,32,32,6,128]{4,2,3,1,0:T(8,128)(2,1)} %param.4) | copy-start | bytes 4718596
  6.9 62.1 %copy-start.3 = (bf16[16,16]{1,0:T(8,128)(2,1)S(1)}, bf16[16,16]{1,0:T(8,128)(2,1)}, u32[]{:S(2)}) copy-start(bf16[16,16]{1,0:T(8,128)(2,1)} %metric_ref.1) | copy-start | bytes 1540
  6.9 5.5 %collective-permute-start.4 = (s32[128]{0:T(128)S(1)}, s32[128]{0:T(128)S(1)}, u32[]{:S(2)}, u32[]{:S(2)}) collective-permute-start(s32[128]{0:T(128)S(1)} %compare_select_fusion.mine_ref), channel_id=1, source_target_pairs={{0,12},{1,15},{2,14},{3,13},{4,8},{5,11},{6,10},{7,9},{8,4},{9,7},... | collective-permute-start | bytes 1544 | tf_op jit(solution)/shard_map/ppermute | solution.py:147
  7.4 5.2 %collective-permute-start.3 = (s32[128]{0:T(128)S(1)}, s32[128]{0:T(128)S(1)}, u32[]{:S(2)}, u32[]{:S(2)}) collective-permute-start(s32[128]{0:T(128)S(1)} %compare_select_fusion.mine_ref), channel_id=1, source_target_pairs={{0,8},{1,11},{2,10},{3,9},{4,12},{5,15},{6,14},{7,13},{8,0},{9,3},... | collective-permute-start | bytes 1544 | tf_op jit(solution)/shard_map/ppermute | solution.py:147
  10.9 3.5 %collective-permute-start.2 = (s32[128]{0:T(128)S(1)}, s32[128]{0:T(128)S(1)}, u32[]{:S(2)}, u32[]{:S(2)}) collective-permute-start(s32[128]{0:T(128)S(1)} %compare_select_fusion.mine_ref), channel_id=1, source_target_pairs={{0,4},{1,7},{2,6},{3,5},{4,0},{5,3},{6,2},{7,1},{8,12},{9,15},{10,... | collective-permute-start | bytes 1544 | tf_op jit(solution)/shard_map/ppermute | solution.py:147
  10.9 3.8 %collective-permute-start.1 = (s32[128]{0:T(128)S(1)}, s32[128]{0:T(128)S(1)}, u32[]{:S(2)}, u32[]{:S(2)}) collective-permute-start(s32[128]{0:T(128)S(1)} %compare_select_fusion.mine_ref), channel_id=1, source_target_pairs={{0,2},{1,3},{2,0},{3,1},{4,6},{5,7},{6,4},{7,5},{8,10},{9,11},{10,... | collective-permute-start | bytes 1544 | tf_op jit(solution)/shard_map/ppermute | solution.py:147
  12.4 3.2 %copy-start.6 = (s32[128]{0:T(128)}, s32[128]{0:T(128)S(1)}, u32[]{:S(2)}) copy-start(s32[128]{0:T(128)S(1)} %collective-permute-done.4.refs_2_) | copy-start | bytes 1540
  12.4 2.2 %collective-permute-start.7 = (s32[128]{0:T(128)S(1)}, s32[128]{0:T(128)S(1)}, u32[]{:S(2)}, u32[]{:S(2)}) collective-permute-start(s32[128]{0:T(128)S(1)} %collective-permute-done.4.refs_2_), channel_id=1, source_target_pairs={{0,1},{1,0},{2,3},{3,2},{4,5},{5,4},{6,7},{7,6},{8,9},{9,8},{10,11... | collective-permute-start | bytes 1544 | tf_op jit(solution)/shard_map/ppermute | solution.py:140
  12.6 3.0 %copy-start.7 = (s32[128]{0:T(128)}, s32[128]{0:T(128)S(1)}, u32[]{:S(2)}) copy-start(s32[128]{0:T(128)S(1)} %collective-permute-done.3.refs_1_) | copy-start | bytes 1540
  12.6 2.1 %collective-permute-start.6 = (s32[128]{0:T(128)S(1)}, s32[128]{0:T(128)S(1)}, u32[]{:S(2)}, u32[]{:S(2)}) collective-permute-start(s32[128]{0:T(128)S(1)} %collective-permute-done.3.refs_1_), channel_id=1, source_target_pairs={{0,1},{1,0},{2,3},{3,2},{4,5},{5,4},{6,7},{7,6},{8,9},{9,8},{10,11... | collective-permute-start | bytes 1544 | tf_op jit(solution)/shard_map/ppermute | solution.py:140
  14.4 1.2 %copy-start.8 = (s32[128]{0:T(128)}, s32[128]{0:T(128)S(1)}, u32[]{:S(2)}) copy-start(s32[128]{0:T(128)S(1)} %collective-permute-done.2.refs_0_) | copy-start | bytes 1540
  14.4 1.1 %collective-permute-start.5 = (s32[128]{0:T(128)S(1)}, s32[128]{0:T(128)S(1)}, u32[]{:S(2)}, u32[]{:S(2)}) collective-permute-start(s32[128]{0:T(128)S(1)} %collective-permute-done.2.refs_0_), channel_id=1, source_target_pairs={{0,1},{1,0},{2,3},{3,2},{4,5},{5,4},{6,7},{7,6},{8,9},{9,8},{10,11... | collective-permute-start | bytes 1544 | tf_op jit(solution)/shard_map/ppermute | solution.py:140
  14.6 0.9 %copy-start.9 = (s32[128]{0:T(128)}, s32[128]{0:T(128)S(1)}, u32[]{:S(2)}) copy-start(s32[128]{0:T(128)S(1)} %collective-permute-done.1.side_ref) | copy-start | bytes 1540
  14.7 0.9 %copy-start.10 = (s32[128]{0:T(128)}, s32[128]{0:T(128)S(1)}, u32[]{:S(2)}) copy-start(s32[128]{0:T(128)S(1)} %collective-permute-done.7.refs_5_) | copy-start | bytes 1540
  14.7 0.9 %copy-start.11 = (s32[128]{0:T(128)}, s32[128]{0:T(128)S(1)}, u32[]{:S(2)}) copy-start(s32[128]{0:T(128)S(1)} %collective-permute-done.6.refs_4_) | copy-start | bytes 1540
  15.5 0.6 copy-start.12
  16.1 1.1 %copy-start.1 = (bf16[32,6,32,128]{3,2,1,0:T(8,128)(2,1)}, bf16[32,6,32,128]{3,2,1,0:T(8,128)(2,1)S(1)}, u32[]{:S(2)}) copy-start(bf16[32,6,32,128]{3,2,1,0:T(8,128)(2,1)S(1)} %collective-permute-done.8.refs_7_.refs_1_) | copy-start | bytes 4718596
  41.3 8.0 %collective-permute-start.10 = (bf16[2,2,6,32,128]{4,3,2,1,0:T(8,128)(2,1)}, bf16[2,2,6,32,128]{4,3,2,1,0:T(8,128)(2,1)S(1)}, u32[]{:S(2)}, u32[]{:S(2)}) collective-permute-start(bf16[2,2,6,32,128]{4,3,2,1,0:T(8,128)(2,1)} %get-tuple-element.12), channel_id=1, source_target_pairs={{0,4},{1,7},{2,6},{3,5},{4,0},{5,3},{6,2},{7,1},{8,12},{9,15},{10,... | collective-permute-start | bytes 589832 | tf_op jit(solution)/shard_map/ppermute | solution.py:147
  42.3 10.7 %collective-permute-start.11 = (bf16[2,2,6,32,128]{4,3,2,1,0:T(8,128)(2,1)}, bf16[2,2,6,32,128]{4,3,2,1,0:T(8,128)(2,1)S(1)}, u32[]{:S(2)}, u32[]{:S(2)}) collective-permute-start(bf16[2,2,6,32,128]{4,3,2,1,0:T(8,128)(2,1)} %get-tuple-element.13), channel_id=1, source_target_pairs={{0,8},{1,11},{2,10},{3,9},{4,12},{5,15},{6,14},{7,13},{8,0},{9,3},... | collective-permute-start | bytes 589832 | tf_op jit(solution)/shard_map/ppermute | solution.py:147
  42.9 20.5 %collective-permute-start.12 = (bf16[2,2,6,32,128]{4,3,2,1,0:T(8,128)(2,1)}, bf16[2,2,6,32,128]{4,3,2,1,0:T(8,128)(2,1)S(1)}, u32[]{:S(2)}, u32[]{:S(2)}) collective-permute-start(bf16[2,2,6,32,128]{4,3,2,1,0:T(8,128)(2,1)} %get-tuple-element.14), channel_id=1, source_target_pairs={{0,12},{1,15},{2,14},{3,13},{4,8},{5,11},{6,10},{7,9},{8,4},{9,7},... | collective-permute-start | bytes 589832 | tf_op jit(solution)/shard_map/ppermute | solution.py:147
  49.2 19.7 %collective-permute-start.13 = (bf16[2,2,6,32,128]{4,3,2,1,0:T(8,128)(2,1)S(1)}, bf16[2,2,6,32,128]{4,3,2,1,0:T(8,128)(2,1)S(1)}, u32[]{:S(2)}, u32[]{:S(2)}) collective-permute-start(bf16[2,2,6,32,128]{4,3,2,1,0:T(8,128)(2,1)S(1)} %collective-permute-done.10.refs_3_), channel_id=1, source_target_pairs={{0,1},{1,0},{2,3},{3,2},{4,5},{5,4},{6,7},{7,6},{8,9},{9,8},{10,11... | collective-permute-start | bytes 589832 | tf_op jit(solution)/shard_map/ppermute | solution.py:140
  53.0 15.9 %collective-permute-start.14 = (bf16[2,2,6,32,128]{4,3,2,1,0:T(8,128)(2,1)S(1)}, bf16[2,2,6,32,128]{4,3,2,1,0:T(8,128)(2,1)S(1)}, u32[]{:S(2)}, u32[]{:S(2)}) collective-permute-start(bf16[2,2,6,32,128]{4,3,2,1,0:T(8,128)(2,1)S(1)} %collective-permute-done.11.refs_4_), channel_id=1, source_target_pairs={{0,1},{1,0},{2,3},{3,2},{4,5},{5,4},{6,7},{7,6},{8,9},{9,8},{10,11... | collective-permute-start | bytes 589832 | tf_op jit(solution)/shard_map/ppermute | solution.py:140
  63.4 5.6 %collective-permute-start.15 = (bf16[2,2,6,32,128]{4,3,2,1,0:T(8,128)(2,1)S(1)}, bf16[2,2,6,32,128]{4,3,2,1,0:T(8,128)(2,1)S(1)}, u32[]{:S(2)}, u32[]{:S(2)}) collective-permute-start(bf16[2,2,6,32,128]{4,3,2,1,0:T(8,128)(2,1)S(1)} %collective-permute-done.12.refs_5_), channel_id=1, source_target_pairs={{0,1},{1,0},{2,3},{3,2},{4,5},{5,4},{6,7},{7,6},{8,9},{9,8},{10,11... | collective-permute-start | bytes 589832 | tf_op jit(solution)/shard_map/ppermute | solution.py:140
  64.0 4.9 %collective-permute-start.9 = (bf16[2,6,32,128]{3,2,1,0:T(8,128)(2,1)}, bf16[2,6,32,128]{3,2,1,0:T(8,128)(2,1)S(1)}, u32[]{:S(2)}, u32[]{:S(2)}) collective-permute-start(bf16[2,6,32,128]{3,2,1,0:T(8,128)(2,1)} %get-tuple-element.11), channel_id=1, source_target_pairs={{0,2},{1,3},{2,0},{3,1},{4,6},{5,7},{6,4},{7,5},{8,10},{9,11},{10,... | collective-permute-start | bytes 294920 | tf_op jit(solution)/shard_map/ppermute | solution.py:147
  69.0 1.4 %copy-start.2 = (bf16[32,6,32,128]{3,2,1,0:T(8,128)(2,1)S(1)}, bf16[32,6,32,128]{3,2,1,0:T(8,128)(2,1)}, u32[]{:S(2)}) copy-start(bf16[32,6,32,128]{3,2,1,0:T(8,128)(2,1)} %copy-done.1) | copy-start | bytes 4718596
  70.4 0.7 copy-start.4

commit v2 on v1

v2 whole, which is shorter than its diff:
```python
import functools

import jax
import jax.numpy as jnp
from jax import lax
from jax.experimental import pallas as pl
from jax.experimental.pallas import tpu as pltpu
from jax.sharding import PartitionSpec as P

VMEM = pl.BlockSpec(memory_space=pltpu.VMEM)
SMEM = pl.BlockSpec(memory_space=pltpu.SMEM)
GROUP = 16


def pack_kernel(chips, owner_ref, *refs):
    half = chips // 2
    rows = refs[:chips]
    own_raw, peer_raw = refs[chips : chips + 2]
    outs = refs[chips + 2 : chips + 2 + half]
    self_ref, info_ref, held, table, sems = refs[chips + 2 + half :]
    blocks, slots = own_raw.shape[0], own_raw.shape[1]
    me = lax.axis_index("aux")
    chip, core = me // 2, lax.rem(me, 2)

    copies = [pltpu.make_async_copy(ref, table.at[n], sems.at[n]) for n, ref in enumerate(rows)]
    for copy in copies:
        copy.start()

    def place(o, carry):
        held[owner_ref[o]] = o
        return carry

    lax.fori_loop(0, blocks, place, 0, unroll=True)
    for copy in copies:
        copy.wait()

    def live(block):
        m = lax.bitwise_xor(block // 4, chip)
        far = lax.bitwise_and(lax.bitwise_xor(m, core), 1)
        f = jnp.where(m >= 2, far, lax.bitwise_and(m, 1))
        sender = jnp.where(m >= 2, lax.bitwise_xor(core, far), core)
        lane = 2 * lax.bitwise_xor(lax.bitwise_and(block // 2, 1), sender) + lax.bitwise_and(block, 1)
        return table[(m // 2) * 2 + f, lane]

    def send(dest, target):
        first, second = held[2 * dest], held[2 * dest + 1]
        count = live(first)
        for j in range(slots):
            from_first = j < count
            block = jnp.where(from_first, first, second)
            slot = jnp.where(from_first, j, slots - 1 - j)
            target[core, j] = own_raw[block, slot]
            target[1 - core, j] = peer_raw[block, slot]
        return count, second

    for k in range(half - 1, 0, -1):
        there = lax.bitwise_xor(chip, 2 * k + core)
        for f in range(2):
            send(2 * there + (core if f == 0 else 1 - core), outs[k].at[f])
    send(2 * lax.bitwise_xor(chip, 1) + core, outs[0])
    count, second = send(me, self_ref)
    row = lax.broadcasted_iota(jnp.int32, info_ref.shape, 0)
    info_ref[...] = jnp.where(row == 0, count, live(second))


def factor_kernel(metric_ref, factor_ref):
    wide, aux = factor_ref.shape[0], metric_ref.shape[0]
    me = lax.axis_index("aux")
    chip, core = me // 2, lax.rem(me, 2)
    row = lax.broadcasted_iota(jnp.int32, (wide, aux), 0) // GROUP
    column = lax.broadcasted_iota(jnp.int32, (wide, aux), 1)
    pick = (row == column).astype(jnp.bfloat16)
    place = row // 2
    away = jnp.where(place < 2, place, lax.bitwise_xor(place, core))
    origin = 2 * lax.bitwise_xor(away, chip) + lax.bitwise_and(row, 1)
    pick_origin = (origin == column).astype(jnp.bfloat16)
    tall = jnp.dot(pick, metric_ref[...], preferred_element_type=jnp.float32).astype(jnp.bfloat16)
    spread = lax.dot_general(tall, pick_origin, (((1,), (1,)), ((), ())), preferred_element_type=jnp.float32)
    same = lax.rem(lax.broadcasted_iota(jnp.int32, (wide, wide), 0), GROUP) == lax.rem(
        lax.broadcasted_iota(jnp.int32, (wide, wide), 1), GROUP
    )
    factor_ref[...] = jnp.where(same, spread, 0.0).astype(jnp.bfloat16)


def exchange_kernel(chips, info_ref, factor_ref, self_ref, side_ref, *refs):
    half = chips // 2
    got, swapped = refs[: half - 1], refs[half - 1 : 2 * half - 2]
    out_ref, rows, stage, sems = refs[2 * half - 2 :]
    _, slots, orbitals, width = self_ref.shape
    wide = factor_ref.shape[0]
    arrivals = [self_ref, side_ref]
    for k in range(1, half):
        arrivals += [got[k - 1].at[0], swapped[k - 1].at[1]]

    def span(n):
        return slice(n * width, (n + 1) * width)

    for part in range(orbitals // GROUP):
        columns = [
            jnp.concatenate(
                [ref[q, s, part * GROUP : (part + 1) * GROUP, :] for ref in arrivals for q in range(2)], axis=0
            )
            for s in range(slots)
        ]
        fitted = jnp.dot(factor_ref[...], jnp.concatenate(columns, axis=1), preferred_element_type=jnp.float32)
        rows[part * wide : (part + 1) * wide, :] = fitted.astype(jnp.bfloat16)

    live = [info_ref[0:1, :], info_ref[1:2, :]]
    for s in range(slots):
        product = lax.dot_general(
            rows[:, span(s)], rows[...], (((0,), (0,)), ((), ())), preferred_element_type=jnp.float32
        )
        for which in range(2):
            row = s if which == 0 else slots - 1 - s
            for t in range(slots):
                column = t if which == 0 else slots - 1 - t
                stage[which, span(row), span(column)] = jnp.where(
                    live[which] > max(row, column), product[:, span(t)], 0.0
                )
            pltpu.make_async_copy(
                stage.at[which, span(row)], out_ref.at[which, span(row)], sems.at[which, row]
            ).start()
    for which in range(2):
        for row in range(slots):
            pltpu.make_async_copy(
                stage.at[which, span(row)], out_ref.at[which, span(row)], sems.at[which, row]
            ).wait()


def shards(devices, raw_tiles, metric, owner_map, counts):
    chips = devices // 2
    half = chips // 2
    _, _, orbitals, slots, width = raw_tiles.shape
    raw = raw_tiles[0].transpose(0, 2, 1, 3)

    def swap(x):
        return lax.ppermute(x, "aux", [(i, i ^ 1) for i in range(devices)])

    def hop(x, k):
        def target(i):
            away = 1 if k == 0 else 2 * k + i % 2
            return (i // 2 ^ away) * 2 + i % 2

        return lax.ppermute(x, "aux", [(i, target(i)) for i in range(devices)])

    other = swap(counts)
    mine = jnp.concatenate([counts, other, jnp.zeros((124,), jnp.int32)])
    raw, mine = lax.optimization_barrier((raw, mine))
    peer_raw = swap(raw)
    got = lax.optimization_barrier([hop(mine, k) for k in range(half)])
    rows = [mine, got[0]]
    for x in got[1:]:
        rows += [x, swap(x)]

    pair = jax.ShapeDtypeStruct((2, slots, orbitals, width), raw.dtype)
    pairs = jax.ShapeDtypeStruct((2, 2, slots, orbitals, width), raw.dtype)
    *outgoing, own, info = pl.pallas_call(
        functools.partial(pack_kernel, chips),
        out_shape=[pair] + [pairs] * (half - 1) + [pair, jax.ShapeDtypeStruct((8, 128), jnp.int32)],
        in_specs=[SMEM] + [VMEM] * (chips + 2),
        out_specs=[VMEM] * (half + 2),
        scratch_shapes=[
            pltpu.SMEM((raw.shape[0],), jnp.int32),
            pltpu.SMEM((chips, 128), jnp.int32),
            pltpu.SemaphoreType.DMA((chips,)),
        ],
        compiler_params=pltpu.CompilerParams(vmem_limit_bytes=12 * 1024 * 1024),
        name="pack",
    )(owner_map, *rows, raw, peer_raw)

    metric, own = lax.optimization_barrier((metric, own))
    factor = pl.pallas_call(
        factor_kernel,
        out_shape=jax.ShapeDtypeStruct((devices * GROUP, devices * GROUP), jnp.bfloat16),
        in_specs=[VMEM],
        out_specs=VMEM,
        compiler_params=pltpu.CompilerParams(vmem_limit_bytes=12 * 1024 * 1024),
        name="factor",
    )(metric)

    *arrived, factor = lax.optimization_barrier([hop(x, k) for k, x in enumerate(outgoing)] + [factor])
    crossed = [swap(x) for x in arrived[1:]]

    return pl.pallas_call(
        functools.partial(exchange_kernel, chips),
        out_shape=jax.ShapeDtypeStruct((2, slots * width, slots * width), jnp.float32),
        in_specs=[VMEM] * (2 * half + 2),
        out_specs=pl.BlockSpec(memory_space=pl.ANY),
        scratch_shapes=[
            pltpu.VMEM((devices * orbitals, slots * width), raw.dtype),
            pltpu.VMEM((2, slots * width, slots * width), jnp.float32),
            pltpu.SemaphoreType.DMA((2, slots)),
        ],
        compiler_params=pltpu.CompilerParams(vmem_limit_bytes=32 * 1024 * 1024),
        name="exchange",
    )(info, factor, own, arrived[0], *arrived[1:], *crossed)


def solution(mesh):
    in_specs = (
        P(("grp", "aux"), None, None, None, None),
        P("grp", None),
        P("grp"),
        P(("grp", "aux")),
    )
    out_specs = P(("grp", "aux"), None, None)
    body = functools.partial(shards, mesh.shape["aux"])
    return jax.shard_map(body, mesh=mesh, in_specs=in_specs, out_specs=out_specs, check_vma=False)
```

time: 76.2 us -> 43 us (0.56)
  the two profiles are of different devices: /device:TPU:16 before, /device:TPU:17 now
where the time goes in v2:
time: 43 us; the launch traced here: 42.8 us
  waiting for transfers between devices  22.5 us (52%)
  starting transfers between devices  12.7 us (30%)
  Pallas kernels  4.78 us (11%)
  local copies, waits for them, and re-layouts  2.07 us (5%)
  other arithmetic  0.74 us (2%)
    ppermute x8, waiting for transfers between devices, hop(): return lax.ppermute(x, 'aux', [(i, target(i)) for i in range(devices)])  19.1 us
    ppermute x8, starting transfers between devices, hop(): return lax.ppermute(x, 'aux', [(i, target(i)) for i in range(devices)])  10.5 us
    ppermute x8, waiting for transfers between devices, swap(): return lax.ppermute(x, 'aux', [(i, i ^ 1) for i in range(devices)])  3.45 us
    pallas_call x1, Pallas kernels, shards(): pl.pallas_call(functools.partial(exchange_kernel, chips), out_shape=jax.S...  2.92 us
    ppermute x8, starting transfers between devices, swap(): return lax.ppermute(x, 'aux', [(i, i ^ 1) for i in range(devices)])  2.12 us
    unnamed x6, local copies, waits for them, and re-layouts  2.07 us
    pallas_call x1, Pallas kernels, shards(): pl.pallas_call(functools.partial(pack_kernel, chips), out_shape=[pair] +...  1.56 us
  transfers between devices with their start and end apart: 16, of which 11 were waited for; matrix products, arithmetic and copies ran while one was open for 0% of the time, Pallas kernels for 1%

profile of v2, /device:TPU:17, one launch (start us, length us, event | category | flops | bytes accessed | tf_op | source)
XLA Modules:
  0.0 42.8 jit_solution(10189775174644428534)
XLA Ops:
  0.0 0.7 %collective-permute-start = (s32[2]{0:T(128)}, s32[2]{0:T(128)S(1)}, u32[]{:S(2)}, u32[]{:S(2)}) collective-permute-start(s32[2]{0:T(128)} %param.7), channel_id=1, source_target_pairs={{0,1},{1,0},{2,3},{3,2},{4,5},{5,4},{6,7},{7,6},{8,9},{9,8},{10,11... | collective-permute-start | bytes 32 | tf_op jit(solution)/shard_map/ppermute | solution.py:137
  0.7 1.0 %collective-permute-done = s32[2]{0:T(128)S(1)} collective-permute-done((s32[2]{0:T(128)}, s32[2]{0:T(128)S(1)}, u32[]{:S(2)}, u32[]{:S(2)}) %collective-permute-start) | collective-permute-done | bytes 40 | tf_op jit(solution)/shard_map/ppermute | solution.py:137
  1.6 0.7 %pad_add_fusion.refs_0_ = s32[128]{0:T(128)S(1)} fusion(s32[124]{0:T(128)S(1)} %broadcast_in_dim.3, s32[2]{0:T(128)S(1)} %collective-permute-done, s32[2]{0:T(128)} %param.7), kind=kLoop, calls=%fused_computation | loop fusion | flops 256 | bytes 1024 | tf_op jit(solution)/shard_map/concatenate | solution.py:147
  2.4 0.3 collective-permute-start.8
  2.7 1.1 %collective-permute-start.4 = (s32[128]{0:T(128)S(1)}, s32[128]{0:T(128)S(1)}, u32[]{:S(2)}, u32[]{:S(2)}) collective-permute-start(s32[128]{0:T(128)S(1)} %pad_add_fusion.refs_0_), channel_id=1, source_target_pairs={{0,12},{1,15},{2,14},{3,13},{4,8},{5,11},{6,10},{7,9},{8,4},{9,7},... | collective-permute-start | bytes 1544 | tf_op jit(solution)/shard_map/ppermute | solution.py:144
  3.8 3.2 %collective-permute-start.3 = (s32[128]{0:T(128)S(1)}, s32[128]{0:T(128)S(1)}, u32[]{:S(2)}, u32[]{:S(2)}) collective-permute-start(s32[128]{0:T(128)S(1)} %pad_add_fusion.refs_0_), channel_id=1, source_target_pairs={{0,8},{1,11},{2,10},{3,9},{4,12},{5,15},{6,14},{7,13},{8,0},{9,3},... | collective-permute-start | bytes 1544 | tf_op jit(solution)/shard_map/ppermute | solution.py:144
  7.0 0.2 collective-permute-start.2
  7.2 1.0 %collective-permute-start.1 = (s32[128]{0:T(128)S(1)}, s32[128]{0:T(128)S(1)}, u32[]{:S(2)}, u32[]{:S(2)}) collective-permute-start(s32[128]{0:T(128)S(1)} %pad_add_fusion.refs_0_), channel_id=1, source_target_pairs={{0,2},{1,3},{2,0},{3,1},{4,6},{5,7},{6,4},{7,5},{8,10},{9,11},{10,... | collective-permute-start | bytes 1544 | tf_op jit(solution)/shard_map/ppermute | solution.py:144
  8.2 0.0 collective-permute-done.4.refs_6_
  8.2 2.0 %collective-permute-done.2.refs_2_ = s32[128]{0:T(128)S(1)} collective-permute-done((s32[128]{0:T(128)S(1)}, s32[128]{0:T(128)S(1)}, u32[]{:S(2)}, u32[]{:S(2)}) %collective-permute-start.2) | collective-permute-done | bytes 544 | tf_op jit(solution)/shard_map/ppermute | solution.py:144
  10.3 0.1 collective-permute-start.5
  10.4 0.4 collective-permute-start.6
  10.8 0.1 collective-permute-start.7
  10.9 0.5 %collective-permute-done.5.refs_3_ = s32[128]{0:T(128)S(1)} collective-permute-done((s32[128]{0:T(128)S(1)}, s32[128]{0:T(128)S(1)}, u32[]{:S(2)}, u32[]{:S(2)}) %collective-permute-start.5) | collective-permute-done | bytes 544 | tf_op jit(solution)/shard_map/ppermute | solution.py:137
  11.4 0.2 collective-permute-done.6.refs_5_
  11.6 0.3 collective-permute-done.7.refs_7_
  11.9 1.4 %copy-done = bf16[1,32,32,6,128]{4,2,3,1,0:T(8,128)(2,1)S(1)} copy-done((bf16[1,32,32,6,128]{4,2,3,1,0:T(8,128)(2,1)S(1)}, bf16[1,32,32,6,128]{4,2,3,1,0:T(8,128)(2,1)}, u32[]{:S(2)}) %copy-start) | copy-done | bytes 1572888
  13.3 0.7 %copy-done.2 = s32[32]{0:T(128)S(1)} copy-done((s32[32]{0:T(128)S(1)}, s32[32]{0:T(128)}, u32[]{:S(2)}) %copy-start.2) | copy-done | bytes 152
  14.0 1.6 %pack.1 = (bf16[2,6,32,128]{3,2,1,0:T(8,128)(2,1)S(1)}, bf16[2,2,6,32,128]{4,3,2,1,0:T(8,128)(2,1)S(1)}, bf16[2,2,6,32,128]{4,3,2,1,0:T(8,128)(2,1)S(1)}, bf16[2...) custom-call(s32[32]{0:T(128)S(1)} %copy-done.2, ...), custom_call_target="tpu_custom_call" | custom-call | tf_op jit(solution)/shard_map/pack/pallas_call | solution.py:157
  15.5 2.6 %collective-permute-start.10 = (bf16[2,2,6,32,128]{4,3,2,1,0:T(8,128)(2,1)S(1)}, bf16[2,2,6,32,128]{4,3,2,1,0:T(8,128)(2,1)S(1)}, u32[]{:S(2)}, u32[]{:S(2)}) collective-permute-start(bf16[2,2,6,32,128]{4,3,2,1,0:T(8,128)(2,1)S(1)} %get-tuple-element.32), channel_id=1, source_target_pairs={{0,4},{1,7},{2,6},{3,5},{4,0},{5,3},{6,2},{7,1},{8,12},{9,15},{10,... | collective-permute-start | bytes 589832 | tf_op jit(solution)/shard_map/ppermute | solution.py:144
  18.1 2.0 %collective-permute-start.12 = (bf16[2,2,6,32,128]{4,3,2,1,0:T(8,128)(2,1)S(1)}, bf16[2,2,6,32,128]{4,3,2,1,0:T(8,128)(2,1)S(1)}, u32[]{:S(2)}, u32[]{:S(2)}) collective-permute-start(bf16[2,2,6,32,128]{4,3,2,1,0:T(8,128)(2,1)S(1)} %get-tuple-element.34), channel_id=1, source_target_pairs={{0,12},{1,15},{2,14},{3,13},{4,8},{5,11},{6,10},{7,9},{8,4},{9,7},... | collective-permute-start | bytes 589832 | tf_op jit(solution)/shard_map/ppermute | solution.py:144
  20.1 0.5 %collective-permute-start.9 = (bf16[2,6,32,128]{3,2,1,0:T(8,128)(2,1)S(1)}, bf16[2,6,32,128]{3,2,1,0:T(8,128)(2,1)S(1)}, u32[]{:S(2)}, u32[]{:S(2)}) collective-permute-start(bf16[2,6,32,128]{3,2,1,0:T(8,128)(2,1)S(1)} %get-tuple-element.31), channel_id=1, source_target_pairs={{0,2},{1,3},{2,0},{3,1},{4,6},{5,7},{6,4},{7,5},{8,10},{9,11},{10,... | collective-permute-start | bytes 294920 | tf_op jit(solution)/shard_map/ppermute | solution.py:144
  20.6 0.3 factor.1.factor_ref
  20.9 6.1 %collective-permute-done.9.side_ref = bf16[2,6,32,128]{3,2,1,0:T(8,128)(2,1)S(1)} collective-permute-done((bf16[2,6,32,128]{3,2,1,0:T(8,128)(2,1)S(1)}, bf16[2,6,32,128]{3,2,1,0:T(8,128)(2,1)S(1)}, u32[]{:S(2)}, u32[]{:S(2)}) %collective-permute-start.9) | collective-permute-done | bytes 98336 | tf_op jit(solution)/shard_map/ppermute | solution.py:144
  27.0 4.2 %collective-permute-done.11.refs_1_ = bf16[2,2,6,32,128]{4,3,2,1,0:T(8,128)(2,1)S(1)} collective-permute-done((bf16[2,2,6,32,128]{4,3,2,1,0:T(8,128)(2,1)S(1)}, bf16[2,2,6,32,128]{4,3,2,1,0:T(8,128)(2,1)S(1)}, u32[]{:S(2)}, u32[]{:S(2)}) %collective-permute-start.11) | collective-permute-done | bytes 196640 | tf_op jit(solution)/shard_map/ppermute | solution.py:144
  31.2 6.7 %collective-permute-done.12.refs_2_ = bf16[2,2,6,32,128]{4,3,2,1,0:T(8,128)(2,1)S(1)} collective-permute-done((bf16[2,2,6,32,128]{4,3,2,1,0:T(8,128)(2,1)S(1)}, bf16[2,2,6,32,128]{4,3,2,1,0:T(8,128)(2,1)S(1)}, u32[]{:S(2)}, u32[]{:S(2)}) %collective-permute-start.12) | collective-permute-done | bytes 196640 | tf_op jit(solution)/shard_map/ppermute | solution.py:144
  37.9 0.5 %collective-permute-start.14 = (bf16[2,2,6,32,128]{4,3,2,1,0:T(8,128)(2,1)S(1)}, bf16[2,2,6,32,128]{4,3,2,1,0:T(8,128)(2,1)S(1)}, u32[]{:S(2)}, u32[]{:S(2)}) collective-permute-start(bf16[2,2,6,32,128]{4,3,2,1,0:T(8,128)(2,1)S(1)} %collective-permute-done.11.refs_1_), channel_id=1, source_target_pairs={{0,1},{1,0},{2,3},{3,2},{4,5},{5,4},{6,7},{7,6},{8,9},{9,8},{10,11... | collective-permute-start | bytes 589832 | tf_op jit(solution)/shard_map/ppermute | solution.py:137
  38.4 0.0 collective-permute-start.15
  38.4 0.9 %collective-permute-done.13.refs_3_ = bf16[2,2,6,32,128]{4,3,2,1,0:T(8,128)(2,1)S(1)} collective-permute-done((bf16[2,2,6,32,128]{4,3,2,1,0:T(8,128)(2,1)S(1)}, bf16[2,2,6,32,128]{4,3,2,1,0:T(8,128)(2,1)S(1)}, u32[]{:S(2)}, u32[]{:S(2)}) %collective-permute-start.13) | collective-permute-done | bytes 196640 | tf_op jit(solution)/shard_map/ppermute | solution.py:137
  39.3 0.3 collective-permute-done.14.refs_4_
  39.6 0.3 collective-permute-done.15.refs_5_
  39.9 2.9 %exchange.1 = f32[2,768,768]{2,1,0:T(8,128)} custom-call(s32[8,128]{1,0:T(8,128)S(1)} %get-tuple-element.30.info_ref, bf16[256,256]{1,0:T(8,128)(2,1)S(1)} %factor.1.factor_ref, bf16[2,6,32,128]{3,2,1,0:T(8,128)(2,1)S(1)} %get-tuple-element.38.self_ref, bf16[2,6,32,128]{3,2,1,0:T(8,128)(2,1)S(1)} %collective-permute-done.9.side_ref, ...), custom_call_target="tpu_custom_call" | custom-call | tf_op jit(solution)/shard_map/exchange/pallas_call | solution.py:184
  (11 shorter events, 0.0 us)
Async XLA Ops:
  0.0 1.6 %collective-permute-start = (s32[2]{0:T(128)}, s32[2]{0:T(128)S(1)}, u32[]{:S(2)}, u32[]{:S(2)}) collective-permute-start(s32[2]{0:T(128)} %param.7), channel_id=1, source_target_pairs={{0,1},{1,0},{2,3},{3,2},{4,5},{5,4},{6,7},{7,6},{8,9},{9,8},{10,11... | collective-permute-start | bytes 32 | tf_op jit(solution)/shard_map/ppermute | solution.py:137
  1.6 18.9 %copy-start.1 = (bf16[16,16]{1,0:T(8,128)(2,1)S(1)}, bf16[16,16]{1,0:T(8,128)(2,1)}, u32[]{:S(2)}) copy-start(bf16[16,16]{1,0:T(8,128)(2,1)} %metric_ref) | copy-start | bytes 1540
  2.4 9.5 %collective-permute-start.8 = (bf16[32,6,32,128]{3,2,1,0:T(8,128)(2,1)}, bf16[32,6,32,128]{3,2,1,0:T(8,128)(2,1)S(1)}, u32[]{:S(2)}, u32[]{:S(2)}) collective-permute-start(bf16[32,6,32,128]{3,2,1,0:T(8,128)(2,1)} %bitcast.3), channel_id=1, source_target_pairs={{0,1},{1,0},{2,3},{3,2},{4,5},{5,4},{6,7},{7,6},{8,9},{9,8},{10,11... | collective-permute-start | bytes 4718600 | tf_op jit(solution)/shard_map/ppermute | solution.py:137
  2.7 5.5 %collective-permute-start.4 = (s32[128]{0:T(128)S(1)}, s32[128]{0:T(128)S(1)}, u32[]{:S(2)}, u32[]{:S(2)}) collective-permute-start(s32[128]{0:T(128)S(1)} %pad_add_fusion.refs_0_), channel_id=1, source_target_pairs={{0,12},{1,15},{2,14},{3,13},{4,8},{5,11},{6,10},{7,9},{8,4},{9,7},... | collective-permute-start | bytes 1544 | tf_op jit(solution)/shard_map/ppermute | solution.py:144
  3.8 4.4 %collective-permute-start.3 = (s32[128]{0:T(128)S(1)}, s32[128]{0:T(128)S(1)}, u32[]{:S(2)}, u32[]{:S(2)}) collective-permute-start(s32[128]{0:T(128)S(1)} %pad_add_fusion.refs_0_), channel_id=1, source_target_pairs={{0,8},{1,11},{2,10},{3,9},{4,12},{5,15},{6,14},{7,13},{8,0},{9,3},... | collective-permute-start | bytes 1544 | tf_op jit(solution)/shard_map/ppermute | solution.py:144
  7.0 3.3 %collective-permute-start.2 = (s32[128]{0:T(128)S(1)}, s32[128]{0:T(128)S(1)}, u32[]{:S(2)}, u32[]{:S(2)}) collective-permute-start(s32[128]{0:T(128)S(1)} %pad_add_fusion.refs_0_), channel_id=1, source_target_pairs={{0,4},{1,7},{2,6},{3,5},{4,0},{5,3},{6,2},{7,1},{8,12},{9,15},{10,... | collective-permute-start | bytes 1544 | tf_op jit(solution)/shard_map/ppermute | solution.py:144
  7.2 3.1 %collective-permute-start.1 = (s32[128]{0:T(128)S(1)}, s32[128]{0:T(128)S(1)}, u32[]{:S(2)}, u32[]{:S(2)}) collective-permute-start(s32[128]{0:T(128)S(1)} %pad_add_fusion.refs_0_), channel_id=1, source_target_pairs={{0,2},{1,3},{2,0},{3,1},{4,6},{5,7},{6,4},{7,5},{8,10},{9,11},{10,... | collective-permute-start | bytes 1544 | tf_op jit(solution)/shard_map/ppermute | solution.py:144
  10.3 1.1 %collective-permute-start.5 = (s32[128]{0:T(128)S(1)}, s32[128]{0:T(128)S(1)}, u32[]{:S(2)}, u32[]{:S(2)}) collective-permute-start(s32[128]{0:T(128)S(1)} %collective-permute-done.2.refs_2_), channel_id=1, source_target_pairs={{0,1},{1,0},{2,3},{3,2},{4,5},{5,4},{6,7},{7,6},{8,9},{9,8},{10,11... | collective-permute-start | bytes 1544 | tf_op jit(solution)/shard_map/ppermute | solution.py:137
  10.4 1.2 %collective-permute-start.6 = (s32[128]{0:T(128)S(1)}, s32[128]{0:T(128)S(1)}, u32[]{:S(2)}, u32[]{:S(2)}) collective-permute-start(s32[128]{0:T(128)S(1)} %collective-permute-done.3.refs_4_), channel_id=1, source_target_pairs={{0,1},{1,0},{2,3},{3,2},{4,5},{5,4},{6,7},{7,6},{8,9},{9,8},{10,11... | collective-permute-start | bytes 1544 | tf_op jit(solution)/shard_map/ppermute | solution.py:137
  10.8 1.1 %collective-permute-start.7 = (s32[128]{0:T(128)S(1)}, s32[128]{0:T(128)S(1)}, u32[]{:S(2)}, u32[]{:S(2)}) collective-permute-start(s32[128]{0:T(128)S(1)} %collective-permute-done.4.refs_6_), channel_id=1, source_target_pairs={{0,1},{1,0},{2,3},{3,2},{4,5},{5,4},{6,7},{7,6},{8,9},{9,8},{10,11... | collective-permute-start | bytes 1544 | tf_op jit(solution)/shard_map/ppermute | solution.py:137
  11.9 1.4 %copy-start = (bf16[1,32,32,6,128]{4,2,3,1,0:T(8,128)(2,1)S(1)}, bf16[1,32,32,6,128]{4,2,3,1,0:T(8,128)(2,1)}, u32[]{:S(2)}) copy-start(bf16[1,32,32,6,128]{4,2,3,1,0:T(8,128)(2,1)} %param.4) | copy-start | bytes 4718596
  13.3 0.7 %copy-start.2 = (s32[32]{0:T(128)S(1)}, s32[32]{0:T(128)}, u32[]{:S(2)}) copy-start(s32[32]{0:T(128)} %owner_ref.1) | copy-start | bytes 388
  15.5 11.4 %collective-permute-start.10 = (bf16[2,2,6,32,128]{4,3,2,1,0:T(8,128)(2,1)S(1)}, bf16[2,2,6,32,128]{4,3,2,1,0:T(8,128)(2,1)S(1)}, u32[]{:S(2)}, u32[]{:S(2)}) collective-permute-start(bf16[2,2,6,32,128]{4,3,2,1,0:T(8,128)(2,1)S(1)} %get-tuple-element.32), channel_id=1, source_target_pairs={{0,4},{1,7},{2,6},{3,5},{4,0},{5,3},{6,2},{7,1},{8,12},{9,15},{10,... | collective-permute-start | bytes 589832 | tf_op jit(solution)/shard_map/ppermute | solution.py:144
  18.1 13.1 %collective-permute-start.11 = (bf16[2,2,6,32,128]{4,3,2,1,0:T(8,128)(2,1)S(1)}, bf16[2,2,6,32,128]{4,3,2,1,0:T(8,128)(2,1)S(1)}, u32[]{:S(2)}, u32[]{:S(2)}) collective-permute-start(bf16[2,2,6,32,128]{4,3,2,1,0:T(8,128)(2,1)S(1)} %get-tuple-element.33), channel_id=1, source_target_pairs={{0,8},{1,11},{2,10},{3,9},{4,12},{5,15},{6,14},{7,13},{8,0},{9,3},... | collective-permute-start | bytes 589832 | tf_op jit(solution)/shard_map/ppermute | solution.py:144
  18.1 19.8 %collective-permute-start.12 = (bf16[2,2,6,32,128]{4,3,2,1,0:T(8,128)(2,1)S(1)}, bf16[2,2,6,32,128]{4,3,2,1,0:T(8,128)(2,1)S(1)}, u32[]{:S(2)}, u32[]{:S(2)}) collective-permute-start(bf16[2,2,6,32,128]{4,3,2,1,0:T(8,128)(2,1)S(1)} %get-tuple-element.34), channel_id=1, source_target_pairs={{0,12},{1,15},{2,14},{3,13},{4,8},{5,11},{6,10},{7,9},{8,4},{9,7},... | collective-permute-start | bytes 589832 | tf_op jit(solution)/shard_map/ppermute | solution.py:144
  20.1 6.9 %collective-permute-start.9 = (bf16[2,6,32,128]{3,2,1,0:T(8,128)(2,1)S(1)}, bf16[2,6,32,128]{3,2,1,0:T(8,128)(2,1)S(1)}, u32[]{:S(2)}, u32[]{:S(2)}) collective-permute-start(bf16[2,6,32,128]{3,2,1,0:T(8,128)(2,1)S(1)} %get-tuple-element.31), channel_id=1, source_target_pairs={{0,2},{1,3},{2,0},{3,1},{4,6},{5,7},{6,4},{7,5},{8,10},{9,11},{10,... | collective-permute-start | bytes 294920 | tf_op jit(solution)/shard_map/ppermute | solution.py:144
  37.9 1.4 %collective-permute-start.13 = (bf16[2,2,6,32,128]{4,3,2,1,0:T(8,128)(2,1)S(1)}, bf16[2,2,6,32,128]{4,3,2,1,0:T(8,128)(2,1)S(1)}, u32[]{:S(2)}, u32[]{:S(2)}) collective-permute-start(bf16[2,2,6,32,128]{4,3,2,1,0:T(8,128)(2,1)S(1)} %collective-permute-done.10.refs_0_), channel_id=1, source_target_pairs={{0,1},{1,0},{2,3},{3,2},{4,5},{5,4},{6,7},{7,6},{8,9},{9,8},{10,11... | collective-permute-start | bytes 589832 | tf_op jit(solution)/shard_map/ppermute | solution.py:137
  37.9 1.7 %collective-permute-start.14 = (bf16[2,2,6,32,128]{4,3,2,1,0:T(8,128)(2,1)S(1)}, bf16[2,2,6,32,128]{4,3,2,1,0:T(8,128)(2,1)S(1)}, u32[]{:S(2)}, u32[]{:S(2)}) collective-permute-start(bf16[2,2,6,32,128]{4,3,2,1,0:T(8,128)(2,1)S(1)} %collective-permute-done.11.refs_1_), channel_id=1, source_target_pairs={{0,1},{1,0},{2,3},{3,2},{4,5},{5,4},{6,7},{7,6},{8,9},{9,8},{10,11... | collective-permute-start | bytes 589832 | tf_op jit(solution)/shard_map/ppermute | solution.py:137
  38.4 1.5 %collective-permute-start.15 = (bf16[2,2,6,32,128]{4,3,2,1,0:T(8,128)(2,1)S(1)}, bf16[2,2,6,32,128]{4,3,2,1,0:T(8,128)(2,1)S(1)}, u32[]{:S(2)}, u32[]{:S(2)}) collective-permute-start(bf16[2,2,6,32,128]{4,3,2,1,0:T(8,128)(2,1)S(1)} %collective-permute-done.12.refs_2_), channel_id=1, source_target_pairs={{0,1},{1,0},{2,3},{3,2},{4,5},{5,4},{6,7},{7,6},{8,9},{9,8},{10,11... | collective-permute-start | bytes 589832 | tf_op jit(solution)/shard_map/ppermute | solution.py:137

commit v3 on v2

v3 whole, which is shorter than its diff:
```python
import functools

import jax
import jax.numpy as jnp
from jax import lax
from jax.experimental import pallas as pl
from jax.experimental.pallas import tpu as pltpu
from jax.sharding import PartitionSpec as P

VMEM = pl.BlockSpec(memory_space=pltpu.VMEM)
HBM = pl.BlockSpec(memory_space=pltpu.HBM)
GROUP = 16
EARLY = 2
LIMIT = pltpu.CompilerParams(vmem_limit_bytes=12 * 1024 * 1024)


def position():
    me = lax.axis_index("aux")
    return me // 2, lax.bitwise_and(me, 1)


def factor_kernel(metric_ref, _, factor_ref):
    wide, aux = factor_ref.shape[0], metric_ref.shape[0]
    chip, core = position()
    row = lax.broadcasted_iota(jnp.int32, (wide, aux), 0) // GROUP
    column = lax.broadcasted_iota(jnp.int32, (wide, aux), 1)
    pick = (row == column).astype(jnp.bfloat16)
    place = row // 2
    far = jnp.where(place < 2, 0, lax.bitwise_and(place, 1))
    away = jnp.where(place < 2, place, lax.bitwise_xor(place, core))
    origin = 2 * lax.bitwise_xor(away, chip) + lax.bitwise_xor(lax.bitwise_xor(lax.bitwise_and(row, 1), far), core)
    pick_origin = (origin == column).astype(jnp.bfloat16)
    tall = jnp.dot(pick, metric_ref[...], preferred_element_type=jnp.float32).astype(jnp.bfloat16)
    spread = lax.dot_general(tall, pick_origin, (((1,), (1,)), ((), ())), preferred_element_type=jnp.float32)
    same = lax.rem(lax.broadcasted_iota(jnp.int32, (wide, wide), 0), GROUP) == lax.rem(
        lax.broadcasted_iota(jnp.int32, (wide, wide), 1), GROUP
    )
    factor_ref[...] = jnp.where(same, spread, 0.0).astype(jnp.bfloat16)


def place_blocks(small_ref, ids, held, sem):
    copy = pltpu.make_async_copy(small_ref, ids, sem)
    copy.start()
    copy.wait()

    def place(o, carry):
        held[ids[o]] = o
        return carry

    lax.fori_loop(0, held.shape[0], place, 0, unroll=True)


def served(k, f, chip, core):
    there = lax.bitwise_xor(chip, 2 * k + core)
    return 2 * there + (core if f == 0 else 1 - core)


def early_kernel(hops, small_ref, raw_ref, *refs):
    *outs, ids, held, sem = refs
    place_blocks(small_ref, ids, held, sem)
    blocks, tile = raw_ref.shape[0], raw_ref.shape[2]
    chip, core = position()
    lane = lax.broadcasted_iota(jnp.int32, (tile, 128), 1)
    mine = jnp.zeros((tile, 128), jnp.int32)
    for n in range(4):
        mine = jnp.where(lane == n, ids[blocks + n], mine)
    mine = mine.astype(jnp.float32).astype(jnp.bfloat16)
    for k, out in zip(hops, outs):
        if k > 0:
            for f in range(2):
                for w in range(2):
                    block = held[2 * served(k, f, chip, core) + w]
                    for s in range(EARLY):
                        out[(f * 2 + w) * EARLY + s] = raw_ref[block, s]
        if out.shape[0] % 2:
            out[out.shape[0] - 1] = mine


def counts_kernel(*refs):
    *got, out = refs
    for n, ref in enumerate(got):
        out[n : n + 1, :] = ref[ref.shape[0] - 1, 0:16, :].astype(jnp.float32)[0:1, :].astype(jnp.int32)


def late_kernel(hops, small_ref, counts_ref, crossed_ref, own_raw, peer_raw, *refs):
    outs = refs[: len(hops)]
    ids, held, direct, crossed, sem, sems = refs[-6:]
    blocks, slots = own_raw.shape[0], own_raw.shape[1]
    chip, core = position()
    copies = [
        pltpu.make_async_copy(counts_ref, direct, sems.at[0]),
        pltpu.make_async_copy(crossed_ref, crossed, sems.at[1]),
    ]
    for copy in copies:
        copy.start()
    place_blocks(small_ref, ids, held, sem)
    for copy in copies:
        copy.wait()

    def live(block):
        m = lax.bitwise_xor(block // 4, chip)
        far = lax.bitwise_and(lax.bitwise_xor(m, core), 1)
        sender = jnp.where(m >= 2, lax.bitwise_xor(core, far), core)
        line = 2 * lax.bitwise_xor(lax.bitwise_and(block // 2, 1), sender) + lax.bitwise_and(block, 1)
        near = jnp.where(m == 0, ids[blocks + line], direct[0, line])
        return jnp.where(m < 2, near, jnp.where(far == 0, direct[m // 2, line], crossed[m // 2, line]))

    def fill(target, at, raw, first, second, count, start):
        for j in range(slots - start if start == 0 else slots - 1 - start):
            from_first = j + start < count
            block = jnp.where(from_first, first, second)
            slot = jnp.where(from_first, j + start, (slots - 1 if start == 0 else slots - 2) - j)
            target[at + j] = raw[block, slot]

    def send(dest, target, start):
        first, second = held[2 * dest], held[2 * dest + 1]
        count = live(first)
        fill(target, 0, own_raw, first, second, count, start)
        fill(target, target.shape[0] // 2, peer_raw, first, second, count, start)
        return count, second

    for k, out in zip(hops, outs):
        if k > 0:
            for f in range(2):
                send(served(k, f, chip, core), out.at[f], EARLY)
        else:
            self_ref, info_ref = refs[len(hops) : len(hops) + 2]
            send(2 * lax.bitwise_xor(chip, 1) + core, out, 0)
            count, second = send(2 * chip + core, self_ref, 0)
            row = lax.broadcasted_iota(jnp.int32, info_ref.shape, 0)
            info_ref[...] = jnp.where(row == 0, count, live(second))


def forward_kernel(*refs):
    *got, out = refs
    for n, ref in enumerate(got):
        out[n * 2 * EARLY : (n + 1) * 2 * EARLY] = ref[2 * EARLY : 4 * EARLY]


def exchange_kernel(chips, info_ref, factor_ref, self_ref, side_ref, *refs):
    half = chips // 2
    first, refs = refs[: half - 1], refs[half - 1 :]
    second, refs = refs[: half - 1], refs[half - 1 :]
    forwarded, refs = refs[0], refs[1:]
    third, third_crossed, refs = refs[: half - 1], refs[half - 1 : 2 * half - 2], refs[2 * half - 2 :]
    out_ref, rows, stage, sems = refs
    doubled, orbitals, width = self_ref.shape
    slots = doubled // 2
    wide = factor_ref.shape[0]
    first_live = info_ref[0:1, :]

    def choose(s, early, late, at):
        mirror = slots - 1 - s
        ours = early(s) if s < EARLY else late(s - EARLY) if s < slots - 1 else None
        theirs = early(EARLY + mirror) if mirror < EARLY else late(slots - 2 - mirror) if mirror < slots - 1 else None
        if ours is None or theirs is None:
            return theirs if ours is None else ours
        return jnp.where(first_live > s, ours.astype(jnp.float32), theirs.astype(jnp.float32)).astype(ours.dtype)

    def pieces(s, start):
        at = slice(start, start + GROUP)
        found = []
        for ref in (self_ref, side_ref):
            found += [ref[q * slots + s, at, :] for q in range(2)]
        own_late = slots - 1 - EARLY
        for k in range(1, half):
            for f in range(2):
                late_ref = (third, third_crossed)[f][k - 1]
                for q in range(2):
                    base = q * own_late
                    if f == 0:
                        early_ref, early_base = (first, second)[q][k - 1], 0
                    else:
                        early_ref, early_base = forwarded, 2 * EARLY * (k - 1 + q * (half - 1))
                    found.append(
                        choose(
                            s,
                            lambda n, ref=early_ref, base=early_base: ref[base + n, at, :],
                            lambda n, ref=late_ref, base=base, f=f: ref[f, base + n, at, :],
                            at,
                        )
                    )
        return jnp.concatenate(found, axis=0)

    def span(n):
        return slice(n * width, (n + 1) * width)

    for part in range(orbitals // GROUP):
        columns = [pieces(s, part * GROUP) for s in range(slots)]
        fitted = jnp.dot(factor_ref[...], jnp.concatenate(columns, axis=1), preferred_element_type=jnp.float32)
        rows[part * wide : (part + 1) * wide, :] = fitted.astype(jnp.bfloat16)

    live = [info_ref[0:1, :], info_ref[1:2, :]]
    for s in range(slots):
        product = lax.dot_general(
            rows[:, span(s)], rows[...], (((0,), (0,)), ((), ())), preferred_element_type=jnp.float32
        )
        for which in range(2):
            row = s if which == 0 else slots - 1 - s
            for t in range(slots):
                column = t if which == 0 else slots - 1 - t
                stage[which, span(row), span(column)] = jnp.where(
                    live[which] > max(row, column), product[:, span(t)], 0.0
                )
            pltpu.make_async_copy(
                stage.at[which, span(row)], out_ref.at[which, span(row)], sems.at[which, row]
            ).start()
    for which in range(2):
        for row in range(slots):
            pltpu.make_async_copy(
                stage.at[which, span(row)], out_ref.at[which, span(row)], sems.at[which, row]
            ).wait()


def shards(devices, raw_tiles, metric, owner_map, counts):
    chips = devices // 2
    half = chips // 2
    _, blocks, orbitals, slots, width = raw_tiles.shape
    lines = -(-(blocks + 4) // 128) * 128
    raw = raw_tiles[0].transpose(0, 2, 1, 3)
    tie = lax.optimization_barrier

    def swap(x):
        return lax.ppermute(x, "aux", [(i, i ^ 1) for i in range(devices)])

    def hop(x, k):
        def target(i):
            away = 1 if k == 0 else 2 * k + i % 2
            return (i // 2 ^ away) * 2 + i % 2

        return lax.ppermute(x, "aux", [(i, target(i)) for i in range(devices)])

    def shape(*dims):
        return jax.ShapeDtypeStruct(dims, raw.dtype)

    factor = pl.pallas_call(
        factor_kernel,
        out_shape=shape(devices * GROUP, devices * GROUP),
        in_specs=[VMEM, HBM],
        out_specs=VMEM,
        compiler_params=pltpu.CompilerParams(vmem_limit_bytes=61 * 1024 * 1024),
        name="factor",
    )(metric, raw)
    other, factor = tie((swap(counts), factor))
    small = jnp.concatenate([owner_map, counts, other, jnp.zeros((lines - blocks - 4,), jnp.int32)])
    raw_there, small = tie((raw, small))
    peer_raw = swap(raw_there)

    far = [*reversed(range(2, half))]
    near = [1, 0]
    place = [pltpu.SMEM((lines,), jnp.int32), pltpu.SMEM((blocks,), jnp.int32)]
    one = pltpu.SemaphoreType.DMA(())

    def early(hops, raw, counted):
        return pl.pallas_call(
            functools.partial(early_kernel, hops),
            out_shape=[shape((4 * EARLY if k else 0) + counted, orbitals, width) for k in hops],
            in_specs=[VMEM] * 2,
            out_specs=[VMEM] * len(hops),
            scratch_shapes=place + [one],
            compiler_params=LIMIT,
            name="early",
        )(small, raw)

    def hops(ks, xs):
        return [hop(x, k) for k, x in zip(ks, xs)]

    first = hops(far + near, early(far + near, raw, 1))
    *second, second_near = early(far + near[:1], peer_raw, 0)
    second = hops(far, second)
    first = tie(first)[::-1]
    brought = pl.pallas_call(
        counts_kernel,
        out_shape=jax.ShapeDtypeStruct((half, 128), jnp.int32),
        in_specs=[VMEM] * half,
        out_specs=VMEM,
        compiler_params=LIMIT,
        name="counts",
    )(*first)
    brought_there = swap(brought)

    def late(ks, small, extra=()):
        own = slots - 1 - EARLY
        out_shape = [shape(2, 2 * own, orbitals, width) if k else shape(2 * slots, orbitals, width) for k in ks]
        out_shape += extra
        return pl.pallas_call(
            functools.partial(late_kernel, ks),
            out_shape=out_shape,
            in_specs=[VMEM] * 5,
            out_specs=[VMEM] * len(out_shape),
            scratch_shapes=place
            + [pltpu.SMEM((half, 128), jnp.int32)] * 2
            + [one, pltpu.SemaphoreType.DMA((2,))],
            compiler_params=LIMIT,
            cost_estimate=pl.CostEstimate(flops=0, bytes_accessed=1024, transcendentals=0),
            name="late",
        )(small, brought, brought_there, raw, peer_raw)

    *third, own, info = late(
        far + near, small, [shape(2 * slots, orbitals, width), jax.ShapeDtypeStruct((8, 128), jnp.int32)]
    )
    third, second, second_near = tie((third, second, second_near))
    second_near, *third = tie(hops(near[:1] + far + near, [second_near, *third]))
    third = third[::-1]
    second = [second_near, *second[::-1]]
    forwarded = pl.pallas_call(
        forward_kernel,
        out_shape=shape((2 * half - 2) * 2 * EARLY, orbitals, width),
        in_specs=[VMEM] * (2 * half - 2),
        out_specs=VMEM,
        compiler_params=LIMIT,
        name="forward",
    )(*first[1:], *second)
    forwarded = swap(forwarded)
    crossed = [swap(x) for x in third[1:]]

    return pl.pallas_call(
        functools.partial(exchange_kernel, chips),
        out_shape=jax.ShapeDtypeStruct((2, slots * width, slots * width), jnp.float32),
        in_specs=[VMEM] * (4 * half + 1),
        out_specs=pl.BlockSpec(memory_space=pl.ANY),
        scratch_shapes=[
            pltpu.VMEM((devices * orbitals, slots * width), raw.dtype),
            pltpu.VMEM((2, slots * width, slots * width), jnp.float32),
            pltpu.SemaphoreType.DMA((2, slots)),
        ],
        compiler_params=pltpu.CompilerParams(vmem_limit_bytes=32 * 1024 * 1024),
        name="exchange",
    )(info, factor, own, third[0], *first[1:], *second, forwarded, *third[1:], *crossed)


def solution(mesh):
    in_specs = (
        P(("grp", "aux"), None, None, None, None),
        P("grp", None),
        P("grp"),
        P(("grp", "aux")),
    )
    out_specs = P(("grp", "aux"), None, None)
    body = functools.partial(shards, mesh.shape["aux"])
    return jax.shard_map(body, mesh=mesh, in_specs=in_specs, out_specs=out_specs, check_vma=False)
```

time: 43 us -> 39 us (0.907)
  the two profiles are of different devices: /device:TPU:17 before, /device:TPU:0 now
where the time goes in v3:
time: 39 us; the launch traced here: 38.8 us
  starting transfers between devices  18.6 us (48%)
  waiting for transfers between devices  13.2 us (34%)
  Pallas kernels  6.77 us (17%)
    ppermute x11, starting transfers between devices, hop(): return lax.ppermute(x, 'aux', [(i, target(i)) for i in range(devices)])  16.7 us
    ppermute x11, waiting for transfers between devices, hop(): return lax.ppermute(x, 'aux', [(i, target(i)) for i in range(devices)])  11.2 us
    pallas_call x1, Pallas kernels, shards(): pl.pallas_call(functools.partial(exchange_kernel, chips), out_shape=jax.S...  2.93 us
    ppermute x7, waiting for transfers between devices, swap(): return lax.ppermute(x, 'aux', [(i, i ^ 1) for i in range(devices)])  1.97 us
    ppermute x7, starting transfers between devices, swap(): return lax.ppermute(x, 'aux', [(i, i ^ 1) for i in range(devices)])  1.94 us
    pallas_call x1, Pallas kernels, shards(): pl.pallas_call(factor_kernel, out_shape=shape(devices * GROUP, devices *...  1.64 us
    pallas_call x2, Pallas kernels, early(): pl.pallas_call(functools.partial(early_kernel, hops), out_shape=[shape((4...  1.23 us
    pallas_call x1, Pallas kernels, late(): pl.pallas_call(functools.partial(late_kernel, ks), out_shape=out_shape, i...  0.95 us
  transfers between devices with their start and end apart: 18, of which 8 were waited for; matrix products, arithmetic and copies ran while one was open for 0% of the time, Pallas kernels for 10%

profile of v3, /device:TPU:0, one launch (start us, length us, event | category | flops | bytes accessed | tf_op | source)
XLA Modules:
  0.0 38.8 jit_solution(10172394848300062727)
XLA Ops:
  0.0 0.5 %collective-permute-start = (s32[2]{0:T(128)}, s32[2]{0:T(128)S(1)}, u32[]{:S(2)}, u32[]{:S(2)}) collective-permute-start(s32[2]{0:T(128)} %param.7), channel_id=1, source_target_pairs={{0,1},{1,0},{2,3},{3,2},{4,5},{5,4},{6,7},{7,6},{8,9},{9,8},{10,11... | collective-permute-start | bytes 32 | tf_op jit(solution)/shard_map/ppermute | solution.py:224
  0.5 1.6 %factor.1.factor_ref = bf16[256,256]{1,0:T(8,128)(2,1)} custom-call(bf16[16,16]{1,0:T(8,128)(2,1)} %metric_ref.1, bf16[32,6,32,128]{3,2,1,0:T(8,128)(2,1)} %bitcast.3), custom_call_target="tpu_custom_call" | custom-call | tf_op jit(solution)/shard_map/factor/pallas_call | solution.py:236
  2.2 0.0 collective-permute-done
  2.2 0.1 pad_add_fusion.small_ref
  2.3 0.1 collective-permute-start.6
  2.4 0.6 %early.2 = (bf16[9,32,128]{2,1,0:T(8,128)(2,1)S(1)}, bf16[9,32,128]{2,1,0:T(8,128)(2,1)S(1)}, bf16[9,32,128]{2,1,0:T(8,128)(2,1)S(1)}, bf16[1,32,128]{2,1,0:T(8,128)(2,1)S(1)}) custom-call(s32[128]{0:T(128)S(1)} %pad_add_fusion.small_ref, bf16[32,6,32,128]{3,2,1,0:T(8,128)(2,1)S(1)} %bitcast.5), custom_call_target="tpu_custom_call" | custom-call | tf_op jit(solution)/shard_map/early/pallas_call | solution.py:255
  3.0 5.1 %collective-permute-start.1 = (bf16[9,32,128]{2,1,0:T(8,128)(2,1)S(1)}, bf16[9,32,128]{2,1,0:T(8,128)(2,1)S(1)}, u32[]{:S(2)}, u32[]{:S(2)}) collective-permute-start(bf16[9,32,128]{2,1,0:T(8,128)(2,1)S(1)} %get-tuple-element.40), channel_id=1, source_target_pairs={{0,12},{1,15},{2,14},{3,13},{4,8},{5,11},{6,10},{7,9},{8,4},{9,7},... | collective-permute-start | bytes 221192 | tf_op jit(solution)/shard_map/ppermute | solution.py:231
  8.1 0.6 %collective-permute-start.3 = (bf16[9,32,128]{2,1,0:T(8,128)(2,1)S(1)}, bf16[9,32,128]{2,1,0:T(8,128)(2,1)S(1)}, u32[]{:S(2)}, u32[]{:S(2)}) collective-permute-start(bf16[9,32,128]{2,1,0:T(8,128)(2,1)S(1)} %get-tuple-element.42), channel_id=1, source_target_pairs={{0,4},{1,7},{2,6},{3,5},{4,0},{5,3},{6,2},{7,1},{8,12},{9,15},{10,... | collective-permute-start | bytes 221192 | tf_op jit(solution)/shard_map/ppermute | solution.py:231
  8.7 1.7 %collective-permute-start.4 = (bf16[1,32,128]{2,1,0:T(8,128)(2,1)S(1)}, bf16[1,32,128]{2,1,0:T(8,128)(2,1)S(1)}, u32[]{:S(2)}, u32[]{:S(2)}) collective-permute-start(bf16[1,32,128]{2,1,0:T(8,128)(2,1)S(1)} %get-tuple-element.43), channel_id=1, source_target_pairs={{0,2},{1,3},{2,0},{3,1},{4,6},{5,7},{6,4},{7,5},{8,10},{9,11},{10,... | collective-permute-start | bytes 24584 | tf_op jit(solution)/shard_map/ppermute | solution.py:231
  10.4 0.6 %early.3 = (bf16[8,32,128]{2,1,0:T(8,128)(2,1)S(1)}, bf16[8,32,128]{2,1,0:T(8,128)(2,1)S(1)}, bf16[8,32,128]{2,1,0:T(8,128)(2,1)S(1)}) custom-call(s32[128]{0:T(128)S(1)} %pad_add_fusion.small_ref, bf16[32,6,32,128]{3,2,1,0:T(8,128)(2,1)S(1)} %collective-permute-done.6.peer_raw.raw_ref), custom_call_target="tpu_custom_call" | custom-call | tf_op jit(solution)/shard_map/early/pallas_call | solution.py:255
  11.0 3.7 %collective-permute-start.7 = (bf16[8,32,128]{2,1,0:T(8,128)(2,1)S(1)}, bf16[8,32,128]{2,1,0:T(8,128)(2,1)S(1)}, u32[]{:S(2)}, u32[]{:S(2)}) collective-permute-start(bf16[8,32,128]{2,1,0:T(8,128)(2,1)S(1)} %get-tuple-element.56), channel_id=1, source_target_pairs={{0,12},{1,15},{2,14},{3,13},{4,8},{5,11},{6,10},{7,9},{8,4},{9,7},... | collective-permute-start | bytes 196616 | tf_op jit(solution)/shard_map/ppermute | solution.py:231
  14.7 0.1 collective-permute-start.8
  14.7 0.5 %collective-permute-done.2.refs_2_.refs_1_ = bf16[9,32,128]{2,1,0:T(8,128)(2,1)S(1)} collective-permute-done((bf16[9,32,128]{2,1,0:T(8,128)(2,1)S(1)}, bf16[9,32,128]{2,1,0:T(8,128)(2,1)S(1)}, u32[]{:S(2)}, u32[]{:S(2)}) %collective-permute-start.2) | collective-permute-done | bytes 73760 | tf_op jit(solution)/shard_map/ppermute | solution.py:231
  15.3 0.0 copy-start.1
  15.3 0.2 collective-permute-start.5
  15.5 1.0 %collective-permute-done.5.crossed_ref = s32[4,128]{1,0:T(4,128)S(1)} collective-permute-done((s32[4,128]{1,0:T(4,128)S(1)}, s32[4,128]{1,0:T(4,128)S(1)}, u32[]{:S(2)}, u32[]{:S(2)}) %collective-permute-start.5) | collective-permute-done | bytes 2080 | tf_op jit(solution)/shard_map/ppermute | solution.py:224
  16.5 0.9 %late.1 = (bf16[2,6,32,128]{3,2,1,0:T(8,128)(2,1)S(1)}, bf16[2,6,32,128]{3,2,1,0:T(8,128)(2,1)S(1)}, bf16[2,6,32,128]{3,2,1,0:T(8,128)(2,1)S(1)}, bf16[12,32,128...) custom-call(s32[128]{0:T(128)S(1)} %pad_add_fusion.small_ref, ...), custom_call_target="tpu_custom_call" | custom-call | bytes 1024 | tf_op jit(solution)/shard_map/late/pallas_call | solution.py:286
  17.5 0.5 %collective-permute-done.7.refs_5_ = bf16[8,32,128]{2,1,0:T(8,128)(2,1)S(1)} collective-permute-done((bf16[8,32,128]{2,1,0:T(8,128)(2,1)S(1)}, bf16[8,32,128]{2,1,0:T(8,128)(2,1)S(1)}, u32[]{:S(2)}, u32[]{:S(2)}) %collective-permute-start.7) | collective-permute-done | bytes 65568 | tf_op jit(solution)/shard_map/ppermute | solution.py:231
  17.9 3.0 %collective-permute-done.8.refs_4_ = bf16[8,32,128]{2,1,0:T(8,128)(2,1)S(1)} collective-permute-done((bf16[8,32,128]{2,1,0:T(8,128)(2,1)S(1)}, bf16[8,32,128]{2,1,0:T(8,128)(2,1)S(1)}, u32[]{:S(2)}, u32[]{:S(2)}) %collective-permute-start.8) | collective-permute-done | bytes 65568 | tf_op jit(solution)/shard_map/ppermute | solution.py:231
  21.0 3.1 %collective-permute-start.10 = (bf16[2,6,32,128]{3,2,1,0:T(8,128)(2,1)S(1)}, bf16[2,6,32,128]{3,2,1,0:T(8,128)(2,1)S(1)}, u32[]{:S(2)}, u32[]{:S(2)}) collective-permute-start(bf16[2,6,32,128]{3,2,1,0:T(8,128)(2,1)S(1)} %get-tuple-element.60), channel_id=1, source_target_pairs={{0,12},{1,15},{2,14},{3,13},{4,8},{5,11},{6,10},{7,9},{8,4},{9,7},... | collective-permute-start | bytes 294920 | tf_op jit(solution)/shard_map/ppermute | solution.py:231
  24.1 1.3 %collective-permute-start.12 = (bf16[2,6,32,128]{3,2,1,0:T(8,128)(2,1)S(1)}, bf16[2,6,32,128]{3,2,1,0:T(8,128)(2,1)S(1)}, u32[]{:S(2)}, u32[]{:S(2)}) collective-permute-start(bf16[2,6,32,128]{3,2,1,0:T(8,128)(2,1)S(1)} %get-tuple-element.62), channel_id=1, source_target_pairs={{0,4},{1,7},{2,6},{3,5},{4,0},{5,3},{6,2},{7,1},{8,12},{9,15},{10,... | collective-permute-start | bytes 294920 | tf_op jit(solution)/shard_map/ppermute | solution.py:231
  25.4 0.7 %collective-permute-start.13 = (bf16[12,32,128]{2,1,0:T(8,128)(2,1)S(1)}, bf16[12,32,128]{2,1,0:T(8,128)(2,1)S(1)}, u32[]{:S(2)}, u32[]{:S(2)}) collective-permute-start(bf16[12,32,128]{2,1,0:T(8,128)(2,1)S(1)} %get-tuple-element.63), channel_id=1, source_target_pairs={{0,2},{1,3},{2,0},{3,1},{4,6},{5,7},{6,4},{7,5},{8,10},{9,11},{10,... | collective-permute-start | bytes 294920 | tf_op jit(solution)/shard_map/ppermute | solution.py:231
  26.1 0.6 %collective-permute-start.9 = (bf16[8,32,128]{2,1,0:T(8,128)(2,1)S(1)}, bf16[8,32,128]{2,1,0:T(8,128)(2,1)S(1)}, u32[]{:S(2)}, u32[]{:S(2)}) collective-permute-start(bf16[8,32,128]{2,1,0:T(8,128)(2,1)S(1)} %get-tuple-element.59), channel_id=1, source_target_pairs={{0,4},{1,7},{2,6},{3,5},{4,0},{5,3},{6,2},{7,1},{8,12},{9,15},{10,... | collective-permute-start | bytes 196616 | tf_op jit(solution)/shard_map/ppermute | solution.py:231
  26.6 7.2 %collective-permute-done.9.refs_3_ = bf16[8,32,128]{2,1,0:T(8,128)(2,1)S(1)} collective-permute-done((bf16[8,32,128]{2,1,0:T(8,128)(2,1)S(1)}, bf16[8,32,128]{2,1,0:T(8,128)(2,1)S(1)}, u32[]{:S(2)}, u32[]{:S(2)}) %collective-permute-start.9) | collective-permute-done | bytes 65568 | tf_op jit(solution)/shard_map/ppermute | solution.py:231
  33.9 0.1 collective-permute-start.14
  34.0 0.4 %collective-permute-start.15 = (bf16[2,6,32,128]{3,2,1,0:T(8,128)(2,1)S(1)}, bf16[2,6,32,128]{3,2,1,0:T(8,128)(2,1)S(1)}, u32[]{:S(2)}, u32[]{:S(2)}) collective-permute-start(bf16[2,6,32,128]{3,2,1,0:T(8,128)(2,1)S(1)} %collective-permute-done.12.refs_7_), channel_id=1, source_target_pairs={{0,1},{1,0},{2,3},{3,2},{4,5},{5,4},{6,7},{7,6},{8,9},{9,8},{10,11... | collective-permute-start | bytes 294920 | tf_op jit(solution)/shard_map/ppermute | solution.py:224
  34.4 0.1 collective-permute-start.16
  34.5 0.4 %collective-permute-start.17 = (bf16[2,6,32,128]{3,2,1,0:T(8,128)(2,1)S(1)}, bf16[2,6,32,128]{3,2,1,0:T(8,128)(2,1)S(1)}, u32[]{:S(2)}, u32[]{:S(2)}) collective-permute-start(bf16[2,6,32,128]{3,2,1,0:T(8,128)(2,1)S(1)} %collective-permute-done.10.refs_9_), channel_id=1, source_target_pairs={{0,1},{1,0},{2,3},{3,2},{4,5},{5,4},{6,7},{7,6},{8,9},{9,8},{10,11... | collective-permute-start | bytes 294920 | tf_op jit(solution)/shard_map/ppermute | solution.py:224
  34.9 0.6 %collective-permute-done.15.refs_10_ = bf16[2,6,32,128]{3,2,1,0:T(8,128)(2,1)S(1)} collective-permute-done((bf16[2,6,32,128]{3,2,1,0:T(8,128)(2,1)S(1)}, bf16[2,6,32,128]{3,2,1,0:T(8,128)(2,1)S(1)}, u32[]{:S(2)}, u32[]{:S(2)}) %collective-permute-start.15) | collective-permute-done | bytes 98336 | tf_op jit(solution)/shard_map/ppermute | solution.py:224
  35.5 0.2 collective-permute-done.16.refs_11_
  35.7 0.2 collective-permute-done.17.refs_12_
  35.9 2.9 %exchange.1 = f32[2,768,768]{2,1,0:T(8,128)} custom-call(s32[8,128]{1,0:T(8,128)S(1)} %get-tuple-element.49.info_ref, bf16[256,256]{1,0:T(8,128)(2,1)S(1)} %copy-done.1, bf16[12,32,128]{2,1,0:T(8,128)(2,1)S(1)} %get-tuple-element.51.self_ref, bf16[12,32,128]{2,1,0:T(8,128)(2,1)S(1)} %collective-permute-done.13.side_ref, ...), custom_call_target="tpu_custom_call" | custom-call | tf_op jit(solution)/shard_map/exchange/pallas_call | solution.py:317
  (21 shorter events, 0.1 us)
Async XLA Ops:
  0.0 2.2 %copy-start.2 = (s32[2]{0:T(128)S(1)}, s32[2]{0:T(128)}, u32[]{:S(2)}) copy-start(s32[2]{0:T(128)} %param.7) | copy-start | bytes 28
  0.0 2.3 %copy-start = (bf16[1,32,32,6,128]{4,2,3,1,0:T(8,128)(2,1)S(1)}, bf16[1,32,32,6,128]{4,2,3,1,0:T(8,128)(2,1)}, u32[]{:S(2)}) copy-start(bf16[1,32,32,6,128]{4,2,3,1,0:T(8,128)(2,1)} %param.4) | copy-start | bytes 4718596
  0.0 2.2 %copy-start.3 = (s32[32]{0:T(128)S(1)}, s32[32]{0:T(128)}, u32[]{:S(2)}) copy-start(s32[32]{0:T(128)} %param.6) | copy-start | bytes 388
  0.0 2.2 %collective-permute-start = (s32[2]{0:T(128)}, s32[2]{0:T(128)S(1)}, u32[]{:S(2)}, u32[]{:S(2)}) collective-permute-start(s32[2]{0:T(128)} %param.7), channel_id=1, source_target_pairs={{0,1},{1,0},{2,3},{3,2},{4,5},{5,4},{6,7},{7,6},{8,9},{9,8},{10,11... | collective-permute-start | bytes 32 | tf_op jit(solution)/shard_map/ppermute | solution.py:224
  2.3 8.1 %collective-permute-start.6 = (bf16[32,6,32,128]{3,2,1,0:T(8,128)(2,1)S(1)}, bf16[32,6,32,128]{3,2,1,0:T(8,128)(2,1)S(1)}, u32[]{:S(2)}, u32[]{:S(2)}) collective-permute-start(bf16[32,6,32,128]{3,2,1,0:T(8,128)(2,1)S(1)} %bitcast.4), channel_id=1, source_target_pairs={{0,1},{1,0},{2,3},{3,2},{4,5},{5,4},{6,7},{7,6},{8,9},{9,8},{10,11... | collective-permute-start | bytes 4718600 | tf_op jit(solution)/shard_map/ppermute | solution.py:224
  3.0 11.7 %collective-permute-start.1 = (bf16[9,32,128]{2,1,0:T(8,128)(2,1)S(1)}, bf16[9,32,128]{2,1,0:T(8,128)(2,1)S(1)}, u32[]{:S(2)}, u32[]{:S(2)}) collective-permute-start(bf16[9,32,128]{2,1,0:T(8,128)(2,1)S(1)} %get-tuple-element.40), channel_id=1, source_target_pairs={{0,12},{1,15},{2,14},{3,13},{4,8},{5,11},{6,10},{7,9},{8,4},{9,7},... | collective-permute-start | bytes 221192 | tf_op jit(solution)/shard_map/ppermute | solution.py:231
  8.1 7.2 %collective-permute-start.2 = (bf16[9,32,128]{2,1,0:T(8,128)(2,1)S(1)}, bf16[9,32,128]{2,1,0:T(8,128)(2,1)S(1)}, u32[]{:S(2)}, u32[]{:S(2)}) collective-permute-start(bf16[9,32,128]{2,1,0:T(8,128)(2,1)S(1)} %get-tuple-element.41), channel_id=1, source_target_pairs={{0,8},{1,11},{2,10},{3,9},{4,12},{5,15},{6,14},{7,13},{8,0},{9,3},... | collective-permute-start | bytes 221192 | tf_op jit(solution)/shard_map/ppermute | solution.py:231
  8.1 7.2 %collective-permute-start.3 = (bf16[9,32,128]{2,1,0:T(8,128)(2,1)S(1)}, bf16[9,32,128]{2,1,0:T(8,128)(2,1)S(1)}, u32[]{:S(2)}, u32[]{:S(2)}) collective-permute-start(bf16[9,32,128]{2,1,0:T(8,128)(2,1)S(1)} %get-tuple-element.42), channel_id=1, source_target_pairs={{0,4},{1,7},{2,6},{3,5},{4,0},{5,3},{6,2},{7,1},{8,12},{9,15},{10,... | collective-permute-start | bytes 221192 | tf_op jit(solution)/shard_map/ppermute | solution.py:231
  8.7 6.0 %collective-permute-start.4 = (bf16[1,32,128]{2,1,0:T(8,128)(2,1)S(1)}, bf16[1,32,128]{2,1,0:T(8,128)(2,1)S(1)}, u32[]{:S(2)}, u32[]{:S(2)}) collective-permute-start(bf16[1,32,128]{2,1,0:T(8,128)(2,1)S(1)} %get-tuple-element.43), channel_id=1, source_target_pairs={{0,2},{1,3},{2,0},{3,1},{4,6},{5,7},{6,4},{7,5},{8,10},{9,11},{10,... | collective-permute-start | bytes 24584 | tf_op jit(solution)/shard_map/ppermute | solution.py:231
  11.0 6.9 %collective-permute-start.7 = (bf16[8,32,128]{2,1,0:T(8,128)(2,1)S(1)}, bf16[8,32,128]{2,1,0:T(8,128)(2,1)S(1)}, u32[]{:S(2)}, u32[]{:S(2)}) collective-permute-start(bf16[8,32,128]{2,1,0:T(8,128)(2,1)S(1)} %get-tuple-element.56), channel_id=1, source_target_pairs={{0,12},{1,15},{2,14},{3,13},{4,8},{5,11},{6,10},{7,9},{8,4},{9,7},... | collective-permute-start | bytes 196616 | tf_op jit(solution)/shard_map/ppermute | solution.py:231
  14.7 6.3 %collective-permute-start.8 = (bf16[8,32,128]{2,1,0:T(8,128)(2,1)S(1)}, bf16[8,32,128]{2,1,0:T(8,128)(2,1)S(1)}, u32[]{:S(2)}, u32[]{:S(2)}) collective-permute-start(bf16[8,32,128]{2,1,0:T(8,128)(2,1)S(1)} %get-tuple-element.57), channel_id=1, source_target_pairs={{0,8},{1,11},{2,10},{3,9},{4,12},{5,15},{6,14},{7,13},{8,0},{9,3},... | collective-permute-start | bytes 196616 | tf_op jit(solution)/shard_map/ppermute | solution.py:231
  15.3 20.6 %copy-start.1 = (bf16[256,256]{1,0:T(8,128)(2,1)S(1)}, bf16[256,256]{1,0:T(8,128)(2,1)}, u32[]{:S(2)}) copy-start(bf16[256,256]{1,0:T(8,128)(2,1)} %factor.1.factor_ref) | copy-start | bytes 393220
  15.3 1.2 %collective-permute-start.5 = (s32[4,128]{1,0:T(4,128)S(1)}, s32[4,128]{1,0:T(4,128)S(1)}, u32[]{:S(2)}, u32[]{:S(2)}) collective-permute-start(s32[4,128]{1,0:T(4,128)S(1)} %counts.1.counts_ref), channel_id=1, source_target_pairs={{0,1},{1,0},{2,3},{3,2},{4,5},{5,4},{6,7},{7,6},{8,9},{9,8},{10,11... | collective-permute-start | bytes 6152 | tf_op jit(solution)/shard_map/ppermute | solution.py:224
  21.0 12.8 %collective-permute-start.10 = (bf16[2,6,32,128]{3,2,1,0:T(8,128)(2,1)S(1)}, bf16[2,6,32,128]{3,2,1,0:T(8,128)(2,1)S(1)}, u32[]{:S(2)}, u32[]{:S(2)}) collective-permute-start(bf16[2,6,32,128]{3,2,1,0:T(8,128)(2,1)S(1)} %get-tuple-element.60), channel_id=1, source_target_pairs={{0,12},{1,15},{2,14},{3,13},{4,8},{5,11},{6,10},{7,9},{8,4},{9,7},... | collective-permute-start | bytes 294920 | tf_op jit(solution)/shard_map/ppermute | solution.py:231
  24.1 9.7 %collective-permute-start.11 = (bf16[2,6,32,128]{3,2,1,0:T(8,128)(2,1)S(1)}, bf16[2,6,32,128]{3,2,1,0:T(8,128)(2,1)S(1)}, u32[]{:S(2)}, u32[]{:S(2)}) collective-permute-start(bf16[2,6,32,128]{3,2,1,0:T(8,128)(2,1)S(1)} %get-tuple-element.61), channel_id=1, source_target_pairs={{0,8},{1,11},{2,10},{3,9},{4,12},{5,15},{6,14},{7,13},{8,0},{9,3},... | collective-permute-start | bytes 294920 | tf_op jit(solution)/shard_map/ppermute | solution.py:231
  24.1 9.7 %collective-permute-start.12 = (bf16[2,6,32,128]{3,2,1,0:T(8,128)(2,1)S(1)}, bf16[2,6,32,128]{3,2,1,0:T(8,128)(2,1)S(1)}, u32[]{:S(2)}, u32[]{:S(2)}) collective-permute-start(bf16[2,6,32,128]{3,2,1,0:T(8,128)(2,1)S(1)} %get-tuple-element.62), channel_id=1, source_target_pairs={{0,4},{1,7},{2,6},{3,5},{4,0},{5,3},{6,2},{7,1},{8,12},{9,15},{10,... | collective-permute-start | bytes 294920 | tf_op jit(solution)/shard_map/ppermute | solution.py:231
  25.4 8.4 %collective-permute-start.13 = (bf16[12,32,128]{2,1,0:T(8,128)(2,1)S(1)}, bf16[12,32,128]{2,1,0:T(8,128)(2,1)S(1)}, u32[]{:S(2)}, u32[]{:S(2)}) collective-permute-start(bf16[12,32,128]{2,1,0:T(8,128)(2,1)S(1)} %get-tuple-element.63), channel_id=1, source_target_pairs={{0,2},{1,3},{2,0},{3,1},{4,6},{5,7},{6,4},{7,5},{8,10},{9,11},{10,... | collective-permute-start | bytes 294920 | tf_op jit(solution)/shard_map/ppermute | solution.py:231
  26.1 7.7 %collective-permute-start.9 = (bf16[8,32,128]{2,1,0:T(8,128)(2,1)S(1)}, bf16[8,32,128]{2,1,0:T(8,128)(2,1)S(1)}, u32[]{:S(2)}, u32[]{:S(2)}) collective-permute-start(bf16[8,32,128]{2,1,0:T(8,128)(2,1)S(1)} %get-tuple-element.59), channel_id=1, source_target_pairs={{0,4},{1,7},{2,6},{3,5},{4,0},{5,3},{6,2},{7,1},{8,12},{9,15},{10,... | collective-permute-start | bytes 196616 | tf_op jit(solution)/shard_map/ppermute | solution.py:231
  33.9 2.0 %collective-permute-start.14 = (bf16[24,32,128]{2,1,0:T(8,128)(2,1)S(1)}, bf16[24,32,128]{2,1,0:T(8,128)(2,1)S(1)}, u32[]{:S(2)}, u32[]{:S(2)}) collective-permute-start(bf16[24,32,128]{2,1,0:T(8,128)(2,1)S(1)} %forward.1), channel_id=1, source_target_pairs={{0,1},{1,0},{2,3},{3,2},{4,5},{5,4},{6,7},{7,6},{8,9},{9,8},{10,11... | collective-permute-start | bytes 589832 | tf_op jit(solution)/shard_map/ppermute | solution.py:224
  34.0 1.5 %collective-permute-start.15 = (bf16[2,6,32,128]{3,2,1,0:T(8,128)(2,1)S(1)}, bf16[2,6,32,128]{3,2,1,0:T(8,128)(2,1)S(1)}, u32[]{:S(2)}, u32[]{:S(2)}) collective-permute-start(bf16[2,6,32,128]{3,2,1,0:T(8,128)(2,1)S(1)} %collective-permute-done.12.refs_7_), channel_id=1, source_target_pairs={{0,1},{1,0},{2,3},{3,2},{4,5},{5,4},{6,7},{7,6},{8,9},{9,8},{10,11... | collective-permute-start | bytes 294920 | tf_op jit(solution)/shard_map/ppermute | solution.py:224
  34.4 1.3 %collective-permute-start.16 = (bf16[2,6,32,128]{3,2,1,0:T(8,128)(2,1)S(1)}, bf16[2,6,32,128]{3,2,1,0:T(8,128)(2,1)S(1)}, u32[]{:S(2)}, u32[]{:S(2)}) collective-permute-start(bf16[2,6,32,128]{3,2,1,0:T(8,128)(2,1)S(1)} %collective-permute-done.11.refs_8_), channel_id=1, source_target_pairs={{0,1},{1,0},{2,3},{3,2},{4,5},{5,4},{6,7},{7,6},{8,9},{9,8},{10,11... | collective-permute-start | bytes 294920 | tf_op jit(solution)/shard_map/ppermute | solution.py:224
  34.5 1.4 %collective-permute-start.17 = (bf16[2,6,32,128]{3,2,1,0:T(8,128)(2,1)S(1)}, bf16[2,6,32,128]{3,2,1,0:T(8,128)(2,1)S(1)}, u32[]{:S(2)}, u32[]{:S(2)}) collective-permute-start(bf16[2,6,32,128]{3,2,1,0:T(8,128)(2,1)S(1)} %collective-permute-done.10.refs_9_), channel_id=1, source_target_pairs={{0,1},{1,0},{2,3},{3,2},{4,5},{5,4},{6,7},{7,6},{8,9},{9,8},{10,11... | collective-permute-start | bytes 294920 | tf_op jit(solution)/shard_map/ppermute | solution.py:224

commit v4 on v3

--- a/solution.py
+++ b/solution.py
@@ -17,6 +17,10 @@
 def position():
     me = lax.axis_index("aux")
     return me // 2, lax.bitwise_and(me, 1)
+
+
+def begin_kernel(_, out_ref):
+    out_ref[...] = jnp.zeros_like(out_ref)
 
 
 def factor_kernel(metric_ref, _, factor_ref):
@@ -233,15 +237,15 @@
     def shape(*dims):
         return jax.ShapeDtypeStruct(dims, raw.dtype)
 
-    factor = pl.pallas_call(
-        factor_kernel,
-        out_shape=shape(devices * GROUP, devices * GROUP),
-        in_specs=[VMEM, HBM],
+    began = pl.pallas_call(
+        begin_kernel,
+        out_shape=jax.ShapeDtypeStruct((lines,), jnp.int32),
+        in_specs=[HBM],
         out_specs=VMEM,
         compiler_params=pltpu.CompilerParams(vmem_limit_bytes=61 * 1024 * 1024),
-        name="factor",
-    )(metric, raw)
-    other, factor = tie((swap(counts), factor))
+        name="begin",
+    )(raw)
+    other, began = tie((swap(counts), began))
     small = jnp.concatenate([owner_map, counts, other, jnp.zeros((lines - blocks - 4,), jnp.int32)])
     raw_there, small = tie((raw, small))
     peer_raw = swap(raw_there)
@@ -266,8 +270,7 @@
         return [hop(x, k) for k, x in zip(ks, xs)]
 
     first = hops(far + near, early(far + near, raw, 1))
-    *second, second_near = early(far + near[:1], peer_raw, 0)
-    second = hops(far, second)
+    second = hops(far + near[:1], early(far + near[:1], peer_raw, 0))
     first = tie(first)[::-1]
     brought = pl.pallas_call(
         counts_kernel,
@@ -299,10 +302,21 @@
     *third, own, info = late(
         far + near, small, [shape(2 * slots, orbitals, width), jax.ShapeDtypeStruct((8, 128), jnp.int32)]
     )
-    third, second, second_near = tie((third, second, second_near))
-    second_near, *third = tie(hops(near[:1] + far + near, [second_near, *third]))
+    pairs = [tie((x, y)) for x, y in zip(third[: len(far)], second)]
+    third = [x for x, _ in pairs] + third[len(pairs) :]
+    second = [y for _, y in pairs] + second[len(pairs) :]
+    metric, own_tiles = tie((metric, own))
+    factor = pl.pallas_call(
+        factor_kernel,
+        out_shape=shape(devices * GROUP, devices * GROUP),
+        in_specs=[VMEM, HBM],
+        out_specs=VMEM,
+        compiler_params=LIMIT,
+        name="factor",
+    )(metric, began)
+    *third, factor = tie(hops(far + near, third) + [factor])
     third = third[::-1]
-    second = [second_near, *second[::-1]]
+    second = second[::-1]
     forwarded = pl.pallas_call(
         forward_kernel,
         out_shape=shape((2 * half - 2) * 2 * EARLY, orbitals, width),
@@ -326,7 +340,7 @@
         ],
         compiler_params=pltpu.CompilerParams(vmem_limit_bytes=32 * 1024 * 1024),
         name="exchange",
-    )(info, factor, own, third[0], *first[1:], *second, forwarded, *third[1:], *crossed)
+    )(info, factor, own_tiles, third[0], *first[1:], *second, forwarded, *third[1:], *crossed)
 
 
 def solution(mesh):

time: 39 us -> 36.2 us (0.928)
  waiting for transfers between devices: 13.2 us -> 8.83 us
  starting transfers between devices: 18.6 us -> 20.9 us
  Pallas kernels: 6.77 us -> 5.93 us
    ppermute x11, waiting for transfers between devices: 11.2 us -> 6.27 us  [hop(): return lax.ppermute(x, 'aux', [(i, target(i)) for i in range(devices)])]
    ppermute x11, starting transfers between devices: 16.7 us -> 18.1 us  [hop(): return lax.ppermute(x, 'aux', [(i, target(i)) for i in range(devices)])]
    pallas_call x1, Pallas kernels: 1.64 us -> 0.29 us  [shards(): pl.pallas_call(factor_kernel, out_shape=shape(devices * GROUP, devices *...]
    ppermute x7, starting transfers between devices: 1.94 us -> 2.73 us  [swap(): return lax.ppermute(x, 'aux', [(i, i ^ 1) for i in range(devices)])]
    ppermute x7, waiting for transfers between devices: 1.97 us -> 2.56 us  [swap(): return lax.ppermute(x, 'aux', [(i, i ^ 1) for i in range(devices)])]
    pallas_call x0 -> x1, Pallas kernels: none -> 0.51 us  [shards(): pl.pallas_call(begin_kernel, out_shape=jax.ShapeDtypeStruct((lines,), jnp...]
  transfers between devices with their start and end apart: 18 -> 18, of which waited for: 8 -> 8; matrix products, arithmetic and copies ran while one was open for 0% -> 0% of each run, Pallas kernels for 10% -> 8%
where the time goes in v4:
time: 36.2 us; the launch traced here: 35.8 us
  starting transfers between devices  20.9 us (58%)
  waiting for transfers between devices  8.83 us (24%)
  Pallas kernels  5.93 us (16%)
    ppermute x11, starting transfers between devices, hop(): return lax.ppermute(x, 'aux', [(i, target(i)) for i in range(devices)])  18.1 us
    ppermute x11, waiting for transfers between devices, hop(): return lax.ppermute(x, 'aux', [(i, target(i)) for i in range(devices)])  6.27 us
    pallas_call x1, Pallas kernels, shards(): pl.pallas_call(functools.partial(exchange_kernel, chips), out_shape=jax.S...  2.93 us
    ppermute x7, starting transfers between devices, swap(): return lax.ppermute(x, 'aux', [(i, i ^ 1) for i in range(devices)])  2.73 us
    ppermute x7, waiting for transfers between devices, swap(): return lax.ppermute(x, 'aux', [(i, i ^ 1) for i in range(devices)])  2.56 us
    pallas_call x2, Pallas kernels, early(): pl.pallas_call(functools.partial(early_kernel, hops), out_shape=[shape((4...  1.23 us
    pallas_call x1, Pallas kernels, late(): pl.pallas_call(functools.partial(late_kernel, ks), out_shape=out_shape, i...  0.95 us
  transfers between devices with their start and end apart: 18, of which 8 were waited for; matrix products, arithmetic and copies ran while one was open for 0% of the time, Pallas kernels for 8%

profile of v4, /device:TPU:0, one launch (start us, length us, event | category | flops | bytes accessed | tf_op | source)
XLA Modules:
  0.0 35.8 jit_solution(14547134575955063985)
XLA Ops:
  0.0 0.5 %collective-permute-start = (s32[2]{0:T(128)}, s32[2]{0:T(128)S(1)}, u32[]{:S(2)}, u32[]{:S(2)}) collective-permute-start(s32[2]{0:T(128)} %param.7), channel_id=1, source_target_pairs={{0,1},{1,0},{2,3},{3,2},{4,5},{5,4},{6,7},{7,6},{8,9},{9,8},{10,11... | collective-permute-start | bytes 32 | tf_op jit(solution)/shard_map/ppermute | solution.py:228
  0.5 0.5 %begin.1._ = s32[128]{0:T(128)} custom-call(bf16[32,6,32,128]{3,2,1,0:T(8,128)(2,1)} %bitcast.3), custom_call_target="tpu_custom_call" | custom-call | tf_op jit(solution)/shard_map/begin/pallas_call | solution.py:240
  1.0 0.4 %collective-permute-done = s32[2]{0:T(128)S(1)} collective-permute-done((s32[2]{0:T(128)}, s32[2]{0:T(128)S(1)}, u32[]{:S(2)}, u32[]{:S(2)}) %collective-permute-start) | collective-permute-done | bytes 40 | tf_op jit(solution)/shard_map/ppermute | solution.py:228
  1.5 0.1 pad_add_fusion.small_ref
  1.6 0.3 collective-permute-start.6
  1.9 0.6 %early.2 = (bf16[9,32,128]{2,1,0:T(8,128)(2,1)S(1)}, bf16[9,32,128]{2,1,0:T(8,128)(2,1)S(1)}, bf16[9,32,128]{2,1,0:T(8,128)(2,1)S(1)}, bf16[1,32,128]{2,1,0:T(8,128)(2,1)S(1)}) custom-call(s32[128]{0:T(128)S(1)} %pad_add_fusion.small_ref, bf16[32,6,32,128]{3,2,1,0:T(8,128)(2,1)S(1)} %bitcast.5), custom_call_target="tpu_custom_call" | custom-call | tf_op jit(solution)/shard_map/early/pallas_call | solution.py:259
  2.5 4.9 %collective-permute-start.1 = (bf16[9,32,128]{2,1,0:T(8,128)(2,1)S(1)}, bf16[9,32,128]{2,1,0:T(8,128)(2,1)S(1)}, u32[]{:S(2)}, u32[]{:S(2)}) collective-permute-start(bf16[9,32,128]{2,1,0:T(8,128)(2,1)S(1)} %get-tuple-element.39), channel_id=1, source_target_pairs={{0,12},{1,15},{2,14},{3,13},{4,8},{5,11},{6,10},{7,9},{8,4},{9,7},... | collective-permute-start | bytes 221192 | tf_op jit(solution)/shard_map/ppermute | solution.py:235
  7.4 0.6 %collective-permute-start.3 = (bf16[9,32,128]{2,1,0:T(8,128)(2,1)S(1)}, bf16[9,32,128]{2,1,0:T(8,128)(2,1)S(1)}, u32[]{:S(2)}, u32[]{:S(2)}) collective-permute-start(bf16[9,32,128]{2,1,0:T(8,128)(2,1)S(1)} %get-tuple-element.41), channel_id=1, source_target_pairs={{0,4},{1,7},{2,6},{3,5},{4,0},{5,3},{6,2},{7,1},{8,12},{9,15},{10,... | collective-permute-start | bytes 221192 | tf_op jit(solution)/shard_map/ppermute | solution.py:235
  8.0 1.7 %collective-permute-start.4 = (bf16[1,32,128]{2,1,0:T(8,128)(2,1)S(1)}, bf16[1,32,128]{2,1,0:T(8,128)(2,1)S(1)}, u32[]{:S(2)}, u32[]{:S(2)}) collective-permute-start(bf16[1,32,128]{2,1,0:T(8,128)(2,1)S(1)} %get-tuple-element.42), channel_id=1, source_target_pairs={{0,2},{1,3},{2,0},{3,1},{4,6},{5,7},{6,4},{7,5},{8,10},{9,11},{10,... | collective-permute-start | bytes 24584 | tf_op jit(solution)/shard_map/ppermute | solution.py:235
  9.7 0.6 %early.3 = (bf16[8,32,128]{2,1,0:T(8,128)(2,1)S(1)}, bf16[8,32,128]{2,1,0:T(8,128)(2,1)S(1)}, bf16[8,32,128]{2,1,0:T(8,128)(2,1)S(1)}) custom-call(s32[128]{0:T(128)S(1)} %pad_add_fusion.small_ref, bf16[32,6,32,128]{3,2,1,0:T(8,128)(2,1)S(1)} %collective-permute-done.6.peer_raw.raw_ref), custom_call_target="tpu_custom_call" | custom-call | tf_op jit(solution)/shard_map/early/pallas_call | solution.py:259
  10.3 3.7 %collective-permute-start.7 = (bf16[8,32,128]{2,1,0:T(8,128)(2,1)S(1)}, bf16[8,32,128]{2,1,0:T(8,128)(2,1)S(1)}, u32[]{:S(2)}, u32[]{:S(2)}) collective-permute-start(bf16[8,32,128]{2,1,0:T(8,128)(2,1)S(1)} %get-tuple-element.50), channel_id=1, source_target_pairs={{0,12},{1,15},{2,14},{3,13},{4,8},{5,11},{6,10},{7,9},{8,4},{9,7},... | collective-permute-start | bytes 196616 | tf_op jit(solution)/shard_map/ppermute | solution.py:235
  14.0 0.1 collective-permute-start.9
  14.1 1.9 %collective-permute-start.13 = (bf16[8,32,128]{2,1,0:T(8,128)(2,1)S(1)}, bf16[8,32,128]{2,1,0:T(8,128)(2,1)S(1)}, u32[]{:S(2)}, u32[]{:S(2)}) collective-permute-start(bf16[8,32,128]{2,1,0:T(8,128)(2,1)S(1)} %get-tuple-element.63), channel_id=1, source_target_pairs={{0,4},{1,7},{2,6},{3,5},{4,0},{5,3},{6,2},{7,1},{8,12},{9,15},{10,... | collective-permute-start | bytes 196616 | tf_op jit(solution)/shard_map/ppermute | solution.py:235
  16.1 0.0 copy-start.1
  16.1 0.0 copy-start.2
  16.1 0.8 %collective-permute-start.5 = (s32[4,128]{1,0:T(4,128)S(1)}, s32[4,128]{1,0:T(4,128)S(1)}, u32[]{:S(2)}, u32[]{:S(2)}) collective-permute-start(s32[4,128]{1,0:T(4,128)S(1)} %counts.1.counts_ref), channel_id=1, source_target_pairs={{0,1},{1,0},{2,3},{3,2},{4,5},{5,4},{6,7},{7,6},{8,9},{9,8},{10,11... | collective-permute-start | bytes 6152 | tf_op jit(solution)/shard_map/ppermute | solution.py:228
  16.9 0.8 %collective-permute-done.5.crossed_ref = s32[4,128]{1,0:T(4,128)S(1)} collective-permute-done((s32[4,128]{1,0:T(4,128)S(1)}, s32[4,128]{1,0:T(4,128)S(1)}, u32[]{:S(2)}, u32[]{:S(2)}) %collective-permute-start.5) | collective-permute-done | bytes 2080 | tf_op jit(solution)/shard_map/ppermute | solution.py:228
  17.7 0.9 %late.1 = (bf16[2,6,32,128]{3,2,1,0:T(8,128)(2,1)S(1)}, bf16[2,6,32,128]{3,2,1,0:T(8,128)(2,1)S(1)}, bf16[2,6,32,128]{3,2,1,0:T(8,128)(2,1)S(1)}, bf16[12,32,128...) custom-call(s32[128]{0:T(128)S(1)} %pad_add_fusion.small_ref, ...), custom_call_target="tpu_custom_call" | custom-call | bytes 1024 | tf_op jit(solution)/shard_map/late/pallas_call | solution.py:289
  18.7 0.1 collective-permute-start.11
  18.8 1.2 %collective-permute-start.12 = (bf16[12,32,128]{2,1,0:T(8,128)(2,1)S(1)}, bf16[12,32,128]{2,1,0:T(8,128)(2,1)S(1)}, u32[]{:S(2)}, u32[]{:S(2)}) collective-permute-start(bf16[12,32,128]{2,1,0:T(8,128)(2,1)S(1)} %get-tuple-element.56), channel_id=1, source_target_pairs={{0,2},{1,3},{2,0},{3,1},{4,6},{5,7},{6,4},{7,5},{8,10},{9,11},{10,... | collective-permute-start | bytes 294920 | tf_op jit(solution)/shard_map/ppermute | solution.py:235
  19.9 0.3 collective-permute-done.9.refs_4_
  20.3 2.2 %collective-permute-start.10 = (bf16[2,6,32,128]{3,2,1,0:T(8,128)(2,1)S(1)}, bf16[2,6,32,128]{3,2,1,0:T(8,128)(2,1)S(1)}, u32[]{:S(2)}, u32[]{:S(2)}) collective-permute-start(bf16[2,6,32,128]{3,2,1,0:T(8,128)(2,1)S(1)} %get-tuple-element.54), channel_id=1, source_target_pairs={{0,8},{1,11},{2,10},{3,9},{4,12},{5,15},{6,14},{7,13},{8,0},{9,3},... | collective-permute-start | bytes 294920 | tf_op jit(solution)/shard_map/ppermute | solution.py:235
  22.4 1.8 %collective-permute-start.8 = (bf16[2,6,32,128]{3,2,1,0:T(8,128)(2,1)S(1)}, bf16[2,6,32,128]{3,2,1,0:T(8,128)(2,1)S(1)}, u32[]{:S(2)}, u32[]{:S(2)}) collective-permute-start(bf16[2,6,32,128]{3,2,1,0:T(8,128)(2,1)S(1)} %get-tuple-element.51), channel_id=1, source_target_pairs={{0,12},{1,15},{2,14},{3,13},{4,8},{5,11},{6,10},{7,9},{8,4},{9,7},... | collective-permute-start | bytes 294920 | tf_op jit(solution)/shard_map/ppermute | solution.py:235
  24.3 0.6 %collective-permute-start.14 = (bf16[24,32,128]{2,1,0:T(8,128)(2,1)S(1)}, bf16[24,32,128]{2,1,0:T(8,128)(2,1)S(1)}, u32[]{:S(2)}, u32[]{:S(2)}) collective-permute-start(bf16[24,32,128]{2,1,0:T(8,128)(2,1)S(1)} %forward.1), channel_id=1, source_target_pairs={{0,1},{1,0},{2,3},{3,2},{4,5},{5,4},{6,7},{7,6},{8,9},{9,8},{10,11... | collective-permute-start | bytes 589832 | tf_op jit(solution)/shard_map/ppermute | solution.py:228
  24.8 0.3 factor.1.factor_ref
  25.2 0.5 %collective-permute-done.12.side_ref = bf16[12,32,128]{2,1,0:T(8,128)(2,1)S(1)} collective-permute-done((bf16[12,32,128]{2,1,0:T(8,128)(2,1)S(1)}, bf16[12,32,128]{2,1,0:T(8,128)(2,1)S(1)}, u32[]{:S(2)}, u32[]{:S(2)}) %collective-permute-start.12) | collective-permute-done | bytes 98336 | tf_op jit(solution)/shard_map/ppermute | solution.py:235
  25.7 5.4 %collective-permute-done.10.refs_8_ = bf16[2,6,32,128]{3,2,1,0:T(8,128)(2,1)S(1)} collective-permute-done((bf16[2,6,32,128]{3,2,1,0:T(8,128)(2,1)S(1)}, bf16[2,6,32,128]{3,2,1,0:T(8,128)(2,1)S(1)}, u32[]{:S(2)}, u32[]{:S(2)}) %collective-permute-start.10) | collective-permute-done | bytes 98336 | tf_op jit(solution)/shard_map/ppermute | solution.py:235
  31.1 0.5 %collective-permute-start.16 = (bf16[2,6,32,128]{3,2,1,0:T(8,128)(2,1)S(1)}, bf16[2,6,32,128]{3,2,1,0:T(8,128)(2,1)S(1)}, u32[]{:S(2)}, u32[]{:S(2)}) collective-permute-start(bf16[2,6,32,128]{3,2,1,0:T(8,128)(2,1)S(1)} %collective-permute-done.10.refs_8_), channel_id=1, source_target_pairs={{0,1},{1,0},{2,3},{3,2},{4,5},{5,4},{6,7},{7,6},{8,9},{9,8},{10,11... | collective-permute-start | bytes 294920 | tf_op jit(solution)/shard_map/ppermute | solution.py:228
  31.6 0.8 %collective-permute-done.15.refs_10_ = bf16[2,6,32,128]{3,2,1,0:T(8,128)(2,1)S(1)} collective-permute-done((bf16[2,6,32,128]{3,2,1,0:T(8,128)(2,1)S(1)}, bf16[2,6,32,128]{3,2,1,0:T(8,128)(2,1)S(1)}, u32[]{:S(2)}, u32[]{:S(2)}) %collective-permute-start.15) | collective-permute-done | bytes 98336 | tf_op jit(solution)/shard_map/ppermute | solution.py:228
  32.4 0.2 collective-permute-done.16.refs_11_
  32.5 0.4 collective-permute-done.17.refs_12_
  32.9 2.9 %exchange.1 = f32[2,768,768]{2,1,0:T(8,128)} custom-call(s32[8,128]{1,0:T(8,128)S(1)} %get-tuple-element.48.info_ref, bf16[256,256]{1,0:T(8,128)(2,1)S(1)} %factor.1.factor_ref, bf16[12,32,128]{2,1,0:T(8,128)(2,1)S(1)} %get-tuple-element.61.self_ref, bf16[12,32,128]{2,1,0:T(8,128)(2,1)S(1)} %collective-permute-done.12.side_ref, ...), custom_call_target="tpu_custom_call" | custom-call | tf_op jit(solution)/shard_map/exchange/pallas_call | solution.py:331
  (24 shorter events, 0.1 us)
Async XLA Ops:
  0.0 1.5 %copy-start.3 = (s32[2]{0:T(128)S(1)}, s32[2]{0:T(128)}, u32[]{:S(2)}) copy-start(s32[2]{0:T(128)} %param.7) | copy-start | bytes 28
  0.0 1.6 %copy-start = (bf16[1,32,32,6,128]{4,2,3,1,0:T(8,128)(2,1)S(1)}, bf16[1,32,32,6,128]{4,2,3,1,0:T(8,128)(2,1)}, u32[]{:S(2)}) copy-start(bf16[1,32,32,6,128]{4,2,3,1,0:T(8,128)(2,1)} %param.4) | copy-start | bytes 4718596
  0.0 1.5 %copy-start.4 = (s32[32]{0:T(128)S(1)}, s32[32]{0:T(128)}, u32[]{:S(2)}) copy-start(s32[32]{0:T(128)} %param.6) | copy-start | bytes 388
  0.0 1.5 %collective-permute-start = (s32[2]{0:T(128)}, s32[2]{0:T(128)S(1)}, u32[]{:S(2)}, u32[]{:S(2)}) collective-permute-start(s32[2]{0:T(128)} %param.7), channel_id=1, source_target_pairs={{0,1},{1,0},{2,3},{3,2},{4,5},{5,4},{6,7},{7,6},{8,9},{9,8},{10,11... | collective-permute-start | bytes 32 | tf_op jit(solution)/shard_map/ppermute | solution.py:228
  1.6 8.1 %collective-permute-start.6 = (bf16[32,6,32,128]{3,2,1,0:T(8,128)(2,1)S(1)}, bf16[32,6,32,128]{3,2,1,0:T(8,128)(2,1)S(1)}, u32[]{:S(2)}, u32[]{:S(2)}) collective-permute-start(bf16[32,6,32,128]{3,2,1,0:T(8,128)(2,1)S(1)} %bitcast.4), channel_id=1, source_target_pairs={{0,1},{1,0},{2,3},{3,2},{4,5},{5,4},{6,7},{7,6},{8,9},{9,8},{10,11... | collective-permute-start | bytes 4718600 | tf_op jit(solution)/shard_map/ppermute | solution.py:228
  2.5 11.6 %collective-permute-start.1 = (bf16[9,32,128]{2,1,0:T(8,128)(2,1)S(1)}, bf16[9,32,128]{2,1,0:T(8,128)(2,1)S(1)}, u32[]{:S(2)}, u32[]{:S(2)}) collective-permute-start(bf16[9,32,128]{2,1,0:T(8,128)(2,1)S(1)} %get-tuple-element.39), channel_id=1, source_target_pairs={{0,12},{1,15},{2,14},{3,13},{4,8},{5,11},{6,10},{7,9},{8,4},{9,7},... | collective-permute-start | bytes 221192 | tf_op jit(solution)/shard_map/ppermute | solution.py:235
  7.4 8.7 %collective-permute-start.2 = (bf16[9,32,128]{2,1,0:T(8,128)(2,1)S(1)}, bf16[9,32,128]{2,1,0:T(8,128)(2,1)S(1)}, u32[]{:S(2)}, u32[]{:S(2)}) collective-permute-start(bf16[9,32,128]{2,1,0:T(8,128)(2,1)S(1)} %get-tuple-element.40), channel_id=1, source_target_pairs={{0,8},{1,11},{2,10},{3,9},{4,12},{5,15},{6,14},{7,13},{8,0},{9,3},... | collective-permute-start | bytes 221192 | tf_op jit(solution)/shard_map/ppermute | solution.py:235
  7.4 8.7 %collective-permute-start.3 = (bf16[9,32,128]{2,1,0:T(8,128)(2,1)S(1)}, bf16[9,32,128]{2,1,0:T(8,128)(2,1)S(1)}, u32[]{:S(2)}, u32[]{:S(2)}) collective-permute-start(bf16[9,32,128]{2,1,0:T(8,128)(2,1)S(1)} %get-tuple-element.41), channel_id=1, source_target_pairs={{0,4},{1,7},{2,6},{3,5},{4,0},{5,3},{6,2},{7,1},{8,12},{9,15},{10,... | collective-permute-start | bytes 221192 | tf_op jit(solution)/shard_map/ppermute | solution.py:235
  8.0 6.0 %collective-permute-start.4 = (bf16[1,32,128]{2,1,0:T(8,128)(2,1)S(1)}, bf16[1,32,128]{2,1,0:T(8,128)(2,1)S(1)}, u32[]{:S(2)}, u32[]{:S(2)}) collective-permute-start(bf16[1,32,128]{2,1,0:T(8,128)(2,1)S(1)} %get-tuple-element.42), channel_id=1, source_target_pairs={{0,2},{1,3},{2,0},{3,1},{4,6},{5,7},{6,4},{7,5},{8,10},{9,11},{10,... | collective-permute-start | bytes 24584 | tf_op jit(solution)/shard_map/ppermute | solution.py:235
  10.3 9.6 %collective-permute-start.7 = (bf16[8,32,128]{2,1,0:T(8,128)(2,1)S(1)}, bf16[8,32,128]{2,1,0:T(8,128)(2,1)S(1)}, u32[]{:S(2)}, u32[]{:S(2)}) collective-permute-start(bf16[8,32,128]{2,1,0:T(8,128)(2,1)S(1)} %get-tuple-element.50), channel_id=1, source_target_pairs={{0,12},{1,15},{2,14},{3,13},{4,8},{5,11},{6,10},{7,9},{8,4},{9,7},... | collective-permute-start | bytes 196616 | tf_op jit(solution)/shard_map/ppermute | solution.py:235
  14.0 6.3 %collective-permute-start.9 = (bf16[8,32,128]{2,1,0:T(8,128)(2,1)S(1)}, bf16[8,32,128]{2,1,0:T(8,128)(2,1)S(1)}, u32[]{:S(2)}, u32[]{:S(2)}) collective-permute-start(bf16[8,32,128]{2,1,0:T(8,128)(2,1)S(1)} %get-tuple-element.53), channel_id=1, source_target_pairs={{0,8},{1,11},{2,10},{3,9},{4,12},{5,15},{6,14},{7,13},{8,0},{9,3},... | collective-permute-start | bytes 196616 | tf_op jit(solution)/shard_map/ppermute | solution.py:235
  14.1 10.1 %collective-permute-start.13 = (bf16[8,32,128]{2,1,0:T(8,128)(2,1)S(1)}, bf16[8,32,128]{2,1,0:T(8,128)(2,1)S(1)}, u32[]{:S(2)}, u32[]{:S(2)}) collective-permute-start(bf16[8,32,128]{2,1,0:T(8,128)(2,1)S(1)} %get-tuple-element.63), channel_id=1, source_target_pairs={{0,4},{1,7},{2,6},{3,5},{4,0},{5,3},{6,2},{7,1},{8,12},{9,15},{10,... | collective-permute-start | bytes 196616 | tf_op jit(solution)/shard_map/ppermute | solution.py:235
  16.1 8.8 %copy-start.1 = (bf16[16,16]{1,0:T(8,128)(2,1)S(1)}, bf16[16,16]{1,0:T(8,128)(2,1)}, u32[]{:S(2)}) copy-start(bf16[16,16]{1,0:T(8,128)(2,1)} %metric_ref) | copy-start | bytes 1540
  16.1 8.8 %copy-start.2 = (s32[128]{0:T(128)S(1)}, s32[128]{0:T(128)}, u32[]{:S(2)}) copy-start(s32[128]{0:T(128)} %begin.1._) | copy-start | bytes 1540
  16.1 1.6 %collective-permute-start.5 = (s32[4,128]{1,0:T(4,128)S(1)}, s32[4,128]{1,0:T(4,128)S(1)}, u32[]{:S(2)}, u32[]{:S(2)}) collective-permute-start(s32[4,128]{1,0:T(4,128)S(1)} %counts.1.counts_ref), channel_id=1, source_target_pairs={{0,1},{1,0},{2,3},{3,2},{4,5},{5,4},{6,7},{7,6},{8,9},{9,8},{10,11... | collective-permute-start | bytes 6152 | tf_op jit(solution)/shard_map/ppermute | solution.py:228
  18.7 6.5 %collective-permute-start.11 = (bf16[2,6,32,128]{3,2,1,0:T(8,128)(2,1)S(1)}, bf16[2,6,32,128]{3,2,1,0:T(8,128)(2,1)S(1)}, u32[]{:S(2)}, u32[]{:S(2)}) collective-permute-start(bf16[2,6,32,128]{3,2,1,0:T(8,128)(2,1)S(1)} %get-tuple-element.55), channel_id=1, source_target_pairs={{0,4},{1,7},{2,6},{3,5},{4,0},{5,3},{6,2},{7,1},{8,12},{9,15},{10,... | collective-permute-start | bytes 294920 | tf_op jit(solution)/shard_map/ppermute | solution.py:235
  18.8 6.9 %collective-permute-start.12 = (bf16[12,32,128]{2,1,0:T(8,128)(2,1)S(1)}, bf16[12,32,128]{2,1,0:T(8,128)(2,1)S(1)}, u32[]{:S(2)}, u32[]{:S(2)}) collective-permute-start(bf16[12,32,128]{2,1,0:T(8,128)(2,1)S(1)} %get-tuple-element.56), channel_id=1, source_target_pairs={{0,2},{1,3},{2,0},{3,1},{4,6},{5,7},{6,4},{7,5},{8,10},{9,11},{10,... | collective-permute-start | bytes 294920 | tf_op jit(solution)/shard_map/ppermute | solution.py:235
  20.3 10.8 %collective-permute-start.10 = (bf16[2,6,32,128]{3,2,1,0:T(8,128)(2,1)S(1)}, bf16[2,6,32,128]{3,2,1,0:T(8,128)(2,1)S(1)}, u32[]{:S(2)}, u32[]{:S(2)}) collective-permute-start(bf16[2,6,32,128]{3,2,1,0:T(8,128)(2,1)S(1)} %get-tuple-element.54), channel_id=1, source_target_pairs={{0,8},{1,11},{2,10},{3,9},{4,12},{5,15},{6,14},{7,13},{8,0},{9,3},... | collective-permute-start | bytes 294920 | tf_op jit(solution)/shard_map/ppermute | solution.py:235
  22.4 8.6 %collective-permute-start.8 = (bf16[2,6,32,128]{3,2,1,0:T(8,128)(2,1)S(1)}, bf16[2,6,32,128]{3,2,1,0:T(8,128)(2,1)S(1)}, u32[]{:S(2)}, u32[]{:S(2)}) collective-permute-start(bf16[2,6,32,128]{3,2,1,0:T(8,128)(2,1)S(1)} %get-tuple-element.51), channel_id=1, source_target_pairs={{0,12},{1,15},{2,14},{3,13},{4,8},{5,11},{6,10},{7,9},{8,4},{9,7},... | collective-permute-start | bytes 294920 | tf_op jit(solution)/shard_map/ppermute | solution.py:235
  24.3 8.6 %collective-permute-start.14 = (bf16[24,32,128]{2,1,0:T(8,128)(2,1)S(1)}, bf16[24,32,128]{2,1,0:T(8,128)(2,1)S(1)}, u32[]{:S(2)}, u32[]{:S(2)}) collective-permute-start(bf16[24,32,128]{2,1,0:T(8,128)(2,1)S(1)} %forward.1), channel_id=1, source_target_pairs={{0,1},{1,0},{2,3},{3,2},{4,5},{5,4},{6,7},{7,6},{8,9},{9,8},{10,11... | collective-permute-start | bytes 589832 | tf_op jit(solution)/shard_map/ppermute | solution.py:228
  31.1 1.3 %collective-permute-start.15 = (bf16[2,6,32,128]{3,2,1,0:T(8,128)(2,1)S(1)}, bf16[2,6,32,128]{3,2,1,0:T(8,128)(2,1)S(1)}, u32[]{:S(2)}, u32[]{:S(2)}) collective-permute-start(bf16[2,6,32,128]{3,2,1,0:T(8,128)(2,1)S(1)} %collective-permute-done.11.refs_7_), channel_id=1, source_target_pairs={{0,1},{1,0},{2,3},{3,2},{4,5},{5,4},{6,7},{7,6},{8,9},{9,8},{10,11... | collective-permute-start | bytes 294920 | tf_op jit(solution)/shard_map/ppermute | solution.py:228
  31.1 1.5 %collective-permute-start.16 = (bf16[2,6,32,128]{3,2,1,0:T(8,128)(2,1)S(1)}, bf16[2,6,32,128]{3,2,1,0:T(8,128)(2,1)S(1)}, u32[]{:S(2)}, u32[]{:S(2)}) collective-permute-start(bf16[2,6,32,128]{3,2,1,0:T(8,128)(2,1)S(1)} %collective-permute-done.10.refs_8_), channel_id=1, source_target_pairs={{0,1},{1,0},{2,3},{3,2},{4,5},{5,4},{6,7},{7,6},{8,9},{9,8},{10,11... | collective-permute-start | bytes 294920 | tf_op jit(solution)/shard_map/ppermute | solution.py:228
  31.6 1.3 %collective-permute-start.17 = (bf16[2,6,32,128]{3,2,1,0:T(8,128)(2,1)S(1)}, bf16[2,6,32,128]{3,2,1,0:T(8,128)(2,1)S(1)}, u32[]{:S(2)}, u32[]{:S(2)}) collective-permute-start(bf16[2,6,32,128]{3,2,1,0:T(8,128)(2,1)S(1)} %collective-permute-done.8.refs_9_), channel_id=1, source_target_pairs={{0,1},{1,0},{2,3},{3,2},{4,5},{5,4},{6,7},{7,6},{8,9},{9,8},{10,11... | collective-permute-start | bytes 294920 | tf_op jit(solution)/shard_map/ppermute | solution.py:228

commit v5 on v4

--- a/solution.py
+++ b/solution.py
@@ -19,11 +19,7 @@
     return me // 2, lax.bitwise_and(me, 1)
 
 
-def begin_kernel(_, out_ref):
-    out_ref[...] = jnp.zeros_like(out_ref)
-
-
-def factor_kernel(metric_ref, _, factor_ref):
+def factor_kernel(metric_ref, factor_ref):
     wide, aux = factor_ref.shape[0], metric_ref.shape[0]
     chip, core = position()
     row = lax.broadcasted_iota(jnp.int32, (wide, aux), 0) // GROUP
@@ -89,7 +85,7 @@
 def late_kernel(hops, small_ref, counts_ref, crossed_ref, own_raw, peer_raw, *refs):
     outs = refs[: len(hops)]
     ids, held, direct, crossed, sem, sems = refs[-6:]
-    blocks, slots = own_raw.shape[0], own_raw.shape[1]
+    blocks, slots = own_raw.shape[0], own_raw.shape[1] + 1
     chip, core = position()
     copies = [
         pltpu.make_async_copy(counts_ref, direct, sems.at[0]),
@@ -141,13 +137,29 @@
         out[n * 2 * EARLY : (n + 1) * 2 * EARLY] = ref[2 * EARLY : 4 * EARLY]
 
 
-def exchange_kernel(chips, info_ref, factor_ref, self_ref, side_ref, *refs):
+def blank_kernel(out_ref, zeros, sem):
+    zeros[...] = jnp.zeros_like(zeros)
+    height = zeros.shape[0]
+    copies = [
+        pltpu.make_async_copy(zeros, out_ref.at[which, n * height : (n + 1) * height], sem.at[which, n])
+        for which in range(2)
+        for n in range(out_ref.shape[1] // height)
+    ]
+    for copy in copies:
+        copy.start()
+    for copy in copies:
+        copy.wait()
+
+
+def exchange_kernel(chips, blank_ref, info_ref, factor_ref, self_ref, side_ref, *refs):
     half = chips // 2
     first, refs = refs[: half - 1], refs[half - 1 :]
     second, refs = refs[: half - 1], refs[half - 1 :]
     forwarded, refs = refs[0], refs[1:]
     third, third_crossed, refs = refs[: half - 1], refs[half - 1 : 2 * half - 2], refs[2 * half - 2 :]
-    out_ref, rows, stage, sems = refs
+    out_ref, rows, stage, live, sem, sems = refs
+    copy = pltpu.make_async_copy(info_ref, live, sem)
+    copy.start()
     doubled, orbitals, width = self_ref.shape
     slots = doubled // 2
     wide = factor_ref.shape[0]
@@ -194,26 +206,34 @@
         fitted = jnp.dot(factor_ref[...], jnp.concatenate(columns, axis=1), preferred_element_type=jnp.float32)
         rows[part * wide : (part + 1) * wide, :] = fitted.astype(jnp.bfloat16)
 
-    live = [info_ref[0:1, :], info_ref[1:2, :]]
-    for s in range(slots):
-        product = lax.dot_general(
-            rows[:, span(s)], rows[...], (((0,), (0,)), ((), ())), preferred_element_type=jnp.float32
-        )
+    def tiles(s, act):
         for which in range(2):
             row = s if which == 0 else slots - 1 - s
             for t in range(slots):
                 column = t if which == 0 else slots - 1 - t
-                stage[which, span(row), span(column)] = jnp.where(
-                    live[which] > max(row, column), product[:, span(t)], 0.0
-                )
-            pltpu.make_async_copy(
-                stage.at[which, span(row)], out_ref.at[which, span(row)], sems.at[which, row]
-            ).start()
-    for which in range(2):
-        for row in range(slots):
-            pltpu.make_async_copy(
-                stage.at[which, span(row)], out_ref.at[which, span(row)], sems.at[which, row]
-            ).wait()
+                if max(row, column) < slots - 1:
+
+                    @pl.when(max(row, column) < live[which, 0])
+                    def _(which=which, row=row, column=column, t=t):
+                        act(
+                            pltpu.make_async_copy(
+                                stage.at[span(s), span(t)],
+                                out_ref.at[which, span(row), span(column)],
+                                sems.at[which, row],
+                            )
+                        )
+
+    for group in (range(slots - 2), range(slots - 2, slots)):
+        for s in group:
+            stage[span(s), :] = lax.dot_general(
+                rows[:, span(s)], rows[...], (((0,), (0,)), ((), ())), preferred_element_type=jnp.float32
+            )
+        if 0 in group:
+            copy.wait()
+        for s in group:
+            tiles(s, lambda copy: copy.start())
+    for s in range(slots):
+        tiles(s, lambda copy: copy.wait())
 
 
 def shards(devices, raw_tiles, metric, owner_map, counts):
@@ -237,15 +257,7 @@
     def shape(*dims):
         return jax.ShapeDtypeStruct(dims, raw.dtype)
 
-    began = pl.pallas_call(
-        begin_kernel,
-        out_shape=jax.ShapeDtypeStruct((lines,), jnp.int32),
-        in_specs=[HBM],
-        out_specs=VMEM,
-        compiler_params=pltpu.CompilerParams(vmem_limit_bytes=61 * 1024 * 1024),
-        name="begin",
-    )(raw)
-    other, began = tie((swap(counts), began))
+    other, raw = tie((swap(counts), raw[:, : slots - 1]))
     small = jnp.concatenate([owner_map, counts, other, jnp.zeros((lines - blocks - 4,), jnp.int32)])
     raw_there, small = tie((raw, small))
     peer_raw = swap(raw_there)
@@ -269,9 +281,12 @@
     def hops(ks, xs):
         return [hop(x, k) for k, x in zip(ks, xs)]
 
-    first = hops(far + near, early(far + near, raw, 1))
-    second = hops(far + near[:1], early(far + near[:1], peer_raw, 0))
-    first = tie(first)[::-1]
+    ways = far[::-1] + near
+    first = hops(ways, early(ways, raw, 1))
+    *second, beside = hops(ways[:-1], early(ways[:-1], peer_raw, 0))
+    second = [*second[::-1], beside]
+    *first, beside, side = tie(first)
+    first = [side, beside, *first]
     brought = pl.pallas_call(
         counts_kernel,
         out_shape=jax.ShapeDtypeStruct((half, 128), jnp.int32),
@@ -309,12 +324,21 @@
     factor = pl.pallas_call(
         factor_kernel,
         out_shape=shape(devices * GROUP, devices * GROUP),
-        in_specs=[VMEM, HBM],
+        in_specs=[VMEM],
         out_specs=VMEM,
         compiler_params=LIMIT,
         name="factor",
-    )(metric, began)
-    *third, factor = tie(hops(far + near, third) + [factor])
+    )(metric)
+    blank = pl.pallas_call(
+        lambda _, *refs: blank_kernel(*refs),
+        out_shape=jax.ShapeDtypeStruct((2, slots * width, slots * width), jnp.float32),
+        in_specs=[HBM],
+        out_specs=HBM,
+        scratch_shapes=[pltpu.VMEM((width, slots * width), jnp.float32), pltpu.SemaphoreType.DMA((2, slots))],
+        compiler_params=LIMIT,
+        name="blank",
+    )(factor)
+    *third, factor, blank = tie(hops(far + near, third) + [factor, blank])
     third = third[::-1]
     second = second[::-1]
     forwarded = pl.pallas_call(
@@ -331,16 +355,19 @@
     return pl.pallas_call(
         functools.partial(exchange_kernel, chips),
         out_shape=jax.ShapeDtypeStruct((2, slots * width, slots * width), jnp.float32),
-        in_specs=[VMEM] * (4 * half + 1),
-        out_specs=pl.BlockSpec(memory_space=pl.ANY),
+        in_specs=[HBM] + [VMEM] * (4 * half + 1),
+        out_specs=HBM,
         scratch_shapes=[
             pltpu.VMEM((devices * orbitals, slots * width), raw.dtype),
-            pltpu.VMEM((2, slots * width, slots * width), jnp.float32),
+            pltpu.VMEM((slots * width, slots * width), jnp.float32),
+            pltpu.SMEM((8, 128), jnp.int32),
+            one,
             pltpu.SemaphoreType.DMA((2, slots)),
         ],
+        input_output_aliases={0: 0},
         compiler_params=pltpu.CompilerParams(vmem_limit_bytes=32 * 1024 * 1024),
         name="exchange",
-    )(info, factor, own_tiles, third[0], *first[1:], *second, forwarded, *third[1:], *crossed)
+    )(blank, info, factor, own_tiles, third[0], *first[1:], *second, forwarded, *third[1:], *crossed)
 
 
 def solution(mesh):

time: 36.2 us -> 35.8 us (0.989)
  waiting for transfers between devices: 8.83 us -> 6.31 us
  local copies, waits for them, and re-layouts: 0.03 us -> 1.56 us
  Pallas kernels: 5.93 us -> 6.89 us
  starting transfers between devices: 20.9 us -> 20.5 us
    ppermute x11, waiting for transfers between devices: 6.27 us -> 4.19 us  [hop(): return lax.ppermute(x, 'aux', [(i, target(i)) for i in range(devices)])]
    pallas_call x1, Pallas kernels: 0.51 us -> 2.3 us  [shards(): pl.pallas_call(lambda _, *refs: blank_kernel(*refs), out_shape=jax.ShapeD...]
    slice x0 -> x1, local copies, waits for them, and re-layouts: none -> 1.55 us  [shards(): other, raw = tie((swap(counts), raw[:, :slots - 1]))]
    pallas_call x1, Pallas kernels: 2.93 us -> 2.1 us  [shards(): pl.pallas_call(functools.partial(exchange_kernel, chips), out_shape=jax.S...]
    ppermute x7, starting transfers between devices: 2.73 us -> 2.26 us  [swap(): return lax.ppermute(x, 'aux', [(i, i ^ 1) for i in range(devices)])]
    ppermute x7, waiting for transfers between devices: 2.56 us -> 2.12 us  [swap(): return lax.ppermute(x, 'aux', [(i, i ^ 1) for i in range(devices)])]
  transfers between devices with their start and end apart: 18 -> 18, of which waited for: 8 -> 5; matrix products, arithmetic and copies ran while one was open for 0% -> 4% of each run, Pallas kernels for 8% -> 13%
where the time goes in v5:
time: 35.8 us; the launch traced here: 35.5 us
  starting transfers between devices  20.5 us (57%)
  Pallas kernels  6.89 us (19%)
  waiting for transfers between devices  6.31 us (18%)
  local copies, waits for them, and re-layouts  1.56 us (4%)
    ppermute x11, starting transfers between devices, hop(): return lax.ppermute(x, 'aux', [(i, target(i)) for i in range(devices)])  18.3 us
    ppermute x11, waiting for transfers between devices, hop(): return lax.ppermute(x, 'aux', [(i, target(i)) for i in range(devices)])  4.19 us
    pallas_call x1, Pallas kernels, shards(): pl.pallas_call(lambda _, *refs: blank_kernel(*refs), out_shape=jax.ShapeD...  2.3 us
    ppermute x7, starting transfers between devices, swap(): return lax.ppermute(x, 'aux', [(i, i ^ 1) for i in range(devices)])  2.26 us
    ppermute x7, waiting for transfers between devices, swap(): return lax.ppermute(x, 'aux', [(i, i ^ 1) for i in range(devices)])  2.12 us
    pallas_call x1, Pallas kernels, shards(): pl.pallas_call(functools.partial(exchange_kernel, chips), out_shape=jax.S...  2.1 us
    slice x1, local copies, waits for them, and re-layouts, shards(): other, raw = tie((swap(counts), raw[:, :slots - 1]))  1.55 us
    pallas_call x2, Pallas kernels, early(): pl.pallas_call(functools.partial(early_kernel, hops), out_shape=[shape((4...  1.23 us
  transfers between devices with their start and end apart: 18, of which 5 were waited for; matrix products, arithmetic and copies ran while one was open for 4% of the time, Pallas kernels for 13%

profile of v5, /device:TPU:0, one launch (start us, length us, event | category | flops | bytes accessed | tf_op | source)
XLA Modules:
  0.0 35.5 jit_solution(10991741419653479867)
XLA Ops:
  0.0 0.5 %collective-permute-start = (s32[2]{0:T(128)}, s32[2]{0:T(128)S(1)}, u32[]{:S(2)}, u32[]{:S(2)}) collective-permute-start(s32[2]{0:T(128)} %param.7), channel_id=1, source_target_pairs={{0,1},{1,0},{2,3},{3,2},{4,5},{5,4},{6,7},{7,6},{8,9},{9,8},{10,11... | collective-permute-start | bytes 32 | tf_op jit(solution)/shard_map/ppermute | solution.py:248
  0.5 1.5 %slice.4.raw_ref.own_raw = bf16[32,5,32,128]{3,2,1,0:T(8,128)(2,1)S(1)} slice(bf16[32,6,32,128]{3,2,1,0:T(8,128)(2,1)} %bitcast.3), slice={[0:32], [0:5], [0:32], [0:128]} | slice | bytes 2621440 | tf_op jit(solution)/shard_map/slice | solution.py:260
  2.0 0.1 pad_add_fusion.small_ref
  2.1 0.1 collective-permute-start.6
  2.2 0.6 %early.2 = (bf16[9,32,128]{2,1,0:T(8,128)(2,1)S(1)}, bf16[9,32,128]{2,1,0:T(8,128)(2,1)S(1)}, bf16[9,32,128]{2,1,0:T(8,128)(2,1)S(1)}, bf16[1,32,128]{2,1,0:T(8,128)(2,1)S(1)}) custom-call(s32[128]{0:T(128)S(1)} %pad_add_fusion.small_ref, bf16[32,5,32,128]{3,2,1,0:T(8,128)(2,1)S(1)} %slice.4.raw_ref.own_raw), custom_call_target="tpu_custom_call" | custom-call | tf_op jit(solution)/shard_map/early/pallas_call | solution.py:271
  2.8 4.1 %collective-permute-start.1 = (bf16[9,32,128]{2,1,0:T(8,128)(2,1)S(1)}, bf16[9,32,128]{2,1,0:T(8,128)(2,1)S(1)}, u32[]{:S(2)}, u32[]{:S(2)}) collective-permute-start(bf16[9,32,128]{2,1,0:T(8,128)(2,1)S(1)} %get-tuple-element.41), channel_id=1, source_target_pairs={{0,8},{1,11},{2,10},{3,9},{4,12},{5,15},{6,14},{7,13},{8,0},{9,3},... | collective-permute-start | bytes 221192 | tf_op jit(solution)/shard_map/ppermute | solution.py:255
  6.9 1.3 %collective-permute-start.2 = (bf16[9,32,128]{2,1,0:T(8,128)(2,1)S(1)}, bf16[9,32,128]{2,1,0:T(8,128)(2,1)S(1)}, u32[]{:S(2)}, u32[]{:S(2)}) collective-permute-start(bf16[9,32,128]{2,1,0:T(8,128)(2,1)S(1)} %get-tuple-element.42), channel_id=1, source_target_pairs={{0,12},{1,15},{2,14},{3,13},{4,8},{5,11},{6,10},{7,9},{8,4},{9,7},... | collective-permute-start | bytes 221192 | tf_op jit(solution)/shard_map/ppermute | solution.py:255
  8.3 0.2 collective-permute-start.3
  8.5 1.5 %collective-permute-start.4 = (bf16[1,32,128]{2,1,0:T(8,128)(2,1)S(1)}, bf16[1,32,128]{2,1,0:T(8,128)(2,1)S(1)}, u32[]{:S(2)}, u32[]{:S(2)}) collective-permute-start(bf16[1,32,128]{2,1,0:T(8,128)(2,1)S(1)} %get-tuple-element.44), channel_id=1, source_target_pairs={{0,2},{1,3},{2,0},{3,1},{4,6},{5,7},{6,4},{7,5},{8,10},{9,11},{10,... | collective-permute-start | bytes 24584 | tf_op jit(solution)/shard_map/ppermute | solution.py:255
  10.0 0.6 %early.3 = (bf16[8,32,128]{2,1,0:T(8,128)(2,1)S(1)}, bf16[8,32,128]{2,1,0:T(8,128)(2,1)S(1)}, bf16[8,32,128]{2,1,0:T(8,128)(2,1)S(1)}) custom-call(s32[128]{0:T(128)S(1)} %pad_add_fusion.small_ref, bf16[32,5,32,128]{3,2,1,0:T(8,128)(2,1)S(1)} %collective-permute-done.6.peer_raw.raw_ref), custom_call_target="tpu_custom_call" | custom-call | tf_op jit(solution)/shard_map/early/pallas_call | solution.py:271
  10.7 3.0 %collective-permute-start.7 = (bf16[8,32,128]{2,1,0:T(8,128)(2,1)S(1)}, bf16[8,32,128]{2,1,0:T(8,128)(2,1)S(1)}, u32[]{:S(2)}, u32[]{:S(2)}) collective-permute-start(bf16[8,32,128]{2,1,0:T(8,128)(2,1)S(1)} %get-tuple-element.51), channel_id=1, source_target_pairs={{0,12},{1,15},{2,14},{3,13},{4,8},{5,11},{6,10},{7,9},{8,4},{9,7},... | collective-permute-start | bytes 196616 | tf_op jit(solution)/shard_map/ppermute | solution.py:255
  13.6 1.5 %collective-permute-start.9 = (bf16[8,32,128]{2,1,0:T(8,128)(2,1)S(1)}, bf16[8,32,128]{2,1,0:T(8,128)(2,1)S(1)}, u32[]{:S(2)}, u32[]{:S(2)}) collective-permute-start(bf16[8,32,128]{2,1,0:T(8,128)(2,1)S(1)} %get-tuple-element.54), channel_id=1, source_target_pairs={{0,8},{1,11},{2,10},{3,9},{4,12},{5,15},{6,14},{7,13},{8,0},{9,3},... | collective-permute-start | bytes 196616 | tf_op jit(solution)/shard_map/ppermute | solution.py:255
  15.1 0.6 %collective-permute-start.13 = (bf16[8,32,128]{2,1,0:T(8,128)(2,1)S(1)}, bf16[8,32,128]{2,1,0:T(8,128)(2,1)S(1)}, u32[]{:S(2)}, u32[]{:S(2)}) collective-permute-start(bf16[8,32,128]{2,1,0:T(8,128)(2,1)S(1)} %get-tuple-element.65), channel_id=1, source_target_pairs={{0,4},{1,7},{2,6},{3,5},{4,0},{5,3},{6,2},{7,1},{8,12},{9,15},{10,... | collective-permute-start | bytes 196616 | tf_op jit(solution)/shard_map/ppermute | solution.py:255
  15.7 0.0 copy-start
  15.8 0.7 %collective-permute-start.5 = (s32[4,128]{1,0:T(4,128)S(1)}, s32[4,128]{1,0:T(4,128)S(1)}, u32[]{:S(2)}, u32[]{:S(2)}) collective-permute-start(s32[4,128]{1,0:T(4,128)S(1)} %counts.1.counts_ref), channel_id=1, source_target_pairs={{0,1},{1,0},{2,3},{3,2},{4,5},{5,4},{6,7},{7,6},{8,9},{9,8},{10,11... | collective-permute-start | bytes 6152 | tf_op jit(solution)/shard_map/ppermute | solution.py:248
  16.5 0.8 %collective-permute-done.5.crossed_ref = s32[4,128]{1,0:T(4,128)S(1)} collective-permute-done((s32[4,128]{1,0:T(4,128)S(1)}, s32[4,128]{1,0:T(4,128)S(1)}, u32[]{:S(2)}, u32[]{:S(2)}) %collective-permute-start.5) | collective-permute-done | bytes 2080 | tf_op jit(solution)/shard_map/ppermute | solution.py:248
  17.3 0.9 %late.1 = (bf16[2,6,32,128]{3,2,1,0:T(8,128)(2,1)S(1)}, bf16[2,6,32,128]{3,2,1,0:T(8,128)(2,1)S(1)}, bf16[2,6,32,128]{3,2,1,0:T(8,128)(2,1)S(1)}, bf16[12,32,128...) custom-call(s32[128]{0:T(128)S(1)} %pad_add_fusion.small_ref, ...), custom_call_target="tpu_custom_call" | custom-call | bytes 1024 | tf_op jit(solution)/shard_map/late/pallas_call | solution.py:304
  18.2 1.4 %collective-permute-start.11 = (bf16[2,6,32,128]{3,2,1,0:T(8,128)(2,1)S(1)}, bf16[2,6,32,128]{3,2,1,0:T(8,128)(2,1)S(1)}, u32[]{:S(2)}, u32[]{:S(2)}) collective-permute-start(bf16[2,6,32,128]{3,2,1,0:T(8,128)(2,1)S(1)} %get-tuple-element.56), channel_id=1, source_target_pairs={{0,4},{1,7},{2,6},{3,5},{4,0},{5,3},{6,2},{7,1},{8,12},{9,15},{10,... | collective-permute-start | bytes 294920 | tf_op jit(solution)/shard_map/ppermute | solution.py:255
  19.6 1.2 %collective-permute-start.12 = (bf16[12,32,128]{2,1,0:T(8,128)(2,1)S(1)}, bf16[12,32,128]{2,1,0:T(8,128)(2,1)S(1)}, u32[]{:S(2)}, u32[]{:S(2)}) collective-permute-start(bf16[12,32,128]{2,1,0:T(8,128)(2,1)S(1)} %get-tuple-element.57), channel_id=1, source_target_pairs={{0,2},{1,3},{2,0},{3,1},{4,6},{5,7},{6,4},{7,5},{8,10},{9,11},{10,... | collective-permute-start | bytes 294920 | tf_op jit(solution)/shard_map/ppermute | solution.py:255
  20.9 0.0 collective-permute-done.9.refs_4_
  20.9 1.8 %collective-permute-start.10 = (bf16[2,6,32,128]{3,2,1,0:T(8,128)(2,1)S(1)}, bf16[2,6,32,128]{3,2,1,0:T(8,128)(2,1)S(1)}, u32[]{:S(2)}, u32[]{:S(2)}) collective-permute-start(bf16[2,6,32,128]{3,2,1,0:T(8,128)(2,1)S(1)} %get-tuple-element.55), channel_id=1, source_target_pairs={{0,8},{1,11},{2,10},{3,9},{4,12},{5,15},{6,14},{7,13},{8,0},{9,3},... | collective-permute-start | bytes 294920 | tf_op jit(solution)/shard_map/ppermute | solution.py:255
  22.7 1.6 %collective-permute-start.8 = (bf16[2,6,32,128]{3,2,1,0:T(8,128)(2,1)S(1)}, bf16[2,6,32,128]{3,2,1,0:T(8,128)(2,1)S(1)}, u32[]{:S(2)}, u32[]{:S(2)}) collective-permute-start(bf16[2,6,32,128]{3,2,1,0:T(8,128)(2,1)S(1)} %get-tuple-element.52), channel_id=1, source_target_pairs={{0,12},{1,15},{2,14},{3,13},{4,8},{5,11},{6,10},{7,9},{8,4},{9,7},... | collective-permute-start | bytes 294920 | tf_op jit(solution)/shard_map/ppermute | solution.py:255
  24.3 0.5 %collective-permute-start.14 = (bf16[24,32,128]{2,1,0:T(8,128)(2,1)S(1)}, bf16[24,32,128]{2,1,0:T(8,128)(2,1)S(1)}, u32[]{:S(2)}, u32[]{:S(2)}) collective-permute-start(bf16[24,32,128]{2,1,0:T(8,128)(2,1)S(1)} %forward.1), channel_id=1, source_target_pairs={{0,1},{1,0},{2,3},{3,2},{4,5},{5,4},{6,7},{7,6},{8,9},{9,8},{10,11... | collective-permute-start | bytes 589832 | tf_op jit(solution)/shard_map/ppermute | solution.py:248
  24.8 0.3 factor.1._.factor_ref
  25.1 2.3 %blank.1.blank_ref = f32[2,768,768]{2,1,0:T(8,128)} custom-call(bf16[256,256]{1,0:T(8,128)(2,1)S(1)} %factor.1._.factor_ref), custom_call_target="tpu_custom_call" | custom-call | tf_op jit(solution)/shard_map/blank/pallas_call | solution.py:332
  27.4 4.2 %collective-permute-done.10.refs_8_ = bf16[2,6,32,128]{3,2,1,0:T(8,128)(2,1)S(1)} collective-permute-done((bf16[2,6,32,128]{3,2,1,0:T(8,128)(2,1)S(1)}, bf16[2,6,32,128]{3,2,1,0:T(8,128)(2,1)S(1)}, u32[]{:S(2)}, u32[]{:S(2)}) %collective-permute-start.10) | collective-permute-done | bytes 98336 | tf_op jit(solution)/shard_map/ppermute | solution.py:255
  31.6 0.5 %collective-permute-start.16 = (bf16[2,6,32,128]{3,2,1,0:T(8,128)(2,1)S(1)}, bf16[2,6,32,128]{3,2,1,0:T(8,128)(2,1)S(1)}, u32[]{:S(2)}, u32[]{:S(2)}) collective-permute-start(bf16[2,6,32,128]{3,2,1,0:T(8,128)(2,1)S(1)} %collective-permute-done.10.refs_8_), channel_id=1, source_target_pairs={{0,1},{1,0},{2,3},{3,2},{4,5},{5,4},{6,7},{7,6},{8,9},{9,8},{10,11... | collective-permute-start | bytes 294920 | tf_op jit(solution)/shard_map/ppermute | solution.py:248
  32.1 0.0 collective-permute-start.17
  32.1 0.8 %collective-permute-done.15.refs_10_ = bf16[2,6,32,128]{3,2,1,0:T(8,128)(2,1)S(1)} collective-permute-done((bf16[2,6,32,128]{3,2,1,0:T(8,128)(2,1)S(1)}, bf16[2,6,32,128]{3,2,1,0:T(8,128)(2,1)S(1)}, u32[]{:S(2)}, u32[]{:S(2)}) %collective-permute-start.15) | collective-permute-done | bytes 98336 | tf_op jit(solution)/shard_map/ppermute | solution.py:248
  32.9 0.2 collective-permute-done.16.refs_11_
  33.0 0.4 %collective-permute-done.17.refs_12_ = bf16[2,6,32,128]{3,2,1,0:T(8,128)(2,1)S(1)} collective-permute-done((bf16[2,6,32,128]{3,2,1,0:T(8,128)(2,1)S(1)}, bf16[2,6,32,128]{3,2,1,0:T(8,128)(2,1)S(1)}, u32[]{:S(2)}, u32[]{:S(2)}) %collective-permute-start.17) | collective-permute-done | bytes 98336 | tf_op jit(solution)/shard_map/ppermute | solution.py:248
  33.4 2.1 %exchange.1 = f32[2,768,768]{2,1,0:T(8,128)} custom-call(f32[2,768,768]{2,1,0:T(8,128)} %blank.1.blank_ref, s32[8,128]{1,0:T(8,128)S(1)} %get-tuple-element.61.info_ref, bf16[256,256]{1,0:T(8,128)(2,1)S(1)} %factor.1._.factor_ref, bf16[12,32,128]{2,1,0:T(8,128)(2,1)S(1)} %get-tuple-element.63.self_ref, ...), custom_call_target="tpu_custom_call", output_to_operand_aliasing={{}: (0, {})} | custom-call | tf_op jit(solution)/shard_map/exchange/pallas_call | solution.py:355
  (21 shorter events, 0.1 us)
Async XLA Ops:
  0.0 2.0 %copy-start.1 = (s32[2]{0:T(128)S(1)}, s32[2]{0:T(128)}, u32[]{:S(2)}) copy-start(s32[2]{0:T(128)} %param.7) | copy-start | bytes 28
  0.0 2.0 %copy-start.2 = (s32[32]{0:T(128)S(1)}, s32[32]{0:T(128)}, u32[]{:S(2)}) copy-start(s32[32]{0:T(128)} %param.6) | copy-start | bytes 388
  0.0 2.0 %collective-permute-start = (s32[2]{0:T(128)}, s32[2]{0:T(128)S(1)}, u32[]{:S(2)}, u32[]{:S(2)}) collective-permute-start(s32[2]{0:T(128)} %param.7), channel_id=1, source_target_pairs={{0,1},{1,0},{2,3},{3,2},{4,5},{5,4},{6,7},{7,6},{8,9},{9,8},{10,11... | collective-permute-start | bytes 32 | tf_op jit(solution)/shard_map/ppermute | solution.py:248
  2.1 7.9 %collective-permute-start.6 = (bf16[32,5,32,128]{3,2,1,0:T(8,128)(2,1)S(1)}, bf16[32,5,32,128]{3,2,1,0:T(8,128)(2,1)S(1)}, u32[]{:S(2)}, u32[]{:S(2)}) collective-permute-start(bf16[32,5,32,128]{3,2,1,0:T(8,128)(2,1)S(1)} %slice.4.raw_ref.own_raw), channel_id=1, source_target_pairs={{0,1},{1,0},{2,3},{3,2},{4,5},{5,4},{6,7},{7,6},{8,9},{9,8},{10,11... | collective-permute-start | bytes 3932168 | tf_op jit(solution)/shard_map/ppermute | solution.py:248
  2.8 12.3 %collective-permute-start.1 = (bf16[9,32,128]{2,1,0:T(8,128)(2,1)S(1)}, bf16[9,32,128]{2,1,0:T(8,128)(2,1)S(1)}, u32[]{:S(2)}, u32[]{:S(2)}) collective-permute-start(bf16[9,32,128]{2,1,0:T(8,128)(2,1)S(1)} %get-tuple-element.41), channel_id=1, source_target_pairs={{0,8},{1,11},{2,10},{3,9},{4,12},{5,15},{6,14},{7,13},{8,0},{9,3},... | collective-permute-start | bytes 221192 | tf_op jit(solution)/shard_map/ppermute | solution.py:255
  6.9 8.8 %collective-permute-start.2 = (bf16[9,32,128]{2,1,0:T(8,128)(2,1)S(1)}, bf16[9,32,128]{2,1,0:T(8,128)(2,1)S(1)}, u32[]{:S(2)}, u32[]{:S(2)}) collective-permute-start(bf16[9,32,128]{2,1,0:T(8,128)(2,1)S(1)} %get-tuple-element.42), channel_id=1, source_target_pairs={{0,12},{1,15},{2,14},{3,13},{4,8},{5,11},{6,10},{7,9},{8,4},{9,7},... | collective-permute-start | bytes 221192 | tf_op jit(solution)/shard_map/ppermute | solution.py:255
  8.3 7.5 %collective-permute-start.3 = (bf16[9,32,128]{2,1,0:T(8,128)(2,1)S(1)}, bf16[9,32,128]{2,1,0:T(8,128)(2,1)S(1)}, u32[]{:S(2)}, u32[]{:S(2)}) collective-permute-start(bf16[9,32,128]{2,1,0:T(8,128)(2,1)S(1)} %get-tuple-element.43), channel_id=1, source_target_pairs={{0,4},{1,7},{2,6},{3,5},{4,0},{5,3},{6,2},{7,1},{8,12},{9,15},{10,... | collective-permute-start | bytes 221192 | tf_op jit(solution)/shard_map/ppermute | solution.py:255
  8.5 5.1 %collective-permute-start.4 = (bf16[1,32,128]{2,1,0:T(8,128)(2,1)S(1)}, bf16[1,32,128]{2,1,0:T(8,128)(2,1)S(1)}, u32[]{:S(2)}, u32[]{:S(2)}) collective-permute-start(bf16[1,32,128]{2,1,0:T(8,128)(2,1)S(1)} %get-tuple-element.44), channel_id=1, source_target_pairs={{0,2},{1,3},{2,0},{3,1},{4,6},{5,7},{6,4},{7,5},{8,10},{9,11},{10,... | collective-permute-start | bytes 24584 | tf_op jit(solution)/shard_map/ppermute | solution.py:255
  10.7 10.2 %collective-permute-start.7 = (bf16[8,32,128]{2,1,0:T(8,128)(2,1)S(1)}, bf16[8,32,128]{2,1,0:T(8,128)(2,1)S(1)}, u32[]{:S(2)}, u32[]{:S(2)}) collective-permute-start(bf16[8,32,128]{2,1,0:T(8,128)(2,1)S(1)} %get-tuple-element.51), channel_id=1, source_target_pairs={{0,12},{1,15},{2,14},{3,13},{4,8},{5,11},{6,10},{7,9},{8,4},{9,7},... | collective-permute-start | bytes 196616 | tf_op jit(solution)/shard_map/ppermute | solution.py:255
  13.6 7.2 %collective-permute-start.9 = (bf16[8,32,128]{2,1,0:T(8,128)(2,1)S(1)}, bf16[8,32,128]{2,1,0:T(8,128)(2,1)S(1)}, u32[]{:S(2)}, u32[]{:S(2)}) collective-permute-start(bf16[8,32,128]{2,1,0:T(8,128)(2,1)S(1)} %get-tuple-element.54), channel_id=1, source_target_pairs={{0,8},{1,11},{2,10},{3,9},{4,12},{5,15},{6,14},{7,13},{8,0},{9,3},... | collective-permute-start | bytes 196616 | tf_op jit(solution)/shard_map/ppermute | solution.py:255
  15.1 9.1 %collective-permute-start.13 = (bf16[8,32,128]{2,1,0:T(8,128)(2,1)S(1)}, bf16[8,32,128]{2,1,0:T(8,128)(2,1)S(1)}, u32[]{:S(2)}, u32[]{:S(2)}) collective-permute-start(bf16[8,32,128]{2,1,0:T(8,128)(2,1)S(1)} %get-tuple-element.65), channel_id=1, source_target_pairs={{0,4},{1,7},{2,6},{3,5},{4,0},{5,3},{6,2},{7,1},{8,12},{9,15},{10,... | collective-permute-start | bytes 196616 | tf_op jit(solution)/shard_map/ppermute | solution.py:255
  15.7 9.0 %copy-start = (bf16[16,16]{1,0:T(8,128)(2,1)S(1)}, bf16[16,16]{1,0:T(8,128)(2,1)}, u32[]{:S(2)}) copy-start(bf16[16,16]{1,0:T(8,128)(2,1)} %metric_ref) | copy-start | bytes 1540
  15.8 1.5 %collective-permute-start.5 = (s32[4,128]{1,0:T(4,128)S(1)}, s32[4,128]{1,0:T(4,128)S(1)}, u32[]{:S(2)}, u32[]{:S(2)}) collective-permute-start(s32[4,128]{1,0:T(4,128)S(1)} %counts.1.counts_ref), channel_id=1, source_target_pairs={{0,1},{1,0},{2,3},{3,2},{4,5},{5,4},{6,7},{7,6},{8,9},{9,8},{10,11... | collective-permute-start | bytes 6152 | tf_op jit(solution)/shard_map/ppermute | solution.py:248
  18.2 9.2 %collective-permute-start.11 = (bf16[2,6,32,128]{3,2,1,0:T(8,128)(2,1)S(1)}, bf16[2,6,32,128]{3,2,1,0:T(8,128)(2,1)S(1)}, u32[]{:S(2)}, u32[]{:S(2)}) collective-permute-start(bf16[2,6,32,128]{3,2,1,0:T(8,128)(2,1)S(1)} %get-tuple-element.56), channel_id=1, source_target_pairs={{0,4},{1,7},{2,6},{3,5},{4,0},{5,3},{6,2},{7,1},{8,12},{9,15},{10,... | collective-permute-start | bytes 294920 | tf_op jit(solution)/shard_map/ppermute | solution.py:255
  19.6 7.8 %collective-permute-start.12 = (bf16[12,32,128]{2,1,0:T(8,128)(2,1)S(1)}, bf16[12,32,128]{2,1,0:T(8,128)(2,1)S(1)}, u32[]{:S(2)}, u32[]{:S(2)}) collective-permute-start(bf16[12,32,128]{2,1,0:T(8,128)(2,1)S(1)} %get-tuple-element.57), channel_id=1, source_target_pairs={{0,2},{1,3},{2,0},{3,1},{4,6},{5,7},{6,4},{7,5},{8,10},{9,11},{10,... | collective-permute-start | bytes 294920 | tf_op jit(solution)/shard_map/ppermute | solution.py:255
  20.9 10.7 %collective-permute-start.10 = (bf16[2,6,32,128]{3,2,1,0:T(8,128)(2,1)S(1)}, bf16[2,6,32,128]{3,2,1,0:T(8,128)(2,1)S(1)}, u32[]{:S(2)}, u32[]{:S(2)}) collective-permute-start(bf16[2,6,32,128]{3,2,1,0:T(8,128)(2,1)S(1)} %get-tuple-element.55), channel_id=1, source_target_pairs={{0,8},{1,11},{2,10},{3,9},{4,12},{5,15},{6,14},{7,13},{8,0},{9,3},... | collective-permute-start | bytes 294920 | tf_op jit(solution)/shard_map/ppermute | solution.py:255
  22.7 8.9 %collective-permute-start.8 = (bf16[2,6,32,128]{3,2,1,0:T(8,128)(2,1)S(1)}, bf16[2,6,32,128]{3,2,1,0:T(8,128)(2,1)S(1)}, u32[]{:S(2)}, u32[]{:S(2)}) collective-permute-start(bf16[2,6,32,128]{3,2,1,0:T(8,128)(2,1)S(1)} %get-tuple-element.52), channel_id=1, source_target_pairs={{0,12},{1,15},{2,14},{3,13},{4,8},{5,11},{6,10},{7,9},{8,4},{9,7},... | collective-permute-start | bytes 294920 | tf_op jit(solution)/shard_map/ppermute | solution.py:255
  24.3 7.8 %collective-permute-start.14 = (bf16[24,32,128]{2,1,0:T(8,128)(2,1)S(1)}, bf16[24,32,128]{2,1,0:T(8,128)(2,1)S(1)}, u32[]{:S(2)}, u32[]{:S(2)}) collective-permute-start(bf16[24,32,128]{2,1,0:T(8,128)(2,1)S(1)} %forward.1), channel_id=1, source_target_pairs={{0,1},{1,0},{2,3},{3,2},{4,5},{5,4},{6,7},{7,6},{8,9},{9,8},{10,11... | collective-permute-start | bytes 589832 | tf_op jit(solution)/shard_map/ppermute | solution.py:248
  31.6 1.3 %collective-permute-start.15 = (bf16[2,6,32,128]{3,2,1,0:T(8,128)(2,1)S(1)}, bf16[2,6,32,128]{3,2,1,0:T(8,128)(2,1)S(1)}, u32[]{:S(2)}, u32[]{:S(2)}) collective-permute-start(bf16[2,6,32,128]{3,2,1,0:T(8,128)(2,1)S(1)} %collective-permute-done.11.refs_7_), channel_id=1, source_target_pairs={{0,1},{1,0},{2,3},{3,2},{4,5},{5,4},{6,7},{7,6},{8,9},{9,8},{10,11... | collective-permute-start | bytes 294920 | tf_op jit(solution)/shard_map/ppermute | solution.py:248
  31.6 1.5 %collective-permute-start.16 = (bf16[2,6,32,128]{3,2,1,0:T(8,128)(2,1)S(1)}, bf16[2,6,32,128]{3,2,1,0:T(8,128)(2,1)S(1)}, u32[]{:S(2)}, u32[]{:S(2)}) collective-permute-start(bf16[2,6,32,128]{3,2,1,0:T(8,128)(2,1)S(1)} %collective-permute-done.10.refs_8_), channel_id=1, source_target_pairs={{0,1},{1,0},{2,3},{3,2},{4,5},{5,4},{6,7},{7,6},{8,9},{9,8},{10,11... | collective-permute-start | bytes 294920 | tf_op jit(solution)/shard_map/ppermute | solution.py:248
  32.1 1.3 %collective-permute-start.17 = (bf16[2,6,32,128]{3,2,1,0:T(8,128)(2,1)S(1)}, bf16[2,6,32,128]{3,2,1,0:T(8,128)(2,1)S(1)}, u32[]{:S(2)}, u32[]{:S(2)}) collective-permute-start(bf16[2,6,32,128]{3,2,1,0:T(8,128)(2,1)S(1)} %collective-permute-done.8.refs_9_), channel_id=1, source_target_pairs={{0,1},{1,0},{2,3},{3,2},{4,5},{5,4},{6,7},{7,6},{8,9},{9,8},{10,11... | collective-permute-start | bytes 294920 | tf_op jit(solution)/shard_map/ppermute | solution.py:248

commit v6 on v5

--- a/solution.py
+++ b/solution.py
@@ -38,16 +38,9 @@
     factor_ref[...] = jnp.where(same, spread, 0.0).astype(jnp.bfloat16)
 
 
-def place_blocks(small_ref, ids, held, sem):
-    copy = pltpu.make_async_copy(small_ref, ids, sem)
-    copy.start()
-    copy.wait()
-
-    def place(o, carry):
-        held[ids[o]] = o
-        return carry
-
-    lax.fori_loop(0, held.shape[0], place, 0, unroll=True)
+def place_blocks(small_ref, held):
+    for o in range(held.shape[0]):
+        held[small_ref[0, o]] = o
 
 
 def served(k, f, chip, core):
@@ -56,14 +49,21 @@
 
 
 def early_kernel(hops, small_ref, raw_ref, *refs):
-    *outs, ids, held, sem = refs
-    place_blocks(small_ref, ids, held, sem)
+    *outs, held, ids, sem = refs
+    if outs[0].shape[0] % 2:
+        place_blocks(small_ref, held)
+    else:
+        copy = pltpu.make_async_copy(small_ref, ids, sem)
+        copy.start()
+        copy.wait()
+        for o in range(held.shape[0]):
+            held[ids[0, o]] = o
     blocks, tile = raw_ref.shape[0], raw_ref.shape[2]
     chip, core = position()
     lane = lax.broadcasted_iota(jnp.int32, (tile, 128), 1)
     mine = jnp.zeros((tile, 128), jnp.int32)
     for n in range(4):
-        mine = jnp.where(lane == n, ids[blocks + n], mine)
+        mine = jnp.where(lane == n, small_ref[0:1, blocks + n : blocks + n + 1], mine)
     mine = mine.astype(jnp.float32).astype(jnp.bfloat16)
     for k, out in zip(hops, outs):
         if k > 0:
@@ -84,26 +84,24 @@
 
 def late_kernel(hops, small_ref, counts_ref, crossed_ref, own_raw, peer_raw, *refs):
     outs = refs[: len(hops)]
-    ids, held, direct, crossed, sem, sems = refs[-6:]
+    held, table = refs[-2:]
     blocks, slots = own_raw.shape[0], own_raw.shape[1] + 1
+    half = counts_ref.shape[0]
     chip, core = position()
-    copies = [
-        pltpu.make_async_copy(counts_ref, direct, sems.at[0]),
-        pltpu.make_async_copy(crossed_ref, crossed, sems.at[1]),
-    ]
-    for copy in copies:
-        copy.start()
-    place_blocks(small_ref, ids, held, sem)
-    for copy in copies:
-        copy.wait()
+    place_blocks(small_ref, held)
+    for line in range(4):
+        for k in range(half):
+            table[4 * k + line] = counts_ref[k, line]
+            table[4 * (half + k) + line] = crossed_ref[k, line]
+        table[8 * half + line] = small_ref[0, blocks + line]
 
     def live(block):
         m = lax.bitwise_xor(block // 4, chip)
         far = lax.bitwise_and(lax.bitwise_xor(m, core), 1)
         sender = jnp.where(m >= 2, lax.bitwise_xor(core, far), core)
         line = 2 * lax.bitwise_xor(lax.bitwise_and(block // 2, 1), sender) + lax.bitwise_and(block, 1)
-        near = jnp.where(m == 0, ids[blocks + line], direct[0, line])
-        return jnp.where(m < 2, near, jnp.where(far == 0, direct[m // 2, line], crossed[m // 2, line]))
+        row = jnp.where(m < 2, jnp.where(m == 0, 2 * half, 0), m // 2 + half * far)
+        return table[4 * row + line]
 
     def fill(target, at, raw, first, second, count, start):
         for j in range(slots - start if start == 0 else slots - 1 - start):
@@ -112,21 +110,21 @@
             slot = jnp.where(from_first, j + start, (slots - 1 if start == 0 else slots - 2) - j)
             target[at + j] = raw[block, slot]
 
-    def send(dest, target, start):
+    def send(dest, target, own_start, peer_start):
         first, second = held[2 * dest], held[2 * dest + 1]
         count = live(first)
-        fill(target, 0, own_raw, first, second, count, start)
-        fill(target, target.shape[0] // 2, peer_raw, first, second, count, start)
+        fill(target, 0, own_raw, first, second, count, own_start)
+        fill(target, slots - 1 - own_start if own_start else slots, peer_raw, first, second, count, peer_start)
         return count, second
 
     for k, out in zip(hops, outs):
         if k > 0:
             for f in range(2):
-                send(served(k, f, chip, core), out.at[f], EARLY)
+                send(served(k, f, chip, core), out.at[f], EARLY, EARLY if k > 1 else 0)
         else:
             self_ref, info_ref = refs[len(hops) : len(hops) + 2]
-            send(2 * lax.bitwise_xor(chip, 1) + core, out, 0)
-            count, second = send(2 * chip + core, self_ref, 0)
+            send(2 * lax.bitwise_xor(chip, 1) + core, out, 0, 0)
+            count, second = send(2 * chip + core, self_ref, 0, 0)
             row = lax.broadcasted_iota(jnp.int32, info_ref.shape, 0)
             info_ref[...] = jnp.where(row == 0, count, live(second))
 
@@ -154,12 +152,10 @@
 def exchange_kernel(chips, blank_ref, info_ref, factor_ref, self_ref, side_ref, *refs):
     half = chips // 2
     first, refs = refs[: half - 1], refs[half - 1 :]
-    second, refs = refs[: half - 1], refs[half - 1 :]
+    second, refs = (None, *refs[: half - 2]), refs[half - 2 :]
     forwarded, refs = refs[0], refs[1:]
     third, third_crossed, refs = refs[: half - 1], refs[half - 1 : 2 * half - 2], refs[2 * half - 2 :]
-    out_ref, rows, stage, live, sem, sems = refs
-    copy = pltpu.make_async_copy(info_ref, live, sem)
-    copy.start()
+    out_ref, rows, stage, sems = refs
     doubled, orbitals, width = self_ref.shape
     slots = doubled // 2
     wide = factor_ref.shape[0]
@@ -184,10 +180,13 @@
                 late_ref = (third, third_crossed)[f][k - 1]
                 for q in range(2):
                     base = q * own_late
+                    if q == 1 and k == 1:
+                        found.append(late_ref[f, base + s, at, :])
+                        continue
                     if f == 0:
                         early_ref, early_base = (first, second)[q][k - 1], 0
                     else:
-                        early_ref, early_base = forwarded, 2 * EARLY * (k - 1 + q * (half - 1))
+                        early_ref, early_base = forwarded, 2 * EARLY * (k - 1 + q * (half - 2))
                     found.append(
                         choose(
                             s,
@@ -206,6 +205,8 @@
         fitted = jnp.dot(factor_ref[...], jnp.concatenate(columns, axis=1), preferred_element_type=jnp.float32)
         rows[part * wide : (part + 1) * wide, :] = fitted.astype(jnp.bfloat16)
 
+    live = [info_ref[which, 0] for which in range(2)]
+
     def tiles(s, act):
         for which in range(2):
             row = s if which == 0 else slots - 1 - s
@@ -213,7 +214,7 @@
                 column = t if which == 0 else slots - 1 - t
                 if max(row, column) < slots - 1:
 
-                    @pl.when(max(row, column) < live[which, 0])
+                    @pl.when(max(row, column) < live[which])
                     def _(which=which, row=row, column=column, t=t):
                         act(
                             pltpu.make_async_copy(
@@ -228,8 +229,6 @@
             stage[span(s), :] = lax.dot_general(
                 rows[:, span(s)], rows[...], (((0,), (0,)), ((), ())), preferred_element_type=jnp.float32
             )
-        if 0 in group:
-            copy.wait()
         for s in group:
             tiles(s, lambda copy: copy.start())
     for s in range(slots):
@@ -258,14 +257,13 @@
         return jax.ShapeDtypeStruct(dims, raw.dtype)
 
     other, raw = tie((swap(counts), raw[:, : slots - 1]))
-    small = jnp.concatenate([owner_map, counts, other, jnp.zeros((lines - blocks - 4,), jnp.int32)])
+    small = jnp.concatenate([owner_map, counts, other, jnp.zeros((lines - blocks - 4,), jnp.int32)]).reshape(1, lines)
     raw_there, small = tie((raw, small))
     peer_raw = swap(raw_there)
 
     far = [*reversed(range(2, half))]
     near = [1, 0]
-    place = [pltpu.SMEM((lines,), jnp.int32), pltpu.SMEM((blocks,), jnp.int32)]
-    one = pltpu.SemaphoreType.DMA(())
+    place = pltpu.SMEM((blocks,), jnp.int32)
 
     def early(hops, raw, counted):
         return pl.pallas_call(
@@ -273,7 +271,7 @@
             out_shape=[shape((4 * EARLY if k else 0) + counted, orbitals, width) for k in hops],
             in_specs=[VMEM] * 2,
             out_specs=[VMEM] * len(hops),
-            scratch_shapes=place + [one],
+            scratch_shapes=[place, pltpu.SMEM((1, lines), jnp.int32), pltpu.SemaphoreType.DMA(())],
             compiler_params=LIMIT,
             name="early",
         )(small, raw)
@@ -283,8 +281,7 @@
 
     ways = far[::-1] + near
     first = hops(ways, early(ways, raw, 1))
-    *second, beside = hops(ways[:-1], early(ways[:-1], peer_raw, 0))
-    second = [*second[::-1], beside]
+    second = hops(ways[:-2], early(ways[:-2], peer_raw, 0))[::-1]
     *first, beside, side = tie(first)
     first = [side, beside, *first]
     brought = pl.pallas_call(
@@ -299,16 +296,15 @@
 
     def late(ks, small, extra=()):
         own = slots - 1 - EARLY
-        out_shape = [shape(2, 2 * own, orbitals, width) if k else shape(2 * slots, orbitals, width) for k in ks]
+        tiles = [own + (own if k > 1 else slots) for k in ks]
+        out_shape = [shape(2, n, orbitals, width) if k else shape(2 * slots, orbitals, width) for k, n in zip(ks, tiles)]
         out_shape += extra
         return pl.pallas_call(
             functools.partial(late_kernel, ks),
             out_shape=out_shape,
             in_specs=[VMEM] * 5,
             out_specs=[VMEM] * len(out_shape),
-            scratch_shapes=place
-            + [pltpu.SMEM((half, 128), jnp.int32)] * 2
-            + [one, pltpu.SemaphoreType.DMA((2,))],
+            scratch_shapes=[place, pltpu.SMEM((8 * half + 4,), jnp.int32)],
             compiler_params=LIMIT,
             cost_estimate=pl.CostEstimate(flops=0, bytes_accessed=1024, transcendentals=0),
             name="late",
@@ -319,7 +315,7 @@
     )
     pairs = [tie((x, y)) for x, y in zip(third[: len(far)], second)]
     third = [x for x, _ in pairs] + third[len(pairs) :]
-    second = [y for _, y in pairs] + second[len(pairs) :]
+    second = [y for _, y in pairs]
     metric, own_tiles = tie((metric, own))
     factor = pl.pallas_call(
         factor_kernel,
@@ -343,8 +339,8 @@
     second = second[::-1]
     forwarded = pl.pallas_call(
         forward_kernel,
-        out_shape=shape((2 * half - 2) * 2 * EARLY, orbitals, width),
-        in_specs=[VMEM] * (2 * half - 2),
+        out_shape=shape((2 * half - 3) * 2 * EARLY, orbitals, width),
+        in_specs=[VMEM] * (2 * half - 3),
         out_specs=VMEM,
         compiler_params=LIMIT,
         name="forward",
@@ -355,13 +351,11 @@
     return pl.pallas_call(
         functools.partial(exchange_kernel, chips),
         out_shape=jax.ShapeDtypeStruct((2, slots * width, slots * width), jnp.float32),
-        in_specs=[HBM] + [VMEM] * (4 * half + 1),
+        in_specs=[HBM] + [VMEM] * (4 * half),
         out_specs=HBM,
         scratch_shapes=[
             pltpu.VMEM((devices * orbitals, slots * width), raw.dtype),
             pltpu.VMEM((slots * width, slots * width), jnp.float32),
-            pltpu.SMEM((8, 128), jnp.int32),
-            one,
             pltpu.SemaphoreType.DMA((2, slots)),
         ],
         input_output_aliases={0: 0},

time: 35.8 us -> 35.1 us (0.980)
  waiting for transfers between devices: 6.31 us -> 8.4 us
  starting transfers between devices: 20.5 us -> 18.9 us
  Pallas kernels: 6.89 us -> 5.88 us
    ppermute x11 -> x10, waiting for transfers between devices: 4.19 us -> 5.95 us  [hop(): return lax.ppermute(x, 'aux', [(i, target(i)) for i in range(devices)])]
    ppermute x11 -> x10, starting transfers between devices: 18.3 us -> 17.3 us  [hop(): return lax.ppermute(x, 'aux', [(i, target(i)) for i in range(devices)])]
    ppermute x7, starting transfers between devices: 2.26 us -> 1.62 us  [swap(): return lax.ppermute(x, 'aux', [(i, i ^ 1) for i in range(devices)])]
    pallas_call x1, Pallas kernels: 0.95 us -> 0.46 us  [late(): pl.pallas_call(functools.partial(late_kernel, ks), out_shape=out_shape, i...]
    pallas_call x2, Pallas kernels: 1.23 us -> 0.78 us  [early(): pl.pallas_call(functools.partial(early_kernel, hops), out_shape=[shape((4...]
  transfers between devices with their start and end apart: 18 -> 17, of which waited for: 5 -> 5; matrix products, arithmetic and copies ran while one was open for 4% -> 4% of each run, Pallas kernels for 13% -> 11%
where the time goes in v6:
time: 35.1 us; the launch traced here: 35 us
  starting transfers between devices  18.9 us (54%)
  waiting for transfers between devices  8.4 us (24%)
  Pallas kernels  5.88 us (17%)
  local copies, waits for them, and re-layouts  1.56 us (4%)
    ppermute x10, starting transfers between devices, hop(): return lax.ppermute(x, 'aux', [(i, target(i)) for i in range(devices)])  17.3 us
    ppermute x10, waiting for transfers between devices, hop(): return lax.ppermute(x, 'aux', [(i, target(i)) for i in range(devices)])  5.95 us
    ppermute x7, waiting for transfers between devices, swap(): return lax.ppermute(x, 'aux', [(i, i ^ 1) for i in range(devices)])  2.45 us
    pallas_call x1, Pallas kernels, shards(): pl.pallas_call(lambda _, *refs: blank_kernel(*refs), out_shape=jax.ShapeD...  2.3 us
    pallas_call x1, Pallas kernels, shards(): pl.pallas_call(functools.partial(exchange_kernel, chips), out_shape=jax.S...  2.03 us
    ppermute x7, starting transfers between devices, swap(): return lax.ppermute(x, 'aux', [(i, i ^ 1) for i in range(devices)])  1.62 us
    slice x1, local copies, waits for them, and re-layouts, shards(): other, raw = tie((swap(counts), raw[:, :slots - 1]))  1.55 us
    pallas_call x2, Pallas kernels, early(): pl.pallas_call(functools.partial(early_kernel, hops), out_shape=[shape((4...  0.78 us
  transfers between devices with their start and end apart: 17, of which 5 were waited for; matrix products, arithmetic and copies ran while one was open for 4% of the time, Pallas kernels for 11%

profile of v6, /device:TPU:0, one launch (start us, length us, event | category | flops | bytes accessed | tf_op | source)
XLA Modules:
  0.0 35.0 jit_solution(17314668196919597469)
XLA Ops:
  0.0 0.5 %collective-permute-start = (s32[2]{0:T(128)}, s32[2]{0:T(128)S(1)}, u32[]{:S(2)}, u32[]{:S(2)}) collective-permute-start(s32[2]{0:T(128)} %param.7), channel_id=1, source_target_pairs={{0,1},{1,0},{2,3},{3,2},{4,5},{5,4},{6,7},{7,6},{8,9},{9,8},{10,11... | collective-permute-start | bytes 32 | tf_op jit(solution)/shard_map/ppermute | solution.py:247
  0.5 1.5 %slice.4.raw_ref.own_raw = bf16[32,5,32,128]{3,2,1,0:T(8,128)(2,1)S(1)} slice(bf16[32,6,32,128]{3,2,1,0:T(8,128)(2,1)} %bitcast.5), slice={[0:32], [0:5], [0:32], [0:128]} | slice | bytes 2621440 | tf_op jit(solution)/shard_map/slice | solution.py:259
  2.0 0.1 add_bitcast_fusion.small_ref
  2.1 0.1 collective-permute-start.6
  2.2 0.2 early.2
  2.4 4.1 %collective-permute-start.1 = (bf16[9,32,128]{2,1,0:T(8,128)(2,1)S(1)}, bf16[9,32,128]{2,1,0:T(8,128)(2,1)S(1)}, u32[]{:S(2)}, u32[]{:S(2)}) collective-permute-start(bf16[9,32,128]{2,1,0:T(8,128)(2,1)S(1)} %get-tuple-element.40), channel_id=1, source_target_pairs={{0,8},{1,11},{2,10},{3,9},{4,12},{5,15},{6,14},{7,13},{8,0},{9,3},... | collective-permute-start | bytes 221192 | tf_op jit(solution)/shard_map/ppermute | solution.py:254
  6.5 1.3 %collective-permute-start.2 = (bf16[9,32,128]{2,1,0:T(8,128)(2,1)S(1)}, bf16[9,32,128]{2,1,0:T(8,128)(2,1)S(1)}, u32[]{:S(2)}, u32[]{:S(2)}) collective-permute-start(bf16[9,32,128]{2,1,0:T(8,128)(2,1)S(1)} %get-tuple-element.41), channel_id=1, source_target_pairs={{0,12},{1,15},{2,14},{3,13},{4,8},{5,11},{6,10},{7,9},{8,4},{9,7},... | collective-permute-start | bytes 221192 | tf_op jit(solution)/shard_map/ppermute | solution.py:254
  7.8 0.2 collective-permute-start.3
  8.0 1.5 %collective-permute-start.4 = (bf16[1,32,128]{2,1,0:T(8,128)(2,1)S(1)}, bf16[1,32,128]{2,1,0:T(8,128)(2,1)S(1)}, u32[]{:S(2)}, u32[]{:S(2)}) collective-permute-start(bf16[1,32,128]{2,1,0:T(8,128)(2,1)S(1)} %get-tuple-element.43), channel_id=1, source_target_pairs={{0,2},{1,3},{2,0},{3,1},{4,6},{5,7},{6,4},{7,5},{8,10},{9,11},{10,... | collective-permute-start | bytes 24584 | tf_op jit(solution)/shard_map/ppermute | solution.py:254
  9.6 0.0 collective-permute-done.6.peer_raw.raw_ref
  9.6 0.6 %early.3 = (bf16[8,32,128]{2,1,0:T(8,128)(2,1)S(1)}, bf16[8,32,128]{2,1,0:T(8,128)(2,1)S(1)}) custom-call(s32[1,128]{1,0:T(1,128)S(1)} %add_bitcast_fusion.small_ref, bf16[32,5,32,128]{3,2,1,0:T(8,128)(2,1)S(1)} %collective-permute-done.6.peer_raw.raw_ref), custom_call_target="tpu_custom_call" | custom-call | tf_op jit(solution)/shard_map/early/pallas_call | solution.py:269
  10.2 3.0 %collective-permute-start.7 = (bf16[8,32,128]{2,1,0:T(8,128)(2,1)S(1)}, bf16[8,32,128]{2,1,0:T(8,128)(2,1)S(1)}, u32[]{:S(2)}, u32[]{:S(2)}) collective-permute-start(bf16[8,32,128]{2,1,0:T(8,128)(2,1)S(1)} %get-tuple-element.50), channel_id=1, source_target_pairs={{0,12},{1,15},{2,14},{3,13},{4,8},{5,11},{6,10},{7,9},{8,4},{9,7},... | collective-permute-start | bytes 196616 | tf_op jit(solution)/shard_map/ppermute | solution.py:254
  13.2 1.5 %collective-permute-start.9 = (bf16[8,32,128]{2,1,0:T(8,128)(2,1)S(1)}, bf16[8,32,128]{2,1,0:T(8,128)(2,1)S(1)}, u32[]{:S(2)}, u32[]{:S(2)}) collective-permute-start(bf16[8,32,128]{2,1,0:T(8,128)(2,1)S(1)} %get-tuple-element.53), channel_id=1, source_target_pairs={{0,8},{1,11},{2,10},{3,9},{4,12},{5,15},{6,14},{7,13},{8,0},{9,3},... | collective-permute-start | bytes 196616 | tf_op jit(solution)/shard_map/ppermute | solution.py:254
  14.7 0.0 copy-start
  14.7 0.1 collective-permute-start.5
  14.8 1.1 %collective-permute-done.5.crossed_ref = s32[4,128]{1,0:T(4,128)S(1)} collective-permute-done((s32[4,128]{1,0:T(4,128)S(1)}, s32[4,128]{1,0:T(4,128)S(1)}, u32[]{:S(2)}, u32[]{:S(2)}) %collective-permute-start.5) | collective-permute-done | bytes 2080 | tf_op jit(solution)/shard_map/ppermute | solution.py:247
  16.0 0.5 %late.1 = (bf16[2,6,32,128]{3,2,1,0:T(8,128)(2,1)S(1)}, bf16[2,6,32,128]{3,2,1,0:T(8,128)(2,1)S(1)}, bf16[2,9,32,128]{3,2,1,0:T(8,128)(2,1)S(1)}, bf16[12,32,128...) custom-call(s32[1,128]{1,0:T(1,128)S(1)} %add_bitcast_fusion.small_ref, ...), custom_call_target="tpu_custom_call" | custom-call | bytes 1024 | tf_op jit(solution)/shard_map/late/pallas_call | solution.py:302
  16.4 0.7 %collective-permute-start.11 = (bf16[2,9,32,128]{3,2,1,0:T(8,128)(2,1)S(1)}, bf16[2,9,32,128]{3,2,1,0:T(8,128)(2,1)S(1)}, u32[]{:S(2)}, u32[]{:S(2)}) collective-permute-start(bf16[2,9,32,128]{3,2,1,0:T(8,128)(2,1)S(1)} %get-tuple-element.55), channel_id=1, source_target_pairs={{0,4},{1,7},{2,6},{3,5},{4,0},{5,3},{6,2},{7,1},{8,12},{9,15},{10,... | collective-permute-start | bytes 442376 | tf_op jit(solution)/shard_map/ppermute | solution.py:254
  17.2 1.4 %collective-permute-start.12 = (bf16[12,32,128]{2,1,0:T(8,128)(2,1)S(1)}, bf16[12,32,128]{2,1,0:T(8,128)(2,1)S(1)}, u32[]{:S(2)}, u32[]{:S(2)}) collective-permute-start(bf16[12,32,128]{2,1,0:T(8,128)(2,1)S(1)} %get-tuple-element.56), channel_id=1, source_target_pairs={{0,2},{1,3},{2,0},{3,1},{4,6},{5,7},{6,4},{7,5},{8,10},{9,11},{10,... | collective-permute-start | bytes 294920 | tf_op jit(solution)/shard_map/ppermute | solution.py:254
  18.6 1.8 %collective-permute-done.9.refs_3_ = bf16[8,32,128]{2,1,0:T(8,128)(2,1)S(1)} collective-permute-done((bf16[8,32,128]{2,1,0:T(8,128)(2,1)S(1)}, bf16[8,32,128]{2,1,0:T(8,128)(2,1)S(1)}, u32[]{:S(2)}, u32[]{:S(2)}) %collective-permute-start.9) | collective-permute-done | bytes 65568 | tf_op jit(solution)/shard_map/ppermute | solution.py:254
  20.4 1.4 %collective-permute-start.10 = (bf16[2,6,32,128]{3,2,1,0:T(8,128)(2,1)S(1)}, bf16[2,6,32,128]{3,2,1,0:T(8,128)(2,1)S(1)}, u32[]{:S(2)}, u32[]{:S(2)}) collective-permute-start(bf16[2,6,32,128]{3,2,1,0:T(8,128)(2,1)S(1)} %get-tuple-element.54), channel_id=1, source_target_pairs={{0,8},{1,11},{2,10},{3,9},{4,12},{5,15},{6,14},{7,13},{8,0},{9,3},... | collective-permute-start | bytes 294920 | tf_op jit(solution)/shard_map/ppermute | solution.py:254
  21.7 2.1 %collective-permute-start.8 = (bf16[2,6,32,128]{3,2,1,0:T(8,128)(2,1)S(1)}, bf16[2,6,32,128]{3,2,1,0:T(8,128)(2,1)S(1)}, u32[]{:S(2)}, u32[]{:S(2)}) collective-permute-start(bf16[2,6,32,128]{3,2,1,0:T(8,128)(2,1)S(1)} %get-tuple-element.51), channel_id=1, source_target_pairs={{0,12},{1,15},{2,14},{3,13},{4,8},{5,11},{6,10},{7,9},{8,4},{9,7},... | collective-permute-start | bytes 294920 | tf_op jit(solution)/shard_map/ppermute | solution.py:254
  23.9 0.5 %collective-permute-start.13 = (bf16[20,32,128]{2,1,0:T(8,128)(2,1)S(1)}, bf16[20,32,128]{2,1,0:T(8,128)(2,1)S(1)}, u32[]{:S(2)}, u32[]{:S(2)}) collective-permute-start(bf16[20,32,128]{2,1,0:T(8,128)(2,1)S(1)} %forward.1), channel_id=1, source_target_pairs={{0,1},{1,0},{2,3},{3,2},{4,5},{5,4},{6,7},{7,6},{8,9},{9,8},{10,11... | collective-permute-start | bytes 491528 | tf_op jit(solution)/shard_map/ppermute | solution.py:247
  24.4 0.3 factor.1._.factor_ref
  24.7 2.3 %blank.1.blank_ref = f32[2,768,768]{2,1,0:T(8,128)} custom-call(bf16[256,256]{1,0:T(8,128)(2,1)S(1)} %factor.1._.factor_ref), custom_call_target="tpu_custom_call" | custom-call | tf_op jit(solution)/shard_map/blank/pallas_call | solution.py:328
  27.0 0.0 collective-permute-done.11.refs_6_
  27.0 4.1 %collective-permute-done.10.refs_7_ = bf16[2,6,32,128]{3,2,1,0:T(8,128)(2,1)S(1)} collective-permute-done((bf16[2,6,32,128]{3,2,1,0:T(8,128)(2,1)S(1)}, bf16[2,6,32,128]{3,2,1,0:T(8,128)(2,1)S(1)}, u32[]{:S(2)}, u32[]{:S(2)}) %collective-permute-start.10) | collective-permute-done | bytes 98336 | tf_op jit(solution)/shard_map/ppermute | solution.py:254
  31.1 0.5 %collective-permute-start.15 = (bf16[2,6,32,128]{3,2,1,0:T(8,128)(2,1)S(1)}, bf16[2,6,32,128]{3,2,1,0:T(8,128)(2,1)S(1)}, u32[]{:S(2)}, u32[]{:S(2)}) collective-permute-start(bf16[2,6,32,128]{3,2,1,0:T(8,128)(2,1)S(1)} %collective-permute-done.10.refs_7_), channel_id=1, source_target_pairs={{0,1},{1,0},{2,3},{3,2},{4,5},{5,4},{6,7},{7,6},{8,9},{9,8},{10,11... | collective-permute-start | bytes 294920 | tf_op jit(solution)/shard_map/ppermute | solution.py:247
  31.7 0.0 collective-permute-start.16
  31.7 1.0 %collective-permute-done.15.refs_10_ = bf16[2,6,32,128]{3,2,1,0:T(8,128)(2,1)S(1)} collective-permute-done((bf16[2,6,32,128]{3,2,1,0:T(8,128)(2,1)S(1)}, bf16[2,6,32,128]{3,2,1,0:T(8,128)(2,1)S(1)}, u32[]{:S(2)}, u32[]{:S(2)}) %collective-permute-start.15) | collective-permute-done | bytes 98336 | tf_op jit(solution)/shard_map/ppermute | solution.py:247
  32.7 0.3 collective-permute-done.16.refs_11_
  33.0 2.0 %exchange.1 = f32[2,768,768]{2,1,0:T(8,128)} custom-call(f32[2,768,768]{2,1,0:T(8,128)} %blank.1.blank_ref, s32[8,128]{1,0:T(8,128)S(1)} %get-tuple-element.60.info_ref, bf16[256,256]{1,0:T(8,128)(2,1)S(1)} %factor.1._.factor_ref, bf16[12,32,128]{2,1,0:T(8,128)(2,1)S(1)} %get-tuple-element.62.self_ref, ...), custom_call_target="tpu_custom_call", output_to_operand_aliasing={{}: (0, {})} | custom-call | tf_op jit(solution)/shard_map/exchange/pallas_call | solution.py:351
  (19 shorter events, 0.1 us)
Async XLA Ops:
  0.0 2.0 %copy-start.1 = (s32[2]{0:T(128)S(1)}, s32[2]{0:T(128)}, u32[]{:S(2)}) copy-start(s32[2]{0:T(128)} %param.7) | copy-start | bytes 28
  0.0 2.0 %copy-start.2 = (s32[32]{0:T(128)S(1)}, s32[32]{0:T(128)}, u32[]{:S(2)}) copy-start(s32[32]{0:T(128)} %param.6) | copy-start | bytes 388
  0.0 2.0 %collective-permute-start = (s32[2]{0:T(128)}, s32[2]{0:T(128)S(1)}, u32[]{:S(2)}, u32[]{:S(2)}) collective-permute-start(s32[2]{0:T(128)} %param.7), channel_id=1, source_target_pairs={{0,1},{1,0},{2,3},{3,2},{4,5},{5,4},{6,7},{7,6},{8,9},{9,8},{10,11... | collective-permute-start | bytes 32 | tf_op jit(solution)/shard_map/ppermute | solution.py:247
  2.1 7.5 %collective-permute-start.6 = (bf16[32,5,32,128]{3,2,1,0:T(8,128)(2,1)S(1)}, bf16[32,5,32,128]{3,2,1,0:T(8,128)(2,1)S(1)}, u32[]{:S(2)}, u32[]{:S(2)}) collective-permute-start(bf16[32,5,32,128]{3,2,1,0:T(8,128)(2,1)S(1)} %slice.4.raw_ref.own_raw), channel_id=1, source_target_pairs={{0,1},{1,0},{2,3},{3,2},{4,5},{5,4},{6,7},{7,6},{8,9},{9,8},{10,11... | collective-permute-start | bytes 3932168 | tf_op jit(solution)/shard_map/ppermute | solution.py:247
  2.4 12.3 %collective-permute-start.1 = (bf16[9,32,128]{2,1,0:T(8,128)(2,1)S(1)}, bf16[9,32,128]{2,1,0:T(8,128)(2,1)S(1)}, u32[]{:S(2)}, u32[]{:S(2)}) collective-permute-start(bf16[9,32,128]{2,1,0:T(8,128)(2,1)S(1)} %get-tuple-element.40), channel_id=1, source_target_pairs={{0,8},{1,11},{2,10},{3,9},{4,12},{5,15},{6,14},{7,13},{8,0},{9,3},... | collective-permute-start | bytes 221192 | tf_op jit(solution)/shard_map/ppermute | solution.py:254
  6.5 8.2 %collective-permute-start.2 = (bf16[9,32,128]{2,1,0:T(8,128)(2,1)S(1)}, bf16[9,32,128]{2,1,0:T(8,128)(2,1)S(1)}, u32[]{:S(2)}, u32[]{:S(2)}) collective-permute-start(bf16[9,32,128]{2,1,0:T(8,128)(2,1)S(1)} %get-tuple-element.41), channel_id=1, source_target_pairs={{0,12},{1,15},{2,14},{3,13},{4,8},{5,11},{6,10},{7,9},{8,4},{9,7},... | collective-permute-start | bytes 221192 | tf_op jit(solution)/shard_map/ppermute | solution.py:254
  7.8 6.9 %collective-permute-start.3 = (bf16[9,32,128]{2,1,0:T(8,128)(2,1)S(1)}, bf16[9,32,128]{2,1,0:T(8,128)(2,1)S(1)}, u32[]{:S(2)}, u32[]{:S(2)}) collective-permute-start(bf16[9,32,128]{2,1,0:T(8,128)(2,1)S(1)} %get-tuple-element.42), channel_id=1, source_target_pairs={{0,4},{1,7},{2,6},{3,5},{4,0},{5,3},{6,2},{7,1},{8,12},{9,15},{10,... | collective-permute-start | bytes 221192 | tf_op jit(solution)/shard_map/ppermute | solution.py:254
  8.0 5.1 %collective-permute-start.4 = (bf16[1,32,128]{2,1,0:T(8,128)(2,1)S(1)}, bf16[1,32,128]{2,1,0:T(8,128)(2,1)S(1)}, u32[]{:S(2)}, u32[]{:S(2)}) collective-permute-start(bf16[1,32,128]{2,1,0:T(8,128)(2,1)S(1)} %get-tuple-element.43), channel_id=1, source_target_pairs={{0,2},{1,3},{2,0},{3,1},{4,6},{5,7},{6,4},{7,5},{8,10},{9,11},{10,... | collective-permute-start | bytes 24584 | tf_op jit(solution)/shard_map/ppermute | solution.py:254
  10.2 8.4 %collective-permute-start.7 = (bf16[8,32,128]{2,1,0:T(8,128)(2,1)S(1)}, bf16[8,32,128]{2,1,0:T(8,128)(2,1)S(1)}, u32[]{:S(2)}, u32[]{:S(2)}) collective-permute-start(bf16[8,32,128]{2,1,0:T(8,128)(2,1)S(1)} %get-tuple-element.50), channel_id=1, source_target_pairs={{0,12},{1,15},{2,14},{3,13},{4,8},{5,11},{6,10},{7,9},{8,4},{9,7},... | collective-permute-start | bytes 196616 | tf_op jit(solution)/shard_map/ppermute | solution.py:254
  13.2 7.2 %collective-permute-start.9 = (bf16[8,32,128]{2,1,0:T(8,128)(2,1)S(1)}, bf16[8,32,128]{2,1,0:T(8,128)(2,1)S(1)}, u32[]{:S(2)}, u32[]{:S(2)}) collective-permute-start(bf16[8,32,128]{2,1,0:T(8,128)(2,1)S(1)} %get-tuple-element.53), channel_id=1, source_target_pairs={{0,8},{1,11},{2,10},{3,9},{4,12},{5,15},{6,14},{7,13},{8,0},{9,3},... | collective-permute-start | bytes 196616 | tf_op jit(solution)/shard_map/ppermute | solution.py:254
  14.7 9.7 %copy-start = (bf16[16,16]{1,0:T(8,128)(2,1)S(1)}, bf16[16,16]{1,0:T(8,128)(2,1)}, u32[]{:S(2)}) copy-start(bf16[16,16]{1,0:T(8,128)(2,1)} %metric_ref) | copy-start | bytes 1540
  14.7 1.2 %collective-permute-start.5 = (s32[4,128]{1,0:T(4,128)S(1)}, s32[4,128]{1,0:T(4,128)S(1)}, u32[]{:S(2)}, u32[]{:S(2)}) collective-permute-start(s32[4,128]{1,0:T(4,128)S(1)} %counts.1.counts_ref), channel_id=1, source_target_pairs={{0,1},{1,0},{2,3},{3,2},{4,5},{5,4},{6,7},{7,6},{8,9},{9,8},{10,11... | collective-permute-start | bytes 6152 | tf_op jit(solution)/shard_map/ppermute | solution.py:247
  16.4 10.6 %collective-permute-start.11 = (bf16[2,9,32,128]{3,2,1,0:T(8,128)(2,1)S(1)}, bf16[2,9,32,128]{3,2,1,0:T(8,128)(2,1)S(1)}, u32[]{:S(2)}, u32[]{:S(2)}) collective-permute-start(bf16[2,9,32,128]{3,2,1,0:T(8,128)(2,1)S(1)} %get-tuple-element.55), channel_id=1, source_target_pairs={{0,4},{1,7},{2,6},{3,5},{4,0},{5,3},{6,2},{7,1},{8,12},{9,15},{10,... | collective-permute-start | bytes 442376 | tf_op jit(solution)/shard_map/ppermute | solution.py:254
  17.2 9.8 %collective-permute-start.12 = (bf16[12,32,128]{2,1,0:T(8,128)(2,1)S(1)}, bf16[12,32,128]{2,1,0:T(8,128)(2,1)S(1)}, u32[]{:S(2)}, u32[]{:S(2)}) collective-permute-start(bf16[12,32,128]{2,1,0:T(8,128)(2,1)S(1)} %get-tuple-element.56), channel_id=1, source_target_pairs={{0,2},{1,3},{2,0},{3,1},{4,6},{5,7},{6,4},{7,5},{8,10},{9,11},{10,... | collective-permute-start | bytes 294920 | tf_op jit(solution)/shard_map/ppermute | solution.py:254
  20.4 10.8 %collective-permute-start.10 = (bf16[2,6,32,128]{3,2,1,0:T(8,128)(2,1)S(1)}, bf16[2,6,32,128]{3,2,1,0:T(8,128)(2,1)S(1)}, u32[]{:S(2)}, u32[]{:S(2)}) collective-permute-start(bf16[2,6,32,128]{3,2,1,0:T(8,128)(2,1)S(1)} %get-tuple-element.54), channel_id=1, source_target_pairs={{0,8},{1,11},{2,10},{3,9},{4,12},{5,15},{6,14},{7,13},{8,0},{9,3},... | collective-permute-start | bytes 294920 | tf_op jit(solution)/shard_map/ppermute | solution.py:254
  21.7 9.4 %collective-permute-start.8 = (bf16[2,6,32,128]{3,2,1,0:T(8,128)(2,1)S(1)}, bf16[2,6,32,128]{3,2,1,0:T(8,128)(2,1)S(1)}, u32[]{:S(2)}, u32[]{:S(2)}) collective-permute-start(bf16[2,6,32,128]{3,2,1,0:T(8,128)(2,1)S(1)} %get-tuple-element.51), channel_id=1, source_target_pairs={{0,12},{1,15},{2,14},{3,13},{4,8},{5,11},{6,10},{7,9},{8,4},{9,7},... | collective-permute-start | bytes 294920 | tf_op jit(solution)/shard_map/ppermute | solution.py:254
  23.9 7.8 %collective-permute-start.13 = (bf16[20,32,128]{2,1,0:T(8,128)(2,1)S(1)}, bf16[20,32,128]{2,1,0:T(8,128)(2,1)S(1)}, u32[]{:S(2)}, u32[]{:S(2)}) collective-permute-start(bf16[20,32,128]{2,1,0:T(8,128)(2,1)S(1)} %forward.1), channel_id=1, source_target_pairs={{0,1},{1,0},{2,3},{3,2},{4,5},{5,4},{6,7},{7,6},{8,9},{9,8},{10,11... | collective-permute-start | bytes 491528 | tf_op jit(solution)/shard_map/ppermute | solution.py:247
  31.1 1.8 %collective-permute-start.14 = (bf16[2,9,32,128]{3,2,1,0:T(8,128)(2,1)S(1)}, bf16[2,9,32,128]{3,2,1,0:T(8,128)(2,1)S(1)}, u32[]{:S(2)}, u32[]{:S(2)}) collective-permute-start(bf16[2,9,32,128]{3,2,1,0:T(8,128)(2,1)S(1)} %collective-permute-done.11.refs_6_), channel_id=1, source_target_pairs={{0,1},{1,0},{2,3},{3,2},{4,5},{5,4},{6,7},{7,6},{8,9},{9,8},{10,11... | collective-permute-start | bytes 442376 | tf_op jit(solution)/shard_map/ppermute | solution.py:247
  31.1 1.5 %collective-permute-start.15 = (bf16[2,6,32,128]{3,2,1,0:T(8,128)(2,1)S(1)}, bf16[2,6,32,128]{3,2,1,0:T(8,128)(2,1)S(1)}, u32[]{:S(2)}, u32[]{:S(2)}) collective-permute-start(bf16[2,6,32,128]{3,2,1,0:T(8,128)(2,1)S(1)} %collective-permute-done.10.refs_7_), channel_id=1, source_target_pairs={{0,1},{1,0},{2,3},{3,2},{4,5},{5,4},{6,7},{7,6},{8,9},{9,8},{10,11... | collective-permute-start | bytes 294920 | tf_op jit(solution)/shard_map/ppermute | solution.py:247
  31.7 1.3 %collective-permute-start.16 = (bf16[2,6,32,128]{3,2,1,0:T(8,128)(2,1)S(1)}, bf16[2,6,32,128]{3,2,1,0:T(8,128)(2,1)S(1)}, u32[]{:S(2)}, u32[]{:S(2)}) collective-permute-start(bf16[2,6,32,128]{3,2,1,0:T(8,128)(2,1)S(1)} %collective-permute-done.8.refs_8_), channel_id=1, source_target_pairs={{0,1},{1,0},{2,3},{3,2},{4,5},{5,4},{6,7},{7,6},{8,9},{9,8},{10,11... | collective-permute-start | bytes 294920 | tf_op jit(solution)/shard_map/ppermute | solution.py:247

commit v7 on v6

--- a/solution.py
+++ b/solution.py
@@ -279,11 +279,11 @@
     def hops(ks, xs):
         return [hop(x, k) for k, x in zip(ks, xs)]
 
-    ways = far[::-1] + near
+    ways = far + near
     first = hops(ways, early(ways, raw, 1))
-    second = hops(ways[:-2], early(ways[:-2], peer_raw, 0))[::-1]
+    second = hops(far, early(far, peer_raw, 0))
     *first, beside, side = tie(first)
-    first = [side, beside, *first]
+    first = [side, beside, *first[::-1]]
     brought = pl.pallas_call(
         counts_kernel,
         out_shape=jax.ShapeDtypeStruct((half, 128), jnp.int32),
@@ -313,9 +313,9 @@
     *third, own, info = late(
         far + near, small, [shape(2 * slots, orbitals, width), jax.ShapeDtypeStruct((8, 128), jnp.int32)]
     )
-    pairs = [tie((x, y)) for x, y in zip(third[: len(far)], second)]
+    pairs = [tie((x, y)) for x, y in zip(third[: len(far)], second[::-1])]
     third = [x for x, _ in pairs] + third[len(pairs) :]
-    second = [y for _, y in pairs]
+    second = [y for _, y in pairs][::-1]
     metric, own_tiles = tie((metric, own))
     factor = pl.pallas_call(
         factor_kernel,

time: 35.1 us -> 34.2 us (0.974)
  waiting for transfers between devices: 8.4 us -> 6.54 us
  starting transfers between devices: 18.9 us -> 19.8 us
    ppermute x10, waiting for transfers between devices: 5.95 us -> 4.09 us  [hop(): return lax.ppermute(x, 'aux', [(i, target(i)) for i in range(devices)])]
    ppermute x10, starting transfers between devices: 17.3 us -> 18.4 us  [hop(): return lax.ppermute(x, 'aux', [(i, target(i)) for i in range(devices)])]
  transfers between devices with their start and end apart: 17 -> 17, of which waited for: 5 -> 5; matrix products, arithmetic and copies ran while one was open for 4% -> 5% of each run, Pallas kernels for 11% -> 11%
where the time goes in v7:
time: 34.2 us; the launch traced here: 34 us
  starting transfers between devices  19.8 us (58%)
  waiting for transfers between devices  6.54 us (19%)
  Pallas kernels  5.9 us (17%)
  local copies, waits for them, and re-layouts  1.56 us (5%)
    ppermute x10, starting transfers between devices, hop(): return lax.ppermute(x, 'aux', [(i, target(i)) for i in range(devices)])  18.4 us
    ppermute x10, waiting for transfers between devices, hop(): return lax.ppermute(x, 'aux', [(i, target(i)) for i in range(devices)])  4.09 us
    ppermute x7, waiting for transfers between devices, swap(): return lax.ppermute(x, 'aux', [(i, i ^ 1) for i in range(devices)])  2.45 us
    pallas_call x1, Pallas kernels, shards(): pl.pallas_call(lambda _, *refs: blank_kernel(*refs), out_shape=jax.ShapeD...  2.3 us
    pallas_call x1, Pallas kernels, shards(): pl.pallas_call(functools.partial(exchange_kernel, chips), out_shape=jax.S...  2.05 us
    slice x1, local copies, waits for them, and re-layouts, shards(): other, raw = tie((swap(counts), raw[:, :slots - 1]))  1.55 us
    ppermute x7, starting transfers between devices, swap(): return lax.ppermute(x, 'aux', [(i, i ^ 1) for i in range(devices)])  1.4 us
    pallas_call x2, Pallas kernels, early(): pl.pallas_call(functools.partial(early_kernel, hops), out_shape=[shape((4...  0.78 us
  transfers between devices with their start and end apart: 17, of which 5 were waited for; matrix products, arithmetic and copies ran while one was open for 5% of the time, Pallas kernels for 11%

profile of v7, /device:TPU:0, one launch (start us, length us, event | category | flops | bytes accessed | tf_op | source)
XLA Modules:
  0.0 34.0 jit_solution(13013186978486891970)
XLA Ops:
  0.0 0.5 %collective-permute-start = (s32[2]{0:T(128)}, s32[2]{0:T(128)S(1)}, u32[]{:S(2)}, u32[]{:S(2)}) collective-permute-start(s32[2]{0:T(128)} %param.7), channel_id=1, source_target_pairs={{0,1},{1,0},{2,3},{3,2},{4,5},{5,4},{6,7},{7,6},{8,9},{9,8},{10,11... | collective-permute-start | bytes 32 | tf_op jit(solution)/shard_map/ppermute | solution.py:247
  0.5 1.5 %slice.4.raw_ref.own_raw = bf16[32,5,32,128]{3,2,1,0:T(8,128)(2,1)S(1)} slice(bf16[32,6,32,128]{3,2,1,0:T(8,128)(2,1)} %bitcast.5), slice={[0:32], [0:5], [0:32], [0:128]} | slice | bytes 2621440 | tf_op jit(solution)/shard_map/slice | solution.py:259
  2.0 0.0 collective-permute-done
  2.0 0.1 add_bitcast_fusion.small_ref
  2.1 0.1 collective-permute-start.6
  2.2 0.2 early.2
  2.4 5.1 %collective-permute-start.1 = (bf16[9,32,128]{2,1,0:T(8,128)(2,1)S(1)}, bf16[9,32,128]{2,1,0:T(8,128)(2,1)S(1)}, u32[]{:S(2)}, u32[]{:S(2)}) collective-permute-start(bf16[9,32,128]{2,1,0:T(8,128)(2,1)S(1)} %get-tuple-element.40), channel_id=1, source_target_pairs={{0,12},{1,15},{2,14},{3,13},{4,8},{5,11},{6,10},{7,9},{8,4},{9,7},... | collective-permute-start | bytes 221192 | tf_op jit(solution)/shard_map/ppermute | solution.py:254
  7.5 0.6 %collective-permute-start.3 = (bf16[9,32,128]{2,1,0:T(8,128)(2,1)S(1)}, bf16[9,32,128]{2,1,0:T(8,128)(2,1)S(1)}, u32[]{:S(2)}, u32[]{:S(2)}) collective-permute-start(bf16[9,32,128]{2,1,0:T(8,128)(2,1)S(1)} %get-tuple-element.42), channel_id=1, source_target_pairs={{0,4},{1,7},{2,6},{3,5},{4,0},{5,3},{6,2},{7,1},{8,12},{9,15},{10,... | collective-permute-start | bytes 221192 | tf_op jit(solution)/shard_map/ppermute | solution.py:254
  8.1 1.7 %collective-permute-start.4 = (bf16[1,32,128]{2,1,0:T(8,128)(2,1)S(1)}, bf16[1,32,128]{2,1,0:T(8,128)(2,1)S(1)}, u32[]{:S(2)}, u32[]{:S(2)}) collective-permute-start(bf16[1,32,128]{2,1,0:T(8,128)(2,1)S(1)} %get-tuple-element.43), channel_id=1, source_target_pairs={{0,2},{1,3},{2,0},{3,1},{4,6},{5,7},{6,4},{7,5},{8,10},{9,11},{10,... | collective-permute-start | bytes 24584 | tf_op jit(solution)/shard_map/ppermute | solution.py:254
  9.8 0.6 %early.3 = (bf16[8,32,128]{2,1,0:T(8,128)(2,1)S(1)}, bf16[8,32,128]{2,1,0:T(8,128)(2,1)S(1)}) custom-call(s32[1,128]{1,0:T(1,128)S(1)} %add_bitcast_fusion.small_ref, bf16[32,5,32,128]{3,2,1,0:T(8,128)(2,1)S(1)} %collective-permute-done.6.peer_raw.raw_ref), custom_call_target="tpu_custom_call" | custom-call | tf_op jit(solution)/shard_map/early/pallas_call | solution.py:269
  10.4 2.2 %collective-permute-start.7 = (bf16[8,32,128]{2,1,0:T(8,128)(2,1)S(1)}, bf16[8,32,128]{2,1,0:T(8,128)(2,1)S(1)}, u32[]{:S(2)}, u32[]{:S(2)}) collective-permute-start(bf16[8,32,128]{2,1,0:T(8,128)(2,1)S(1)} %get-tuple-element.50), channel_id=1, source_target_pairs={{0,8},{1,11},{2,10},{3,9},{4,12},{5,15},{6,14},{7,13},{8,0},{9,3},... | collective-permute-start | bytes 196616 | tf_op jit(solution)/shard_map/ppermute | solution.py:254
  12.6 0.0 collective-permute-done.4.refs_0_
  12.6 3.0 %collective-permute-start.9 = (bf16[8,32,128]{2,1,0:T(8,128)(2,1)S(1)}, bf16[8,32,128]{2,1,0:T(8,128)(2,1)S(1)}, u32[]{:S(2)}, u32[]{:S(2)}) collective-permute-start(bf16[8,32,128]{2,1,0:T(8,128)(2,1)S(1)} %get-tuple-element.53), channel_id=1, source_target_pairs={{0,12},{1,15},{2,14},{3,13},{4,8},{5,11},{6,10},{7,9},{8,4},{9,7},... | collective-permute-start | bytes 196616 | tf_op jit(solution)/shard_map/ppermute | solution.py:254
  15.6 0.0 collective-permute-done.1.refs_3_.refs_2_
  15.7 0.0 copy-start
  15.7 0.1 collective-permute-start.5
  15.7 1.1 %collective-permute-done.5.crossed_ref = s32[4,128]{1,0:T(4,128)S(1)} collective-permute-done((s32[4,128]{1,0:T(4,128)S(1)}, s32[4,128]{1,0:T(4,128)S(1)}, u32[]{:S(2)}, u32[]{:S(2)}) %collective-permute-start.5) | collective-permute-done | bytes 2080 | tf_op jit(solution)/shard_map/ppermute | solution.py:247
  16.9 0.5 %late.1 = (bf16[2,6,32,128]{3,2,1,0:T(8,128)(2,1)S(1)}, bf16[2,6,32,128]{3,2,1,0:T(8,128)(2,1)S(1)}, bf16[2,9,32,128]{3,2,1,0:T(8,128)(2,1)S(1)}, bf16[12,32,128...) custom-call(s32[1,128]{1,0:T(1,128)S(1)} %add_bitcast_fusion.small_ref, ...), custom_call_target="tpu_custom_call" | custom-call | bytes 1024 | tf_op jit(solution)/shard_map/late/pallas_call | solution.py:302
  17.4 0.2 collective-permute-start.11
  17.6 1.4 %collective-permute-start.12 = (bf16[12,32,128]{2,1,0:T(8,128)(2,1)S(1)}, bf16[12,32,128]{2,1,0:T(8,128)(2,1)S(1)}, u32[]{:S(2)}, u32[]{:S(2)}) collective-permute-start(bf16[12,32,128]{2,1,0:T(8,128)(2,1)S(1)} %get-tuple-element.56), channel_id=1, source_target_pairs={{0,2},{1,3},{2,0},{3,1},{4,6},{5,7},{6,4},{7,5},{8,10},{9,11},{10,... | collective-permute-start | bytes 294920 | tf_op jit(solution)/shard_map/ppermute | solution.py:254
  19.0 0.2 collective-permute-done.9.refs_4_
  19.2 3.1 %collective-permute-start.10 = (bf16[2,6,32,128]{3,2,1,0:T(8,128)(2,1)S(1)}, bf16[2,6,32,128]{3,2,1,0:T(8,128)(2,1)S(1)}, u32[]{:S(2)}, u32[]{:S(2)}) collective-permute-start(bf16[2,6,32,128]{3,2,1,0:T(8,128)(2,1)S(1)} %get-tuple-element.54), channel_id=1, source_target_pairs={{0,8},{1,11},{2,10},{3,9},{4,12},{5,15},{6,14},{7,13},{8,0},{9,3},... | collective-permute-start | bytes 294920 | tf_op jit(solution)/shard_map/ppermute | solution.py:254
  22.3 1.0 %collective-permute-start.8 = (bf16[2,6,32,128]{3,2,1,0:T(8,128)(2,1)S(1)}, bf16[2,6,32,128]{3,2,1,0:T(8,128)(2,1)S(1)}, u32[]{:S(2)}, u32[]{:S(2)}) collective-permute-start(bf16[2,6,32,128]{3,2,1,0:T(8,128)(2,1)S(1)} %get-tuple-element.51), channel_id=1, source_target_pairs={{0,12},{1,15},{2,14},{3,13},{4,8},{5,11},{6,10},{7,9},{8,4},{9,7},... | collective-permute-start | bytes 294920 | tf_op jit(solution)/shard_map/ppermute | solution.py:254
  23.3 0.3 collective-permute-start.13
  23.6 0.3 factor.1._.factor_ref
  23.9 2.3 %blank.1.blank_ref = f32[2,768,768]{2,1,0:T(8,128)} custom-call(bf16[256,256]{1,0:T(8,128)(2,1)S(1)} %factor.1._.factor_ref), custom_call_target="tpu_custom_call" | custom-call | tf_op jit(solution)/shard_map/blank/pallas_call | solution.py:328
  26.3 3.9 %collective-permute-done.10.refs_7_ = bf16[2,6,32,128]{3,2,1,0:T(8,128)(2,1)S(1)} collective-permute-done((bf16[2,6,32,128]{3,2,1,0:T(8,128)(2,1)S(1)}, bf16[2,6,32,128]{3,2,1,0:T(8,128)(2,1)S(1)}, u32[]{:S(2)}, u32[]{:S(2)}) %collective-permute-start.10) | collective-permute-done | bytes 98336 | tf_op jit(solution)/shard_map/ppermute | solution.py:254
  30.1 0.5 %collective-permute-start.15 = (bf16[2,6,32,128]{3,2,1,0:T(8,128)(2,1)S(1)}, bf16[2,6,32,128]{3,2,1,0:T(8,128)(2,1)S(1)}, u32[]{:S(2)}, u32[]{:S(2)}) collective-permute-start(bf16[2,6,32,128]{3,2,1,0:T(8,128)(2,1)S(1)} %collective-permute-done.10.refs_7_), channel_id=1, source_target_pairs={{0,1},{1,0},{2,3},{3,2},{4,5},{5,4},{6,7},{7,6},{8,9},{9,8},{10,11... | collective-permute-start | bytes 294920 | tf_op jit(solution)/shard_map/ppermute | solution.py:247
  30.6 0.0 collective-permute-start.16
  30.6 1.0 %collective-permute-done.15.refs_10_ = bf16[2,6,32,128]{3,2,1,0:T(8,128)(2,1)S(1)} collective-permute-done((bf16[2,6,32,128]{3,2,1,0:T(8,128)(2,1)S(1)}, bf16[2,6,32,128]{3,2,1,0:T(8,128)(2,1)S(1)}, u32[]{:S(2)}, u32[]{:S(2)}) %collective-permute-start.15) | collective-permute-done | bytes 98336 | tf_op jit(solution)/shard_map/ppermute | solution.py:247
  31.6 0.3 collective-permute-done.16.refs_11_
  31.9 2.1 %exchange.1 = f32[2,768,768]{2,1,0:T(8,128)} custom-call(f32[2,768,768]{2,1,0:T(8,128)} %blank.1.blank_ref, s32[8,128]{1,0:T(8,128)S(1)} %get-tuple-element.60.info_ref, bf16[256,256]{1,0:T(8,128)(2,1)S(1)} %factor.1._.factor_ref, bf16[12,32,128]{2,1,0:T(8,128)(2,1)S(1)} %get-tuple-element.62.self_ref, ...), custom_call_target="tpu_custom_call", output_to_operand_aliasing={{}: (0, {})} | custom-call | tf_op jit(solution)/shard_map/exchange/pallas_call | solution.py:351
  (19 shorter events, 0.1 us)
Async XLA Ops:
  0.0 2.0 %copy-start.1 = (s32[2]{0:T(128)S(1)}, s32[2]{0:T(128)}, u32[]{:S(2)}) copy-start(s32[2]{0:T(128)} %param.7) | copy-start | bytes 28
  0.0 2.0 %copy-start.2 = (s32[32]{0:T(128)S(1)}, s32[32]{0:T(128)}, u32[]{:S(2)}) copy-start(s32[32]{0:T(128)} %param.6) | copy-start | bytes 388
  0.0 2.0 %collective-permute-start = (s32[2]{0:T(128)}, s32[2]{0:T(128)S(1)}, u32[]{:S(2)}, u32[]{:S(2)}) collective-permute-start(s32[2]{0:T(128)} %param.7), channel_id=1, source_target_pairs={{0,1},{1,0},{2,3},{3,2},{4,5},{5,4},{6,7},{7,6},{8,9},{9,8},{10,11... | collective-permute-start | bytes 32 | tf_op jit(solution)/shard_map/ppermute | solution.py:247
  2.1 7.7 %collective-permute-start.6 = (bf16[32,5,32,128]{3,2,1,0:T(8,128)(2,1)S(1)}, bf16[32,5,32,128]{3,2,1,0:T(8,128)(2,1)S(1)}, u32[]{:S(2)}, u32[]{:S(2)}) collective-permute-start(bf16[32,5,32,128]{3,2,1,0:T(8,128)(2,1)S(1)} %slice.4.raw_ref.own_raw), channel_id=1, source_target_pairs={{0,1},{1,0},{2,3},{3,2},{4,5},{5,4},{6,7},{7,6},{8,9},{9,8},{10,11... | collective-permute-start | bytes 3932168 | tf_op jit(solution)/shard_map/ppermute | solution.py:247
  2.4 13.3 %collective-permute-start.1 = (bf16[9,32,128]{2,1,0:T(8,128)(2,1)S(1)}, bf16[9,32,128]{2,1,0:T(8,128)(2,1)S(1)}, u32[]{:S(2)}, u32[]{:S(2)}) collective-permute-start(bf16[9,32,128]{2,1,0:T(8,128)(2,1)S(1)} %get-tuple-element.40), channel_id=1, source_target_pairs={{0,12},{1,15},{2,14},{3,13},{4,8},{5,11},{6,10},{7,9},{8,4},{9,7},... | collective-permute-start | bytes 221192 | tf_op jit(solution)/shard_map/ppermute | solution.py:254
  7.5 8.2 %collective-permute-start.2 = (bf16[9,32,128]{2,1,0:T(8,128)(2,1)S(1)}, bf16[9,32,128]{2,1,0:T(8,128)(2,1)S(1)}, u32[]{:S(2)}, u32[]{:S(2)}) collective-permute-start(bf16[9,32,128]{2,1,0:T(8,128)(2,1)S(1)} %get-tuple-element.41), channel_id=1, source_target_pairs={{0,8},{1,11},{2,10},{3,9},{4,12},{5,15},{6,14},{7,13},{8,0},{9,3},... | collective-permute-start | bytes 221192 | tf_op jit(solution)/shard_map/ppermute | solution.py:254
  7.5 8.2 %collective-permute-start.3 = (bf16[9,32,128]{2,1,0:T(8,128)(2,1)S(1)}, bf16[9,32,128]{2,1,0:T(8,128)(2,1)S(1)}, u32[]{:S(2)}, u32[]{:S(2)}) collective-permute-start(bf16[9,32,128]{2,1,0:T(8,128)(2,1)S(1)} %get-tuple-element.42), channel_id=1, source_target_pairs={{0,4},{1,7},{2,6},{3,5},{4,0},{5,3},{6,2},{7,1},{8,12},{9,15},{10,... | collective-permute-start | bytes 221192 | tf_op jit(solution)/shard_map/ppermute | solution.py:254
  8.1 4.5 %collective-permute-start.4 = (bf16[1,32,128]{2,1,0:T(8,128)(2,1)S(1)}, bf16[1,32,128]{2,1,0:T(8,128)(2,1)S(1)}, u32[]{:S(2)}, u32[]{:S(2)}) collective-permute-start(bf16[1,32,128]{2,1,0:T(8,128)(2,1)S(1)} %get-tuple-element.43), channel_id=1, source_target_pairs={{0,2},{1,3},{2,0},{3,1},{4,6},{5,7},{6,4},{7,5},{8,10},{9,11},{10,... | collective-permute-start | bytes 24584 | tf_op jit(solution)/shard_map/ppermute | solution.py:254
  10.4 8.6 %collective-permute-start.7 = (bf16[8,32,128]{2,1,0:T(8,128)(2,1)S(1)}, bf16[8,32,128]{2,1,0:T(8,128)(2,1)S(1)}, u32[]{:S(2)}, u32[]{:S(2)}) collective-permute-start(bf16[8,32,128]{2,1,0:T(8,128)(2,1)S(1)} %get-tuple-element.50), channel_id=1, source_target_pairs={{0,8},{1,11},{2,10},{3,9},{4,12},{5,15},{6,14},{7,13},{8,0},{9,3},... | collective-permute-start | bytes 196616 | tf_op jit(solution)/shard_map/ppermute | solution.py:254
  12.6 6.6 %collective-permute-start.9 = (bf16[8,32,128]{2,1,0:T(8,128)(2,1)S(1)}, bf16[8,32,128]{2,1,0:T(8,128)(2,1)S(1)}, u32[]{:S(2)}, u32[]{:S(2)}) collective-permute-start(bf16[8,32,128]{2,1,0:T(8,128)(2,1)S(1)} %get-tuple-element.53), channel_id=1, source_target_pairs={{0,12},{1,15},{2,14},{3,13},{4,8},{5,11},{6,10},{7,9},{8,4},{9,7},... | collective-permute-start | bytes 196616 | tf_op jit(solution)/shard_map/ppermute | solution.py:254
  15.7 8.0 %copy-start = (bf16[16,16]{1,0:T(8,128)(2,1)S(1)}, bf16[16,16]{1,0:T(8,128)(2,1)}, u32[]{:S(2)}) copy-start(bf16[16,16]{1,0:T(8,128)(2,1)} %metric_ref) | copy-start | bytes 1540
  15.7 1.2 %collective-permute-start.5 = (s32[4,128]{1,0:T(4,128)S(1)}, s32[4,128]{1,0:T(4,128)S(1)}, u32[]{:S(2)}, u32[]{:S(2)}) collective-permute-start(s32[4,128]{1,0:T(4,128)S(1)} %counts.1.counts_ref), channel_id=1, source_target_pairs={{0,1},{1,0},{2,3},{3,2},{4,5},{5,4},{6,7},{7,6},{8,9},{9,8},{10,11... | collective-permute-start | bytes 6152 | tf_op jit(solution)/shard_map/ppermute | solution.py:247
  17.4 8.9 %collective-permute-start.11 = (bf16[2,9,32,128]{3,2,1,0:T(8,128)(2,1)S(1)}, bf16[2,9,32,128]{3,2,1,0:T(8,128)(2,1)S(1)}, u32[]{:S(2)}, u32[]{:S(2)}) collective-permute-start(bf16[2,9,32,128]{3,2,1,0:T(8,128)(2,1)S(1)} %get-tuple-element.55), channel_id=1, source_target_pairs={{0,4},{1,7},{2,6},{3,5},{4,0},{5,3},{6,2},{7,1},{8,12},{9,15},{10,... | collective-permute-start | bytes 442376 | tf_op jit(solution)/shard_map/ppermute | solution.py:254
  17.6 8.7 %collective-permute-start.12 = (bf16[12,32,128]{2,1,0:T(8,128)(2,1)S(1)}, bf16[12,32,128]{2,1,0:T(8,128)(2,1)S(1)}, u32[]{:S(2)}, u32[]{:S(2)}) collective-permute-start(bf16[12,32,128]{2,1,0:T(8,128)(2,1)S(1)} %get-tuple-element.56), channel_id=1, source_target_pairs={{0,2},{1,3},{2,0},{3,1},{4,6},{5,7},{6,4},{7,5},{8,10},{9,11},{10,... | collective-permute-start | bytes 294920 | tf_op jit(solution)/shard_map/ppermute | solution.py:254
  19.2 10.9 %collective-permute-start.10 = (bf16[2,6,32,128]{3,2,1,0:T(8,128)(2,1)S(1)}, bf16[2,6,32,128]{3,2,1,0:T(8,128)(2,1)S(1)}, u32[]{:S(2)}, u32[]{:S(2)}) collective-permute-start(bf16[2,6,32,128]{3,2,1,0:T(8,128)(2,1)S(1)} %get-tuple-element.54), channel_id=1, source_target_pairs={{0,8},{1,11},{2,10},{3,9},{4,12},{5,15},{6,14},{7,13},{8,0},{9,3},... | collective-permute-start | bytes 294920 | tf_op jit(solution)/shard_map/ppermute | solution.py:254
  22.3 7.8 %collective-permute-start.8 = (bf16[2,6,32,128]{3,2,1,0:T(8,128)(2,1)S(1)}, bf16[2,6,32,128]{3,2,1,0:T(8,128)(2,1)S(1)}, u32[]{:S(2)}, u32[]{:S(2)}) collective-permute-start(bf16[2,6,32,128]{3,2,1,0:T(8,128)(2,1)S(1)} %get-tuple-element.51), channel_id=1, source_target_pairs={{0,12},{1,15},{2,14},{3,13},{4,8},{5,11},{6,10},{7,9},{8,4},{9,7},... | collective-permute-start | bytes 294920 | tf_op jit(solution)/shard_map/ppermute | solution.py:254
  23.3 7.3 %collective-permute-start.13 = (bf16[20,32,128]{2,1,0:T(8,128)(2,1)S(1)}, bf16[20,32,128]{2,1,0:T(8,128)(2,1)S(1)}, u32[]{:S(2)}, u32[]{:S(2)}) collective-permute-start(bf16[20,32,128]{2,1,0:T(8,128)(2,1)S(1)} %forward.1), channel_id=1, source_target_pairs={{0,1},{1,0},{2,3},{3,2},{4,5},{5,4},{6,7},{7,6},{8,9},{9,8},{10,11... | collective-permute-start | bytes 491528 | tf_op jit(solution)/shard_map/ppermute | solution.py:247
  30.1 1.8 %collective-permute-start.14 = (bf16[2,9,32,128]{3,2,1,0:T(8,128)(2,1)S(1)}, bf16[2,9,32,128]{3,2,1,0:T(8,128)(2,1)S(1)}, u32[]{:S(2)}, u32[]{:S(2)}) collective-permute-start(bf16[2,9,32,128]{3,2,1,0:T(8,128)(2,1)S(1)} %collective-permute-done.11.refs_6_), channel_id=1, source_target_pairs={{0,1},{1,0},{2,3},{3,2},{4,5},{5,4},{6,7},{7,6},{8,9},{9,8},{10,11... | collective-permute-start | bytes 442376 | tf_op jit(solution)/shard_map/ppermute | solution.py:247
  30.1 1.5 %collective-permute-start.15 = (bf16[2,6,32,128]{3,2,1,0:T(8,128)(2,1)S(1)}, bf16[2,6,32,128]{3,2,1,0:T(8,128)(2,1)S(1)}, u32[]{:S(2)}, u32[]{:S(2)}) collective-permute-start(bf16[2,6,32,128]{3,2,1,0:T(8,128)(2,1)S(1)} %collective-permute-done.10.refs_7_), channel_id=1, source_target_pairs={{0,1},{1,0},{2,3},{3,2},{4,5},{5,4},{6,7},{7,6},{8,9},{9,8},{10,11... | collective-permute-start | bytes 294920 | tf_op jit(solution)/shard_map/ppermute | solution.py:247
  30.6 1.3 %collective-permute-start.16 = (bf16[2,6,32,128]{3,2,1,0:T(8,128)(2,1)S(1)}, bf16[2,6,32,128]{3,2,1,0:T(8,128)(2,1)S(1)}, u32[]{:S(2)}, u32[]{:S(2)}) collective-permute-start(bf16[2,6,32,128]{3,2,1,0:T(8,128)(2,1)S(1)} %collective-permute-done.8.refs_8_), channel_id=1, source_target_pairs={{0,1},{1,0},{2,3},{3,2},{4,5},{5,4},{6,7},{7,6},{8,9},{9,8},{10,11... | collective-permute-start | bytes 294920 | tf_op jit(solution)/shard_map/ppermute | solution.py:247

commit v8 on v7

--- a/solution.py
+++ b/solution.py
@@ -49,15 +49,8 @@
 
 
 def early_kernel(hops, small_ref, raw_ref, *refs):
-    *outs, held, ids, sem = refs
-    if outs[0].shape[0] % 2:
-        place_blocks(small_ref, held)
-    else:
-        copy = pltpu.make_async_copy(small_ref, ids, sem)
-        copy.start()
-        copy.wait()
-        for o in range(held.shape[0]):
-            held[ids[0, o]] = o
+    *outs, held = refs
+    place_blocks(small_ref, held)
     blocks, tile = raw_ref.shape[0], raw_ref.shape[2]
     chip, core = position()
     lane = lax.broadcasted_iota(jnp.int32, (tile, 128), 1)
@@ -224,7 +217,7 @@
                             )
                         )
 
-    for group in (range(slots - 2), range(slots - 2, slots)):
+    for group in [range(n, n + 2) for n in range(0, slots, 2)]:
         for s in group:
             stage[span(s), :] = lax.dot_general(
                 rows[:, span(s)], rows[...], (((0,), (0,)), ((), ())), preferred_element_type=jnp.float32
@@ -259,7 +252,15 @@
     other, raw = tie((swap(counts), raw[:, : slots - 1]))
     small = jnp.concatenate([owner_map, counts, other, jnp.zeros((lines - blocks - 4,), jnp.int32)]).reshape(1, lines)
     raw_there, small = tie((raw, small))
-    peer_raw = swap(raw_there)
+    factor = pl.pallas_call(
+        factor_kernel,
+        out_shape=shape(devices * GROUP, devices * GROUP),
+        in_specs=[VMEM],
+        out_specs=VMEM,
+        compiler_params=LIMIT,
+        name="factor",
+    )(metric)
+    peer_raw, factor = tie((swap(raw_there), factor))
 
     far = [*reversed(range(2, half))]
     near = [1, 0]
@@ -271,7 +272,7 @@
             out_shape=[shape((4 * EARLY if k else 0) + counted, orbitals, width) for k in hops],
             in_specs=[VMEM] * 2,
             out_specs=[VMEM] * len(hops),
-            scratch_shapes=[place, pltpu.SMEM((1, lines), jnp.int32), pltpu.SemaphoreType.DMA(())],
+            scratch_shapes=[place],
             compiler_params=LIMIT,
             name="early",
         )(small, raw)
@@ -316,15 +317,7 @@
     pairs = [tie((x, y)) for x, y in zip(third[: len(far)], second[::-1])]
     third = [x for x, _ in pairs] + third[len(pairs) :]
     second = [y for _, y in pairs][::-1]
-    metric, own_tiles = tie((metric, own))
-    factor = pl.pallas_call(
-        factor_kernel,
-        out_shape=shape(devices * GROUP, devices * GROUP),
-        in_specs=[VMEM],
-        out_specs=VMEM,
-        compiler_params=LIMIT,
-        name="factor",
-    )(metric)
+    own_tiles = own
     blank = pl.pallas_call(
         lambda _, *refs: blank_kernel(*refs),
         out_shape=jax.ShapeDtypeStruct((2, slots * width, slots * width), jnp.float32),
@@ -333,8 +326,8 @@
         scratch_shapes=[pltpu.VMEM((width, slots * width), jnp.float32), pltpu.SemaphoreType.DMA((2, slots))],
         compiler_params=LIMIT,
         name="blank",
-    )(factor)
-    *third, factor, blank = tie(hops(far + near, third) + [factor, blank])
+    )(info)
+    *third, blank = tie(hops(far + near, third) + [blank])
     third = third[::-1]
     second = second[::-1]
     forwarded = pl.pallas_call(

time: 34.2 us -> 34.2 us (level)
  Pallas kernels: 5.9 us -> 5.43 us
    pallas_call x2, Pallas kernels: 0.78 us -> 0.32 us  [early(): pl.pallas_call(functools.partial(early_kernel, hops), out_shape=[shape((4...]
  transfers between devices with their start and end apart: 17 -> 17, of which waited for: 5 -> 5; matrix products, arithmetic and copies ran while one was open for 5% -> 5% of each run, Pallas kernels for 11% -> 10%
where the time goes in v8:
time: 34.2 us; the launch traced here: 34.1 us
  starting transfers between devices  20.1 us (59%)
  waiting for transfers between devices  6.79 us (20%)
  Pallas kernels  5.43 us (16%)
  local copies, waits for them, and re-layouts  1.57 us (5%)
    ppermute x10, starting transfers between devices, hop(): return lax.ppermute(x, 'aux', [(i, target(i)) for i in range(devices)])  18.7 us
    ppermute x10, waiting for transfers between devices, hop(): return lax.ppermute(x, 'aux', [(i, target(i)) for i in range(devices)])  4.35 us
    ppermute x7, waiting for transfers between devices, swap(): return lax.ppermute(x, 'aux', [(i, i ^ 1) for i in range(devices)])  2.45 us
    pallas_call x1, Pallas kernels, shards(): pl.pallas_call(lambda _, *refs: blank_kernel(*refs), out_shape=jax.ShapeD...  2.3 us
    pallas_call x1, Pallas kernels, shards(): pl.pallas_call(functools.partial(exchange_kernel, chips), out_shape=jax.S...  2.04 us
    slice x1, local copies, waits for them, and re-layouts, shards(): other, raw = tie((swap(counts), raw[:, :slots - 1]))  1.56 us
    ppermute x7, starting transfers between devices, swap(): return lax.ppermute(x, 'aux', [(i, i ^ 1) for i in range(devices)])  1.4 us
  transfers between devices with their start and end apart: 17, of which 5 were waited for; matrix products, arithmetic and copies ran while one was open for 5% of the time, Pallas kernels for 10%

profile of v8, /device:TPU:0, one launch (start us, length us, event | category | flops | bytes accessed | tf_op | source)
XLA Modules:
  0.0 34.1 jit_solution(16743815709776881087)
XLA Ops:
  0.0 0.5 %collective-permute-start = (s32[2]{0:T(128)}, s32[2]{0:T(128)S(1)}, u32[]{:S(2)}, u32[]{:S(2)}) collective-permute-start(s32[2]{0:T(128)} %param.7), channel_id=1, source_target_pairs={{0,1},{1,0},{2,3},{3,2},{4,5},{5,4},{6,7},{7,6},{8,9},{9,8},{10,11... | collective-permute-start | bytes 32 | tf_op jit(solution)/shard_map/ppermute | solution.py:240
  0.5 1.6 %slice.4.raw_ref.own_raw = bf16[32,5,32,128]{3,2,1,0:T(8,128)(2,1)S(1)} slice(bf16[32,6,32,128]{3,2,1,0:T(8,128)(2,1)} %bitcast.5), slice={[0:32], [0:5], [0:32], [0:128]} | slice | bytes 2621440 | tf_op jit(solution)/shard_map/slice | solution.py:252
  2.1 0.1 add_bitcast_fusion.small_ref
  2.1 0.1 collective-permute-start.6
  2.2 0.2 early.2
  2.4 5.1 %collective-permute-start.1 = (bf16[9,32,128]{2,1,0:T(8,128)(2,1)S(1)}, bf16[9,32,128]{2,1,0:T(8,128)(2,1)S(1)}, u32[]{:S(2)}, u32[]{:S(2)}) collective-permute-start(bf16[9,32,128]{2,1,0:T(8,128)(2,1)S(1)} %get-tuple-element.39), channel_id=1, source_target_pairs={{0,12},{1,15},{2,14},{3,13},{4,8},{5,11},{6,10},{7,9},{8,4},{9,7},... | collective-permute-start | bytes 221192 | tf_op jit(solution)/shard_map/ppermute | solution.py:247
  7.5 0.6 %collective-permute-start.3 = (bf16[9,32,128]{2,1,0:T(8,128)(2,1)S(1)}, bf16[9,32,128]{2,1,0:T(8,128)(2,1)S(1)}, u32[]{:S(2)}, u32[]{:S(2)}) collective-permute-start(bf16[9,32,128]{2,1,0:T(8,128)(2,1)S(1)} %get-tuple-element.41), channel_id=1, source_target_pairs={{0,4},{1,7},{2,6},{3,5},{4,0},{5,3},{6,2},{7,1},{8,12},{9,15},{10,... | collective-permute-start | bytes 221192 | tf_op jit(solution)/shard_map/ppermute | solution.py:247
  8.1 1.7 %collective-permute-start.4 = (bf16[1,32,128]{2,1,0:T(8,128)(2,1)S(1)}, bf16[1,32,128]{2,1,0:T(8,128)(2,1)S(1)}, u32[]{:S(2)}, u32[]{:S(2)}) collective-permute-start(bf16[1,32,128]{2,1,0:T(8,128)(2,1)S(1)} %get-tuple-element.42), channel_id=1, source_target_pairs={{0,2},{1,3},{2,0},{3,1},{4,6},{5,7},{6,4},{7,5},{8,10},{9,11},{10,... | collective-permute-start | bytes 24584 | tf_op jit(solution)/shard_map/ppermute | solution.py:247
  9.8 0.3 factor.1.factor_ref
  10.1 0.0 collective-permute-done.6.peer_raw.raw_ref
  10.1 0.2 early.3
  10.3 2.2 %collective-permute-start.7 = (bf16[8,32,128]{2,1,0:T(8,128)(2,1)S(1)}, bf16[8,32,128]{2,1,0:T(8,128)(2,1)S(1)}, u32[]{:S(2)}, u32[]{:S(2)}) collective-permute-start(bf16[8,32,128]{2,1,0:T(8,128)(2,1)S(1)} %get-tuple-element.50), channel_id=1, source_target_pairs={{0,8},{1,11},{2,10},{3,9},{4,12},{5,15},{6,14},{7,13},{8,0},{9,3},... | collective-permute-start | bytes 196616 | tf_op jit(solution)/shard_map/ppermute | solution.py:247
  12.5 0.0 collective-permute-done.4.refs_0_
  12.5 3.1 %collective-permute-start.9 = (bf16[8,32,128]{2,1,0:T(8,128)(2,1)S(1)}, bf16[8,32,128]{2,1,0:T(8,128)(2,1)S(1)}, u32[]{:S(2)}, u32[]{:S(2)}) collective-permute-start(bf16[8,32,128]{2,1,0:T(8,128)(2,1)S(1)} %get-tuple-element.53), channel_id=1, source_target_pairs={{0,12},{1,15},{2,14},{3,13},{4,8},{5,11},{6,10},{7,9},{8,4},{9,7},... | collective-permute-start | bytes 196616 | tf_op jit(solution)/shard_map/ppermute | solution.py:247
  15.6 0.0 collective-permute-done.1.refs_3_.refs_2_
  15.6 0.0 collective-permute-done.2.refs_2_.refs_1_
  15.7 0.1 collective-permute-start.5
  15.7 1.1 %collective-permute-done.5.crossed_ref = s32[4,128]{1,0:T(4,128)S(1)} collective-permute-done((s32[4,128]{1,0:T(4,128)S(1)}, s32[4,128]{1,0:T(4,128)S(1)}, u32[]{:S(2)}, u32[]{:S(2)}) %collective-permute-start.5) | collective-permute-done | bytes 2080 | tf_op jit(solution)/shard_map/ppermute | solution.py:240
  16.9 0.5 %late.1 = (bf16[2,6,32,128]{3,2,1,0:T(8,128)(2,1)S(1)}, bf16[2,6,32,128]{3,2,1,0:T(8,128)(2,1)S(1)}, bf16[2,9,32,128]{3,2,1,0:T(8,128)(2,1)S(1)}, bf16[12,32,128...) custom-call(s32[1,128]{1,0:T(1,128)S(1)} %add_bitcast_fusion.small_ref, ...), custom_call_target="tpu_custom_call" | custom-call | bytes 1024 | tf_op jit(solution)/shard_map/late/pallas_call | solution.py:303
  17.4 0.2 collective-permute-start.11
  17.5 1.5 %collective-permute-start.12 = (bf16[12,32,128]{2,1,0:T(8,128)(2,1)S(1)}, bf16[12,32,128]{2,1,0:T(8,128)(2,1)S(1)}, u32[]{:S(2)}, u32[]{:S(2)}) collective-permute-start(bf16[12,32,128]{2,1,0:T(8,128)(2,1)S(1)} %get-tuple-element.56), channel_id=1, source_target_pairs={{0,2},{1,3},{2,0},{3,1},{4,6},{5,7},{6,4},{7,5},{8,10},{9,11},{10,... | collective-permute-start | bytes 294920 | tf_op jit(solution)/shard_map/ppermute | solution.py:247
  19.0 0.1 collective-permute-done.9.refs_4_
  19.1 3.3 %collective-permute-start.10 = (bf16[2,6,32,128]{3,2,1,0:T(8,128)(2,1)S(1)}, bf16[2,6,32,128]{3,2,1,0:T(8,128)(2,1)S(1)}, u32[]{:S(2)}, u32[]{:S(2)}) collective-permute-start(bf16[2,6,32,128]{3,2,1,0:T(8,128)(2,1)S(1)} %get-tuple-element.54), channel_id=1, source_target_pairs={{0,8},{1,11},{2,10},{3,9},{4,12},{5,15},{6,14},{7,13},{8,0},{9,3},... | collective-permute-start | bytes 294920 | tf_op jit(solution)/shard_map/ppermute | solution.py:247
  22.4 1.0 %collective-permute-start.8 = (bf16[2,6,32,128]{3,2,1,0:T(8,128)(2,1)S(1)}, bf16[2,6,32,128]{3,2,1,0:T(8,128)(2,1)S(1)}, u32[]{:S(2)}, u32[]{:S(2)}) collective-permute-start(bf16[2,6,32,128]{3,2,1,0:T(8,128)(2,1)S(1)} %get-tuple-element.51), channel_id=1, source_target_pairs={{0,12},{1,15},{2,14},{3,13},{4,8},{5,11},{6,10},{7,9},{8,4},{9,7},... | collective-permute-start | bytes 294920 | tf_op jit(solution)/shard_map/ppermute | solution.py:247
  23.3 0.3 collective-permute-start.13
  23.6 2.3 %blank.1.blank_ref = f32[2,768,768]{2,1,0:T(8,128)} custom-call(s32[8,128]{1,0:T(8,128)S(1)} %get-tuple-element.57._.info_ref), custom_call_target="tpu_custom_call" | custom-call | tf_op jit(solution)/shard_map/blank/pallas_call | solution.py:321
  26.0 4.2 %collective-permute-done.10.refs_7_ = bf16[2,6,32,128]{3,2,1,0:T(8,128)(2,1)S(1)} collective-permute-done((bf16[2,6,32,128]{3,2,1,0:T(8,128)(2,1)S(1)}, bf16[2,6,32,128]{3,2,1,0:T(8,128)(2,1)S(1)}, u32[]{:S(2)}, u32[]{:S(2)}) %collective-permute-start.10) | collective-permute-done | bytes 98336 | tf_op jit(solution)/shard_map/ppermute | solution.py:247
  30.2 0.5 %collective-permute-start.15 = (bf16[2,6,32,128]{3,2,1,0:T(8,128)(2,1)S(1)}, bf16[2,6,32,128]{3,2,1,0:T(8,128)(2,1)S(1)}, u32[]{:S(2)}, u32[]{:S(2)}) collective-permute-start(bf16[2,6,32,128]{3,2,1,0:T(8,128)(2,1)S(1)} %collective-permute-done.10.refs_7_), channel_id=1, source_target_pairs={{0,1},{1,0},{2,3},{3,2},{4,5},{5,4},{6,7},{7,6},{8,9},{9,8},{10,11... | collective-permute-start | bytes 294920 | tf_op jit(solution)/shard_map/ppermute | solution.py:240
  30.7 0.0 collective-permute-start.16
  30.7 1.0 %collective-permute-done.15.refs_10_ = bf16[2,6,32,128]{3,2,1,0:T(8,128)(2,1)S(1)} collective-permute-done((bf16[2,6,32,128]{3,2,1,0:T(8,128)(2,1)S(1)}, bf16[2,6,32,128]{3,2,1,0:T(8,128)(2,1)S(1)}, u32[]{:S(2)}, u32[]{:S(2)}) %collective-permute-start.15) | collective-permute-done | bytes 98336 | tf_op jit(solution)/shard_map/ppermute | solution.py:240
  31.7 0.3 collective-permute-done.16.refs_11_
  32.0 2.0 %exchange.1 = f32[2,768,768]{2,1,0:T(8,128)} custom-call(f32[2,768,768]{2,1,0:T(8,128)} %blank.1.blank_ref, s32[8,128]{1,0:T(8,128)S(1)} %get-tuple-element.57._.info_ref, bf16[256,256]{1,0:T(8,128)(2,1)S(1)} %factor.1.factor_ref, bf16[12,32,128]{2,1,0:T(8,128)(2,1)S(1)} %get-tuple-element.60.self_ref, ...), custom_call_target="tpu_custom_call", output_to_operand_aliasing={{}: (0, {})} | custom-call | tf_op jit(solution)/shard_map/exchange/pallas_call | solution.py:344
  (19 shorter events, 0.1 us)
Async XLA Ops:
  0.0 2.0 %copy-start.1 = (s32[2]{0:T(128)S(1)}, s32[2]{0:T(128)}, u32[]{:S(2)}) copy-start(s32[2]{0:T(128)} %param.7) | copy-start | bytes 28
  0.0 2.1 %copy-start.2 = (s32[32]{0:T(128)S(1)}, s32[32]{0:T(128)}, u32[]{:S(2)}) copy-start(s32[32]{0:T(128)} %param.6) | copy-start | bytes 388
  0.0 2.0 %collective-permute-start = (s32[2]{0:T(128)}, s32[2]{0:T(128)S(1)}, u32[]{:S(2)}, u32[]{:S(2)}) collective-permute-start(s32[2]{0:T(128)} %param.7), channel_id=1, source_target_pairs={{0,1},{1,0},{2,3},{3,2},{4,5},{5,4},{6,7},{7,6},{8,9},{9,8},{10,11... | collective-permute-start | bytes 32 | tf_op jit(solution)/shard_map/ppermute | solution.py:240
  0.5 9.3 %copy-start = (bf16[16,16]{1,0:T(8,128)(2,1)S(1)}, bf16[16,16]{1,0:T(8,128)(2,1)}, u32[]{:S(2)}) copy-start(bf16[16,16]{1,0:T(8,128)(2,1)} %metric_ref.1) | copy-start | bytes 1540
  2.1 8.0 %collective-permute-start.6 = (bf16[32,5,32,128]{3,2,1,0:T(8,128)(2,1)S(1)}, bf16[32,5,32,128]{3,2,1,0:T(8,128)(2,1)S(1)}, u32[]{:S(2)}, u32[]{:S(2)}) collective-permute-start(bf16[32,5,32,128]{3,2,1,0:T(8,128)(2,1)S(1)} %slice.4.raw_ref.own_raw), channel_id=1, source_target_pairs={{0,1},{1,0},{2,3},{3,2},{4,5},{5,4},{6,7},{7,6},{8,9},{9,8},{10,11... | collective-permute-start | bytes 3932168 | tf_op jit(solution)/shard_map/ppermute | solution.py:240
  2.4 13.3 %collective-permute-start.1 = (bf16[9,32,128]{2,1,0:T(8,128)(2,1)S(1)}, bf16[9,32,128]{2,1,0:T(8,128)(2,1)S(1)}, u32[]{:S(2)}, u32[]{:S(2)}) collective-permute-start(bf16[9,32,128]{2,1,0:T(8,128)(2,1)S(1)} %get-tuple-element.39), channel_id=1, source_target_pairs={{0,12},{1,15},{2,14},{3,13},{4,8},{5,11},{6,10},{7,9},{8,4},{9,7},... | collective-permute-start | bytes 221192 | tf_op jit(solution)/shard_map/ppermute | solution.py:247
  7.5 8.2 %collective-permute-start.2 = (bf16[9,32,128]{2,1,0:T(8,128)(2,1)S(1)}, bf16[9,32,128]{2,1,0:T(8,128)(2,1)S(1)}, u32[]{:S(2)}, u32[]{:S(2)}) collective-permute-start(bf16[9,32,128]{2,1,0:T(8,128)(2,1)S(1)} %get-tuple-element.40), channel_id=1, source_target_pairs={{0,8},{1,11},{2,10},{3,9},{4,12},{5,15},{6,14},{7,13},{8,0},{9,3},... | collective-permute-start | bytes 221192 | tf_op jit(solution)/shard_map/ppermute | solution.py:247
  7.5 8.2 %collective-permute-start.3 = (bf16[9,32,128]{2,1,0:T(8,128)(2,1)S(1)}, bf16[9,32,128]{2,1,0:T(8,128)(2,1)S(1)}, u32[]{:S(2)}, u32[]{:S(2)}) collective-permute-start(bf16[9,32,128]{2,1,0:T(8,128)(2,1)S(1)} %get-tuple-element.41), channel_id=1, source_target_pairs={{0,4},{1,7},{2,6},{3,5},{4,0},{5,3},{6,2},{7,1},{8,12},{9,15},{10,... | collective-permute-start | bytes 221192 | tf_op jit(solution)/shard_map/ppermute | solution.py:247
  8.1 4.4 %collective-permute-start.4 = (bf16[1,32,128]{2,1,0:T(8,128)(2,1)S(1)}, bf16[1,32,128]{2,1,0:T(8,128)(2,1)S(1)}, u32[]{:S(2)}, u32[]{:S(2)}) collective-permute-start(bf16[1,32,128]{2,1,0:T(8,128)(2,1)S(1)} %get-tuple-element.42), channel_id=1, source_target_pairs={{0,2},{1,3},{2,0},{3,1},{4,6},{5,7},{6,4},{7,5},{8,10},{9,11},{10,... | collective-permute-start | bytes 24584 | tf_op jit(solution)/shard_map/ppermute | solution.py:247
  10.3 8.7 %collective-permute-start.7 = (bf16[8,32,128]{2,1,0:T(8,128)(2,1)S(1)}, bf16[8,32,128]{2,1,0:T(8,128)(2,1)S(1)}, u32[]{:S(2)}, u32[]{:S(2)}) collective-permute-start(bf16[8,32,128]{2,1,0:T(8,128)(2,1)S(1)} %get-tuple-element.50), channel_id=1, source_target_pairs={{0,8},{1,11},{2,10},{3,9},{4,12},{5,15},{6,14},{7,13},{8,0},{9,3},... | collective-permute-start | bytes 196616 | tf_op jit(solution)/shard_map/ppermute | solution.py:247
  12.5 6.6 %collective-permute-start.9 = (bf16[8,32,128]{2,1,0:T(8,128)(2,1)S(1)}, bf16[8,32,128]{2,1,0:T(8,128)(2,1)S(1)}, u32[]{:S(2)}, u32[]{:S(2)}) collective-permute-start(bf16[8,32,128]{2,1,0:T(8,128)(2,1)S(1)} %get-tuple-element.53), channel_id=1, source_target_pairs={{0,12},{1,15},{2,14},{3,13},{4,8},{5,11},{6,10},{7,9},{8,4},{9,7},... | collective-permute-start | bytes 196616 | tf_op jit(solution)/shard_map/ppermute | solution.py:247
  15.7 1.2 %collective-permute-start.5 = (s32[4,128]{1,0:T(4,128)S(1)}, s32[4,128]{1,0:T(4,128)S(1)}, u32[]{:S(2)}, u32[]{:S(2)}) collective-permute-start(s32[4,128]{1,0:T(4,128)S(1)} %counts.1.counts_ref), channel_id=1, source_target_pairs={{0,1},{1,0},{2,3},{3,2},{4,5},{5,4},{6,7},{7,6},{8,9},{9,8},{10,11... | collective-permute-start | bytes 6152 | tf_op jit(solution)/shard_map/ppermute | solution.py:240
  17.4 8.6 %collective-permute-start.11 = (bf16[2,9,32,128]{3,2,1,0:T(8,128)(2,1)S(1)}, bf16[2,9,32,128]{3,2,1,0:T(8,128)(2,1)S(1)}, u32[]{:S(2)}, u32[]{:S(2)}) collective-permute-start(bf16[2,9,32,128]{3,2,1,0:T(8,128)(2,1)S(1)} %get-tuple-element.55), channel_id=1, source_target_pairs={{0,4},{1,7},{2,6},{3,5},{4,0},{5,3},{6,2},{7,1},{8,12},{9,15},{10,... | collective-permute-start | bytes 442376 | tf_op jit(solution)/shard_map/ppermute | solution.py:247
  17.5 8.4 %collective-permute-start.12 = (bf16[12,32,128]{2,1,0:T(8,128)(2,1)S(1)}, bf16[12,32,128]{2,1,0:T(8,128)(2,1)S(1)}, u32[]{:S(2)}, u32[]{:S(2)}) collective-permute-start(bf16[12,32,128]{2,1,0:T(8,128)(2,1)S(1)} %get-tuple-element.56), channel_id=1, source_target_pairs={{0,2},{1,3},{2,0},{3,1},{4,6},{5,7},{6,4},{7,5},{8,10},{9,11},{10,... | collective-permute-start | bytes 294920 | tf_op jit(solution)/shard_map/ppermute | solution.py:247
  19.1 11.1 %collective-permute-start.10 = (bf16[2,6,32,128]{3,2,1,0:T(8,128)(2,1)S(1)}, bf16[2,6,32,128]{3,2,1,0:T(8,128)(2,1)S(1)}, u32[]{:S(2)}, u32[]{:S(2)}) collective-permute-start(bf16[2,6,32,128]{3,2,1,0:T(8,128)(2,1)S(1)} %get-tuple-element.54), channel_id=1, source_target_pairs={{0,8},{1,11},{2,10},{3,9},{4,12},{5,15},{6,14},{7,13},{8,0},{9,3},... | collective-permute-start | bytes 294920 | tf_op jit(solution)/shard_map/ppermute | solution.py:247
  22.4 7.8 %collective-permute-start.8 = (bf16[2,6,32,128]{3,2,1,0:T(8,128)(2,1)S(1)}, bf16[2,6,32,128]{3,2,1,0:T(8,128)(2,1)S(1)}, u32[]{:S(2)}, u32[]{:S(2)}) collective-permute-start(bf16[2,6,32,128]{3,2,1,0:T(8,128)(2,1)S(1)} %get-tuple-element.51), channel_id=1, source_target_pairs={{0,12},{1,15},{2,14},{3,13},{4,8},{5,11},{6,10},{7,9},{8,4},{9,7},... | collective-permute-start | bytes 294920 | tf_op jit(solution)/shard_map/ppermute | solution.py:247
  23.3 7.4 %collective-permute-start.13 = (bf16[20,32,128]{2,1,0:T(8,128)(2,1)S(1)}, bf16[20,32,128]{2,1,0:T(8,128)(2,1)S(1)}, u32[]{:S(2)}, u32[]{:S(2)}) collective-permute-start(bf16[20,32,128]{2,1,0:T(8,128)(2,1)S(1)} %forward.1), channel_id=1, source_target_pairs={{0,1},{1,0},{2,3},{3,2},{4,5},{5,4},{6,7},{7,6},{8,9},{9,8},{10,11... | collective-permute-start | bytes 491528 | tf_op jit(solution)/shard_map/ppermute | solution.py:240
  30.2 1.8 %collective-permute-start.14 = (bf16[2,9,32,128]{3,2,1,0:T(8,128)(2,1)S(1)}, bf16[2,9,32,128]{3,2,1,0:T(8,128)(2,1)S(1)}, u32[]{:S(2)}, u32[]{:S(2)}) collective-permute-start(bf16[2,9,32,128]{3,2,1,0:T(8,128)(2,1)S(1)} %collective-permute-done.11.refs_6_), channel_id=1, source_target_pairs={{0,1},{1,0},{2,3},{3,2},{4,5},{5,4},{6,7},{7,6},{8,9},{9,8},{10,11... | collective-permute-start | bytes 442376 | tf_op jit(solution)/shard_map/ppermute | solution.py:240
  30.2 1.5 %collective-permute-start.15 = (bf16[2,6,32,128]{3,2,1,0:T(8,128)(2,1)S(1)}, bf16[2,6,32,128]{3,2,1,0:T(8,128)(2,1)S(1)}, u32[]{:S(2)}, u32[]{:S(2)}) collective-permute-start(bf16[2,6,32,128]{3,2,1,0:T(8,128)(2,1)S(1)} %collective-permute-done.10.refs_7_), channel_id=1, source_target_pairs={{0,1},{1,0},{2,3},{3,2},{4,5},{5,4},{6,7},{7,6},{8,9},{9,8},{10,11... | collective-permute-start | bytes 294920 | tf_op jit(solution)/shard_map/ppermute | solution.py:240
  30.7 1.3 %collective-permute-start.16 = (bf16[2,6,32,128]{3,2,1,0:T(8,128)(2,1)S(1)}, bf16[2,6,32,128]{3,2,1,0:T(8,128)(2,1)S(1)}, u32[]{:S(2)}, u32[]{:S(2)}) collective-permute-start(bf16[2,6,32,128]{3,2,1,0:T(8,128)(2,1)S(1)} %collective-permute-done.8.refs_8_), channel_id=1, source_target_pairs={{0,1},{1,0},{2,3},{3,2},{4,5},{5,4},{6,7},{7,6},{8,9},{9,8},{10,11... | collective-permute-start | bytes 294920 | tf_op jit(solution)/shard_map/ppermute | solution.py:240

commit v9 on v8

--- a/solution.py
+++ b/solution.py
@@ -122,10 +122,14 @@
             info_ref[...] = jnp.where(row == 0, count, live(second))
 
 
-def forward_kernel(*refs):
+def cross_kernel(*refs):
     *got, out = refs
-    for n, ref in enumerate(got):
-        out[n * 2 * EARLY : (n + 1) * 2 * EARLY] = ref[2 * EARLY : 4 * EARLY]
+    at = 0
+    for ref in got:
+        late = len(ref.shape) == 4
+        tiles = ref.shape[1] if late else 2 * EARLY
+        out[at : at + tiles] = ref[1] if late else ref[2 * EARLY : 4 * EARLY]
+        at += tiles
 
 
 def blank_kernel(out_ref, zeros, sem):
@@ -146,8 +150,7 @@
     half = chips // 2
     first, refs = refs[: half - 1], refs[half - 1 :]
     second, refs = (None, *refs[: half - 2]), refs[half - 2 :]
-    forwarded, refs = refs[0], refs[1:]
-    third, third_crossed, refs = refs[: half - 1], refs[half - 1 : 2 * half - 2], refs[2 * half - 2 :]
+    third, crossed, refs = refs[: half - 1], refs[half - 1], refs[half:]
     out_ref, rows, stage, sems = refs
     doubled, orbitals, width = self_ref.shape
     slots = doubled // 2
@@ -170,21 +173,23 @@
         own_late = slots - 1 - EARLY
         for k in range(1, half):
             for f in range(2):
-                late_ref = (third, third_crossed)[f][k - 1]
+                tiles = third[k - 1].shape[1]
+                skip = (2 * half - 3) * 2 * EARLY + sum(ref.shape[1] for ref in third[: k - 1])
+                late_ref = crossed.at[skip : skip + tiles] if f else third[k - 1].at[0]
                 for q in range(2):
                     base = q * own_late
                     if q == 1 and k == 1:
-                        found.append(late_ref[f, base + s, at, :])
+                        found.append(late_ref[base + s, at, :])
                         continue
                     if f == 0:
                         early_ref, early_base = (first, second)[q][k - 1], 0
                     else:
-                        early_ref, early_base = forwarded, 2 * EARLY * (k - 1 + q * (half - 2))
+                        early_ref, early_base = crossed, 2 * EARLY * (k - 1 + q * (half - 2))
                     found.append(
                         choose(
                             s,
                             lambda n, ref=early_ref, base=early_base: ref[base + n, at, :],
-                            lambda n, ref=late_ref, base=base, f=f: ref[f, base + n, at, :],
+                            lambda n, ref=late_ref, base=base: ref[base + n, at, :],
                             at,
                         )
                     )
@@ -330,21 +335,20 @@
     *third, blank = tie(hops(far + near, third) + [blank])
     third = third[::-1]
     second = second[::-1]
-    forwarded = pl.pallas_call(
-        forward_kernel,
-        out_shape=shape((2 * half - 3) * 2 * EARLY, orbitals, width),
-        in_specs=[VMEM] * (2 * half - 3),
+    crossed = pl.pallas_call(
+        cross_kernel,
+        out_shape=shape((2 * half - 3) * 2 * EARLY + sum(x.shape[1] for x in third[1:]), orbitals, width),
+        in_specs=[VMEM] * (3 * half - 4),
         out_specs=VMEM,
         compiler_params=LIMIT,
-        name="forward",
-    )(*first[1:], *second)
-    forwarded = swap(forwarded)
-    crossed = [swap(x) for x in third[1:]]
+        name="cross",
+    )(*first[1:], *second, *third[1:])
+    crossed = swap(crossed)
 
     return pl.pallas_call(
         functools.partial(exchange_kernel, chips),
         out_shape=jax.ShapeDtypeStruct((2, slots * width, slots * width), jnp.float32),
-        in_specs=[HBM] + [VMEM] * (4 * half),
+        in_specs=[HBM] + [VMEM] * (3 * half + 1),
         out_specs=HBM,
         scratch_shapes=[
             pltpu.VMEM((devices * orbitals, slots * width), raw.dtype),
@@ -354,7 +358,7 @@
         input_output_aliases={0: 0},
         compiler_params=pltpu.CompilerParams(vmem_limit_bytes=32 * 1024 * 1024),
         name="exchange",
-    )(blank, info, factor, own_tiles, third[0], *first[1:], *second, forwarded, *third[1:], *crossed)
+    )(blank, info, factor, own_tiles, third[0], *first[1:], *second, *third[1:], crossed)
 
 
 def solution(mesh):

time: 34.2 us -> 34.1 us (level)
  starting transfers between devices: 20.1 us -> 19.3 us
  waiting for transfers between devices: 6.79 us -> 7.43 us
    ppermute x7 -> x4, starting transfers between devices: 1.4 us -> 0.66 us  [swap(): return lax.ppermute(x, 'aux', [(i, i ^ 1) for i in range(devices)])]
    ppermute x7 -> x4, waiting for transfers between devices: 2.45 us -> 2.78 us  [swap(): return lax.ppermute(x, 'aux', [(i, i ^ 1) for i in range(devices)])]
  transfers between devices with their start and end apart: 17 -> 14, of which waited for: 5 -> 4; matrix products, arithmetic and copies ran while one was open for 5% -> 5% of each run, Pallas kernels for 10% -> 10%
where the time goes in v9:
time: 34.1 us; the launch traced here: 34 us
  starting transfers between devices  19.3 us (57%)
  waiting for transfers between devices  7.43 us (22%)
  Pallas kernels  5.41 us (16%)
  local copies, waits for them, and re-layouts  1.57 us (5%)
    ppermute x10, starting transfers between devices, hop(): return lax.ppermute(x, 'aux', [(i, target(i)) for i in range(devices)])  18.7 us
    ppermute x10, waiting for transfers between devices, hop(): return lax.ppermute(x, 'aux', [(i, target(i)) for i in range(devices)])  4.66 us
    ppermute x4, waiting for transfers between devices, swap(): return lax.ppermute(x, 'aux', [(i, i ^ 1) for i in range(devices)])  2.78 us
    pallas_call x1, Pallas kernels, shards(): pl.pallas_call(lambda _, *refs: blank_kernel(*refs), out_shape=jax.ShapeD...  2.3 us
    pallas_call x1, Pallas kernels, shards(): pl.pallas_call(functools.partial(exchange_kernel, chips), out_shape=jax.S...  2.02 us
    slice x1, local copies, waits for them, and re-layouts, shards(): other, raw = tie((swap(counts), raw[:, :slots - 1]))  1.56 us
  transfers between devices with their start and end apart: 14, of which 4 were waited for; matrix products, arithmetic and copies ran while one was open for 5% of the time, Pallas kernels for 10%

profile of v9, /device:TPU:0, one launch (start us, length us, event | category | flops | bytes accessed | tf_op | source)
XLA Modules:
  0.0 34.0 jit_solution(14714667577149346288)
XLA Ops:
  0.0 0.5 %collective-permute-start = (s32[2]{0:T(128)}, s32[2]{0:T(128)S(1)}, u32[]{:S(2)}, u32[]{:S(2)}) collective-permute-start(s32[2]{0:T(128)} %param.7), channel_id=1, source_target_pairs={{0,1},{1,0},{2,3},{3,2},{4,5},{5,4},{6,7},{7,6},{8,9},{9,8},{10,11... | collective-permute-start | bytes 32 | tf_op jit(solution)/shard_map/ppermute | solution.py:245
  0.5 1.6 %slice.4.raw_ref.own_raw = bf16[32,5,32,128]{3,2,1,0:T(8,128)(2,1)S(1)} slice(bf16[32,6,32,128]{3,2,1,0:T(8,128)(2,1)} %bitcast.5), slice={[0:32], [0:5], [0:32], [0:128]} | slice | bytes 2621440 | tf_op jit(solution)/shard_map/slice | solution.py:257
  2.0 0.0 collective-permute-done
  2.1 0.1 add_bitcast_fusion.small_ref
  2.1 0.1 collective-permute-start.6
  2.2 0.2 early.2
  2.4 5.1 %collective-permute-start.1 = (bf16[9,32,128]{2,1,0:T(8,128)(2,1)S(1)}, bf16[9,32,128]{2,1,0:T(8,128)(2,1)S(1)}, u32[]{:S(2)}, u32[]{:S(2)}) collective-permute-start(bf16[9,32,128]{2,1,0:T(8,128)(2,1)S(1)} %get-tuple-element.39), channel_id=1, source_target_pairs={{0,12},{1,15},{2,14},{3,13},{4,8},{5,11},{6,10},{7,9},{8,4},{9,7},... | collective-permute-start | bytes 221192 | tf_op jit(solution)/shard_map/ppermute | solution.py:252
  7.5 0.0 collective-permute-start.2
  7.5 0.6 %collective-permute-start.3 = (bf16[9,32,128]{2,1,0:T(8,128)(2,1)S(1)}, bf16[9,32,128]{2,1,0:T(8,128)(2,1)S(1)}, u32[]{:S(2)}, u32[]{:S(2)}) collective-permute-start(bf16[9,32,128]{2,1,0:T(8,128)(2,1)S(1)} %get-tuple-element.41), channel_id=1, source_target_pairs={{0,4},{1,7},{2,6},{3,5},{4,0},{5,3},{6,2},{7,1},{8,12},{9,15},{10,... | collective-permute-start | bytes 221192 | tf_op jit(solution)/shard_map/ppermute | solution.py:252
  8.1 1.7 %collective-permute-start.4 = (bf16[1,32,128]{2,1,0:T(8,128)(2,1)S(1)}, bf16[1,32,128]{2,1,0:T(8,128)(2,1)S(1)}, u32[]{:S(2)}, u32[]{:S(2)}) collective-permute-start(bf16[1,32,128]{2,1,0:T(8,128)(2,1)S(1)} %get-tuple-element.42), channel_id=1, source_target_pairs={{0,2},{1,3},{2,0},{3,1},{4,6},{5,7},{6,4},{7,5},{8,10},{9,11},{10,... | collective-permute-start | bytes 24584 | tf_op jit(solution)/shard_map/ppermute | solution.py:252
  9.8 0.3 factor.1.factor_ref
  10.1 0.0 collective-permute-done.6.peer_raw.raw_ref
  10.1 0.2 early.3
  10.3 2.2 %collective-permute-start.7 = (bf16[8,32,128]{2,1,0:T(8,128)(2,1)S(1)}, bf16[8,32,128]{2,1,0:T(8,128)(2,1)S(1)}, u32[]{:S(2)}, u32[]{:S(2)}) collective-permute-start(bf16[8,32,128]{2,1,0:T(8,128)(2,1)S(1)} %get-tuple-element.50), channel_id=1, source_target_pairs={{0,8},{1,11},{2,10},{3,9},{4,12},{5,15},{6,14},{7,13},{8,0},{9,3},... | collective-permute-start | bytes 196616 | tf_op jit(solution)/shard_map/ppermute | solution.py:252
  12.5 0.0 collective-permute-done.4.refs_0_
  12.5 3.1 %collective-permute-start.9 = (bf16[8,32,128]{2,1,0:T(8,128)(2,1)S(1)}, bf16[8,32,128]{2,1,0:T(8,128)(2,1)S(1)}, u32[]{:S(2)}, u32[]{:S(2)}) collective-permute-start(bf16[8,32,128]{2,1,0:T(8,128)(2,1)S(1)} %get-tuple-element.53), channel_id=1, source_target_pairs={{0,12},{1,15},{2,14},{3,13},{4,8},{5,11},{6,10},{7,9},{8,4},{9,7},... | collective-permute-start | bytes 196616 | tf_op jit(solution)/shard_map/ppermute | solution.py:252
  15.6 0.0 collective-permute-done.3.refs_1_.refs_0_
  15.7 0.1 collective-permute-start.5
  15.7 1.1 %collective-permute-done.5.crossed_ref = s32[4,128]{1,0:T(4,128)S(1)} collective-permute-done((s32[4,128]{1,0:T(4,128)S(1)}, s32[4,128]{1,0:T(4,128)S(1)}, u32[]{:S(2)}, u32[]{:S(2)}) %collective-permute-start.5) | collective-permute-done | bytes 2080 | tf_op jit(solution)/shard_map/ppermute | solution.py:245
  16.9 0.5 %late.1 = (bf16[2,6,32,128]{3,2,1,0:T(8,128)(2,1)S(1)}, bf16[2,6,32,128]{3,2,1,0:T(8,128)(2,1)S(1)}, bf16[2,9,32,128]{3,2,1,0:T(8,128)(2,1)S(1)}, bf16[12,32,128...) custom-call(s32[1,128]{1,0:T(1,128)S(1)} %add_bitcast_fusion.small_ref, ...), custom_call_target="tpu_custom_call" | custom-call | bytes 1024 | tf_op jit(solution)/shard_map/late/pallas_call | solution.py:308
  17.4 0.2 collective-permute-start.11
  17.5 1.5 %collective-permute-start.12 = (bf16[12,32,128]{2,1,0:T(8,128)(2,1)S(1)}, bf16[12,32,128]{2,1,0:T(8,128)(2,1)S(1)}, u32[]{:S(2)}, u32[]{:S(2)}) collective-permute-start(bf16[12,32,128]{2,1,0:T(8,128)(2,1)S(1)} %get-tuple-element.56), channel_id=1, source_target_pairs={{0,2},{1,3},{2,0},{3,1},{4,6},{5,7},{6,4},{7,5},{8,10},{9,11},{10,... | collective-permute-start | bytes 294920 | tf_op jit(solution)/shard_map/ppermute | solution.py:252
  19.0 0.1 collective-permute-done.9.refs_4_
  19.1 3.3 %collective-permute-start.10 = (bf16[2,6,32,128]{3,2,1,0:T(8,128)(2,1)S(1)}, bf16[2,6,32,128]{3,2,1,0:T(8,128)(2,1)S(1)}, u32[]{:S(2)}, u32[]{:S(2)}) collective-permute-start(bf16[2,6,32,128]{3,2,1,0:T(8,128)(2,1)S(1)} %get-tuple-element.54), channel_id=1, source_target_pairs={{0,8},{1,11},{2,10},{3,9},{4,12},{5,15},{6,14},{7,13},{8,0},{9,3},... | collective-permute-start | bytes 294920 | tf_op jit(solution)/shard_map/ppermute | solution.py:252
  22.4 1.0 %collective-permute-start.8 = (bf16[2,6,32,128]{3,2,1,0:T(8,128)(2,1)S(1)}, bf16[2,6,32,128]{3,2,1,0:T(8,128)(2,1)S(1)}, u32[]{:S(2)}, u32[]{:S(2)}) collective-permute-start(bf16[2,6,32,128]{3,2,1,0:T(8,128)(2,1)S(1)} %get-tuple-element.51), channel_id=1, source_target_pairs={{0,12},{1,15},{2,14},{3,13},{4,8},{5,11},{6,10},{7,9},{8,4},{9,7},... | collective-permute-start | bytes 294920 | tf_op jit(solution)/shard_map/ppermute | solution.py:252
  23.3 2.3 %blank.1.blank_ref = f32[2,768,768]{2,1,0:T(8,128)} custom-call(s32[8,128]{1,0:T(8,128)S(1)} %get-tuple-element.57._.info_ref), custom_call_target="tpu_custom_call" | custom-call | tf_op jit(solution)/shard_map/blank/pallas_call | solution.py:326
  25.6 0.0 collective-permute-done.11.refs_5_
  25.7 4.5 %collective-permute-done.10.refs_6_ = bf16[2,6,32,128]{3,2,1,0:T(8,128)(2,1)S(1)} collective-permute-done((bf16[2,6,32,128]{3,2,1,0:T(8,128)(2,1)S(1)}, bf16[2,6,32,128]{3,2,1,0:T(8,128)(2,1)S(1)}, u32[]{:S(2)}, u32[]{:S(2)}) %collective-permute-start.10) | collective-permute-done | bytes 98336 | tf_op jit(solution)/shard_map/ppermute | solution.py:252
  30.2 0.0 collective-permute-done.8.refs_7_
  30.2 0.1 collective-permute-start.13
  30.3 1.6 %collective-permute-done.13.refs_8_ = bf16[41,32,128]{2,1,0:T(8,128)(2,1)S(1)} collective-permute-done((bf16[41,32,128]{2,1,0:T(8,128)(2,1)S(1)}, bf16[41,32,128]{2,1,0:T(8,128)(2,1)S(1)}, u32[]{:S(2)}, u32[]{:S(2)}) %collective-permute-start.13) | collective-permute-done | bytes 335904 | tf_op jit(solution)/shard_map/ppermute | solution.py:245
  31.9 2.0 %exchange.1 = f32[2,768,768]{2,1,0:T(8,128)} custom-call(f32[2,768,768]{2,1,0:T(8,128)} %blank.1.blank_ref, s32[8,128]{1,0:T(8,128)S(1)} %get-tuple-element.57._.info_ref, bf16[256,256]{1,0:T(8,128)(2,1)S(1)} %factor.1.factor_ref, bf16[12,32,128]{2,1,0:T(8,128)(2,1)S(1)} %get-tuple-element.60.self_ref, ...), custom_call_target="tpu_custom_call", output_to_operand_aliasing={{}: (0, {})} | custom-call | tf_op jit(solution)/shard_map/exchange/pallas_call | solution.py:348
  (13 shorter events, 0.1 us)
Async XLA Ops:
  0.0 2.0 %copy-start.1 = (s32[2]{0:T(128)S(1)}, s32[2]{0:T(128)}, u32[]{:S(2)}) copy-start(s32[2]{0:T(128)} %param.7) | copy-start | bytes 28
  0.0 2.1 %copy-start.2 = (s32[32]{0:T(128)S(1)}, s32[32]{0:T(128)}, u32[]{:S(2)}) copy-start(s32[32]{0:T(128)} %param.6) | copy-start | bytes 388
  0.0 2.0 %collective-permute-start = (s32[2]{0:T(128)}, s32[2]{0:T(128)S(1)}, u32[]{:S(2)}, u32[]{:S(2)}) collective-permute-start(s32[2]{0:T(128)} %param.7), channel_id=1, source_target_pairs={{0,1},{1,0},{2,3},{3,2},{4,5},{5,4},{6,7},{7,6},{8,9},{9,8},{10,11... | collective-permute-start | bytes 32 | tf_op jit(solution)/shard_map/ppermute | solution.py:245
  0.5 9.3 %copy-start = (bf16[16,16]{1,0:T(8,128)(2,1)S(1)}, bf16[16,16]{1,0:T(8,128)(2,1)}, u32[]{:S(2)}) copy-start(bf16[16,16]{1,0:T(8,128)(2,1)} %metric_ref.1) | copy-start | bytes 1540
  2.1 8.0 %collective-permute-start.6 = (bf16[32,5,32,128]{3,2,1,0:T(8,128)(2,1)S(1)}, bf16[32,5,32,128]{3,2,1,0:T(8,128)(2,1)S(1)}, u32[]{:S(2)}, u32[]{:S(2)}) collective-permute-start(bf16[32,5,32,128]{3,2,1,0:T(8,128)(2,1)S(1)} %slice.4.raw_ref.own_raw), channel_id=1, source_target_pairs={{0,1},{1,0},{2,3},{3,2},{4,5},{5,4},{6,7},{7,6},{8,9},{9,8},{10,11... | collective-permute-start | bytes 3932168 | tf_op jit(solution)/shard_map/ppermute | solution.py:245
  2.4 13.3 %collective-permute-start.1 = (bf16[9,32,128]{2,1,0:T(8,128)(2,1)S(1)}, bf16[9,32,128]{2,1,0:T(8,128)(2,1)S(1)}, u32[]{:S(2)}, u32[]{:S(2)}) collective-permute-start(bf16[9,32,128]{2,1,0:T(8,128)(2,1)S(1)} %get-tuple-element.39), channel_id=1, source_target_pairs={{0,12},{1,15},{2,14},{3,13},{4,8},{5,11},{6,10},{7,9},{8,4},{9,7},... | collective-permute-start | bytes 221192 | tf_op jit(solution)/shard_map/ppermute | solution.py:252
  7.5 8.2 %collective-permute-start.2 = (bf16[9,32,128]{2,1,0:T(8,128)(2,1)S(1)}, bf16[9,32,128]{2,1,0:T(8,128)(2,1)S(1)}, u32[]{:S(2)}, u32[]{:S(2)}) collective-permute-start(bf16[9,32,128]{2,1,0:T(8,128)(2,1)S(1)} %get-tuple-element.40), channel_id=1, source_target_pairs={{0,8},{1,11},{2,10},{3,9},{4,12},{5,15},{6,14},{7,13},{8,0},{9,3},... | collective-permute-start | bytes 221192 | tf_op jit(solution)/shard_map/ppermute | solution.py:252
  7.5 8.2 %collective-permute-start.3 = (bf16[9,32,128]{2,1,0:T(8,128)(2,1)S(1)}, bf16[9,32,128]{2,1,0:T(8,128)(2,1)S(1)}, u32[]{:S(2)}, u32[]{:S(2)}) collective-permute-start(bf16[9,32,128]{2,1,0:T(8,128)(2,1)S(1)} %get-tuple-element.41), channel_id=1, source_target_pairs={{0,4},{1,7},{2,6},{3,5},{4,0},{5,3},{6,2},{7,1},{8,12},{9,15},{10,... | collective-permute-start | bytes 221192 | tf_op jit(solution)/shard_map/ppermute | solution.py:252
  8.1 4.4 %collective-permute-start.4 = (bf16[1,32,128]{2,1,0:T(8,128)(2,1)S(1)}, bf16[1,32,128]{2,1,0:T(8,128)(2,1)S(1)}, u32[]{:S(2)}, u32[]{:S(2)}) collective-permute-start(bf16[1,32,128]{2,1,0:T(8,128)(2,1)S(1)} %get-tuple-element.42), channel_id=1, source_target_pairs={{0,2},{1,3},{2,0},{3,1},{4,6},{5,7},{6,4},{7,5},{8,10},{9,11},{10,... | collective-permute-start | bytes 24584 | tf_op jit(solution)/shard_map/ppermute | solution.py:252
  10.3 8.7 %collective-permute-start.7 = (bf16[8,32,128]{2,1,0:T(8,128)(2,1)S(1)}, bf16[8,32,128]{2,1,0:T(8,128)(2,1)S(1)}, u32[]{:S(2)}, u32[]{:S(2)}) collective-permute-start(bf16[8,32,128]{2,1,0:T(8,128)(2,1)S(1)} %get-tuple-element.50), channel_id=1, source_target_pairs={{0,8},{1,11},{2,10},{3,9},{4,12},{5,15},{6,14},{7,13},{8,0},{9,3},... | collective-permute-start | bytes 196616 | tf_op jit(solution)/shard_map/ppermute | solution.py:252
  12.5 6.6 %collective-permute-start.9 = (bf16[8,32,128]{2,1,0:T(8,128)(2,1)S(1)}, bf16[8,32,128]{2,1,0:T(8,128)(2,1)S(1)}, u32[]{:S(2)}, u32[]{:S(2)}) collective-permute-start(bf16[8,32,128]{2,1,0:T(8,128)(2,1)S(1)} %get-tuple-element.53), channel_id=1, source_target_pairs={{0,12},{1,15},{2,14},{3,13},{4,8},{5,11},{6,10},{7,9},{8,4},{9,7},... | collective-permute-start | bytes 196616 | tf_op jit(solution)/shard_map/ppermute | solution.py:252
  15.7 1.2 %collective-permute-start.5 = (s32[4,128]{1,0:T(4,128)S(1)}, s32[4,128]{1,0:T(4,128)S(1)}, u32[]{:S(2)}, u32[]{:S(2)}) collective-permute-start(s32[4,128]{1,0:T(4,128)S(1)} %counts.1.counts_ref), channel_id=1, source_target_pairs={{0,1},{1,0},{2,3},{3,2},{4,5},{5,4},{6,7},{7,6},{8,9},{9,8},{10,11... | collective-permute-start | bytes 6152 | tf_op jit(solution)/shard_map/ppermute | solution.py:245
  17.4 8.3 %collective-permute-start.11 = (bf16[2,9,32,128]{3,2,1,0:T(8,128)(2,1)S(1)}, bf16[2,9,32,128]{3,2,1,0:T(8,128)(2,1)S(1)}, u32[]{:S(2)}, u32[]{:S(2)}) collective-permute-start(bf16[2,9,32,128]{3,2,1,0:T(8,128)(2,1)S(1)} %get-tuple-element.55), channel_id=1, source_target_pairs={{0,4},{1,7},{2,6},{3,5},{4,0},{5,3},{6,2},{7,1},{8,12},{9,15},{10,... | collective-permute-start | bytes 442376 | tf_op jit(solution)/shard_map/ppermute | solution.py:252
  17.5 8.1 %collective-permute-start.12 = (bf16[12,32,128]{2,1,0:T(8,128)(2,1)S(1)}, bf16[12,32,128]{2,1,0:T(8,128)(2,1)S(1)}, u32[]{:S(2)}, u32[]{:S(2)}) collective-permute-start(bf16[12,32,128]{2,1,0:T(8,128)(2,1)S(1)} %get-tuple-element.56), channel_id=1, source_target_pairs={{0,2},{1,3},{2,0},{3,1},{4,6},{5,7},{6,4},{7,5},{8,10},{9,11},{10,... | collective-permute-start | bytes 294920 | tf_op jit(solution)/shard_map/ppermute | solution.py:252
  19.1 11.1 %collective-permute-start.10 = (bf16[2,6,32,128]{3,2,1,0:T(8,128)(2,1)S(1)}, bf16[2,6,32,128]{3,2,1,0:T(8,128)(2,1)S(1)}, u32[]{:S(2)}, u32[]{:S(2)}) collective-permute-start(bf16[2,6,32,128]{3,2,1,0:T(8,128)(2,1)S(1)} %get-tuple-element.54), channel_id=1, source_target_pairs={{0,8},{1,11},{2,10},{3,9},{4,12},{5,15},{6,14},{7,13},{8,0},{9,3},... | collective-permute-start | bytes 294920 | tf_op jit(solution)/shard_map/ppermute | solution.py:252
  22.4 7.8 %collective-permute-start.8 = (bf16[2,6,32,128]{3,2,1,0:T(8,128)(2,1)S(1)}, bf16[2,6,32,128]{3,2,1,0:T(8,128)(2,1)S(1)}, u32[]{:S(2)}, u32[]{:S(2)}) collective-permute-start(bf16[2,6,32,128]{3,2,1,0:T(8,128)(2,1)S(1)} %get-tuple-element.51), channel_id=1, source_target_pairs={{0,12},{1,15},{2,14},{3,13},{4,8},{5,11},{6,10},{7,9},{8,4},{9,7},... | collective-permute-start | bytes 294920 | tf_op jit(solution)/shard_map/ppermute | solution.py:252
  30.2 1.7 %collective-permute-start.13 = (bf16[41,32,128]{2,1,0:T(8,128)(2,1)S(1)}, bf16[41,32,128]{2,1,0:T(8,128)(2,1)S(1)}, u32[]{:S(2)}, u32[]{:S(2)}) collective-permute-start(bf16[41,32,128]{2,1,0:T(8,128)(2,1)S(1)} %cross.1), channel_id=1, source_target_pairs={{0,1},{1,0},{2,3},{3,2},{4,5},{5,4},{6,7},{7,6},{8,9},{9,8},{10,11... | collective-permute-start | bytes 1007624 | tf_op jit(solution)/shard_map/ppermute | solution.py:245

commit v10 on v9

--- a/solution.py
+++ b/solution.py
@@ -256,16 +256,6 @@
 
     other, raw = tie((swap(counts), raw[:, : slots - 1]))
     small = jnp.concatenate([owner_map, counts, other, jnp.zeros((lines - blocks - 4,), jnp.int32)]).reshape(1, lines)
-    raw_there, small = tie((raw, small))
-    factor = pl.pallas_call(
-        factor_kernel,
-        out_shape=shape(devices * GROUP, devices * GROUP),
-        in_specs=[VMEM],
-        out_specs=VMEM,
-        compiler_params=LIMIT,
-        name="factor",
-    )(metric)
-    peer_raw, factor = tie((swap(raw_there), factor))
 
     far = [*reversed(range(2, half))]
     near = [1, 0]
@@ -286,7 +276,17 @@
         return [hop(x, k) for k, x in zip(ks, xs)]
 
     ways = far + near
-    first = hops(ways, early(ways, raw, 1))
+    first, raw_there = tie((early(ways, raw, 1), raw))
+    factor = pl.pallas_call(
+        factor_kernel,
+        out_shape=shape(devices * GROUP, devices * GROUP),
+        in_specs=[VMEM],
+        out_specs=VMEM,
+        compiler_params=LIMIT,
+        name="factor",
+    )(metric)
+    peer_raw, factor = tie((swap(raw_there), factor))
+    first = hops(ways, first)
     second = hops(far, early(far, peer_raw, 0))
     *first, beside, side = tie(first)
     first = [side, beside, *first[::-1]]

time: 34.1 us -> 34 us (level)
  transfers between devices with their start and end apart: 14 -> 14, of which waited for: 4 -> 4; matrix products, arithmetic and copies ran while one was open for 5% -> 5% of each run, Pallas kernels for 10% -> 9%
where the time goes in v10:
time: 34 us; the launch traced here: 33.9 us
  starting transfers between devices  19.2 us (56%)
  waiting for transfers between devices  7.5 us (22%)
  Pallas kernels  5.37 us (16%)
  local copies, waits for them, and re-layouts  1.57 us (5%)
    ppermute x10, starting transfers between devices, hop(): return lax.ppermute(x, 'aux', [(i, target(i)) for i in range(devices)])  18.5 us
    ppermute x10, waiting for transfers between devices, hop(): return lax.ppermute(x, 'aux', [(i, target(i)) for i in range(devices)])  4.72 us
    ppermute x4, waiting for transfers between devices, swap(): return lax.ppermute(x, 'aux', [(i, i ^ 1) for i in range(devices)])  2.78 us
    pallas_call x1, Pallas kernels, shards(): pl.pallas_call(lambda _, *refs: blank_kernel(*refs), out_shape=jax.ShapeD...  2.3 us
    pallas_call x1, Pallas kernels, shards(): pl.pallas_call(functools.partial(exchange_kernel, chips), out_shape=jax.S...  1.96 us
    slice x1, local copies, waits for them, and re-layouts, shards(): other, raw = tie((swap(counts), raw[:, :slots - 1]))  1.56 us
    ppermute x4, starting transfers between devices, swap(): return lax.ppermute(x, 'aux', [(i, i ^ 1) for i in range(devices)])  0.72 us
  transfers between devices with their start and end apart: 14, of which 4 were waited for; matrix products, arithmetic and copies ran while one was open for 5% of the time, Pallas kernels for 9%

profile of v10, /device:TPU:0, one launch (start us, length us, event | category | flops | bytes accessed | tf_op | source)
XLA Modules:
  0.0 33.9 jit_solution(17877991111855118382)
XLA Ops:
  0.0 0.5 %collective-permute-start = (s32[2]{0:T(128)}, s32[2]{0:T(128)S(1)}, u32[]{:S(2)}, u32[]{:S(2)}) collective-permute-start(s32[2]{0:T(128)} %param.7), channel_id=1, source_target_pairs={{0,1},{1,0},{2,3},{3,2},{4,5},{5,4},{6,7},{7,6},{8,9},{9,8},{10,11... | collective-permute-start | bytes 32 | tf_op jit(solution)/shard_map/ppermute | solution.py:245
  0.5 1.6 %slice.4.raw_ref.own_raw = bf16[32,5,32,128]{3,2,1,0:T(8,128)(2,1)S(1)} slice(bf16[32,6,32,128]{3,2,1,0:T(8,128)(2,1)} %bitcast.5), slice={[0:32], [0:5], [0:32], [0:128]} | slice | bytes 2621440 | tf_op jit(solution)/shard_map/slice | solution.py:257
  2.0 0.0 collective-permute-done
  2.1 0.1 add_bitcast_fusion.small_ref
  2.1 0.2 early.2
  2.3 0.1 collective-permute-start.6
  2.4 5.0 %collective-permute-start.1 = (bf16[9,32,128]{2,1,0:T(8,128)(2,1)S(1)}, bf16[9,32,128]{2,1,0:T(8,128)(2,1)S(1)}, u32[]{:S(2)}, u32[]{:S(2)}) collective-permute-start(bf16[9,32,128]{2,1,0:T(8,128)(2,1)S(1)} %get-tuple-element.45), channel_id=1, source_target_pairs={{0,12},{1,15},{2,14},{3,13},{4,8},{5,11},{6,10},{7,9},{8,4},{9,7},... | collective-permute-start | bytes 221192 | tf_op jit(solution)/shard_map/ppermute | solution.py:252
  7.5 0.0 collective-permute-start.2
  7.5 0.6 %collective-permute-start.3 = (bf16[9,32,128]{2,1,0:T(8,128)(2,1)S(1)}, bf16[9,32,128]{2,1,0:T(8,128)(2,1)S(1)}, u32[]{:S(2)}, u32[]{:S(2)}) collective-permute-start(bf16[9,32,128]{2,1,0:T(8,128)(2,1)S(1)} %get-tuple-element.47), channel_id=1, source_target_pairs={{0,4},{1,7},{2,6},{3,5},{4,0},{5,3},{6,2},{7,1},{8,12},{9,15},{10,... | collective-permute-start | bytes 221192 | tf_op jit(solution)/shard_map/ppermute | solution.py:252
  8.1 1.7 %collective-permute-start.4 = (bf16[1,32,128]{2,1,0:T(8,128)(2,1)S(1)}, bf16[1,32,128]{2,1,0:T(8,128)(2,1)S(1)}, u32[]{:S(2)}, u32[]{:S(2)}) collective-permute-start(bf16[1,32,128]{2,1,0:T(8,128)(2,1)S(1)} %get-tuple-element.48), channel_id=1, source_target_pairs={{0,2},{1,3},{2,0},{3,1},{4,6},{5,7},{6,4},{7,5},{8,10},{9,11},{10,... | collective-permute-start | bytes 24584 | tf_op jit(solution)/shard_map/ppermute | solution.py:252
  9.8 0.3 factor.1.factor_ref
  10.1 0.2 early.3
  10.3 2.2 %collective-permute-start.7 = (bf16[8,32,128]{2,1,0:T(8,128)(2,1)S(1)}, bf16[8,32,128]{2,1,0:T(8,128)(2,1)S(1)}, u32[]{:S(2)}, u32[]{:S(2)}) collective-permute-start(bf16[8,32,128]{2,1,0:T(8,128)(2,1)S(1)} %get-tuple-element.56), channel_id=1, source_target_pairs={{0,8},{1,11},{2,10},{3,9},{4,12},{5,15},{6,14},{7,13},{8,0},{9,3},... | collective-permute-start | bytes 196616 | tf_op jit(solution)/shard_map/ppermute | solution.py:252
  12.5 3.1 %collective-permute-start.9 = (bf16[8,32,128]{2,1,0:T(8,128)(2,1)S(1)}, bf16[8,32,128]{2,1,0:T(8,128)(2,1)S(1)}, u32[]{:S(2)}, u32[]{:S(2)}) collective-permute-start(bf16[8,32,128]{2,1,0:T(8,128)(2,1)S(1)} %get-tuple-element.59), channel_id=1, source_target_pairs={{0,12},{1,15},{2,14},{3,13},{4,8},{5,11},{6,10},{7,9},{8,4},{9,7},... | collective-permute-start | bytes 196616 | tf_op jit(solution)/shard_map/ppermute | solution.py:252
  15.6 0.0 collective-permute-done.1.refs_3_.refs_2_
  15.6 0.0 collective-permute-done.2.refs_2_.refs_1_
  15.6 0.0 collective-permute-done.3.refs_1_.refs_0_
  15.6 0.1 collective-permute-start.5
  15.7 1.1 %collective-permute-done.5.crossed_ref = s32[4,128]{1,0:T(4,128)S(1)} collective-permute-done((s32[4,128]{1,0:T(4,128)S(1)}, s32[4,128]{1,0:T(4,128)S(1)}, u32[]{:S(2)}, u32[]{:S(2)}) %collective-permute-start.5) | collective-permute-done | bytes 2080 | tf_op jit(solution)/shard_map/ppermute | solution.py:245
  16.8 0.5 %late.1 = (bf16[2,6,32,128]{3,2,1,0:T(8,128)(2,1)S(1)}, bf16[2,6,32,128]{3,2,1,0:T(8,128)(2,1)S(1)}, bf16[2,9,32,128]{3,2,1,0:T(8,128)(2,1)S(1)}, bf16[12,32,128...) custom-call(s32[1,128]{1,0:T(1,128)S(1)} %add_bitcast_fusion.small_ref, ...), custom_call_target="tpu_custom_call" | custom-call | bytes 1024 | tf_op jit(solution)/shard_map/late/pallas_call | solution.py:308
  17.3 0.2 collective-permute-start.11
  17.5 1.5 %collective-permute-start.12 = (bf16[12,32,128]{2,1,0:T(8,128)(2,1)S(1)}, bf16[12,32,128]{2,1,0:T(8,128)(2,1)S(1)}, u32[]{:S(2)}, u32[]{:S(2)}) collective-permute-start(bf16[12,32,128]{2,1,0:T(8,128)(2,1)S(1)} %get-tuple-element.62), channel_id=1, source_target_pairs={{0,2},{1,3},{2,0},{3,1},{4,6},{5,7},{6,4},{7,5},{8,10},{9,11},{10,... | collective-permute-start | bytes 294920 | tf_op jit(solution)/shard_map/ppermute | solution.py:252
  19.0 0.2 collective-permute-done.9.refs_4_
  19.2 3.2 %collective-permute-start.10 = (bf16[2,6,32,128]{3,2,1,0:T(8,128)(2,1)S(1)}, bf16[2,6,32,128]{3,2,1,0:T(8,128)(2,1)S(1)}, u32[]{:S(2)}, u32[]{:S(2)}) collective-permute-start(bf16[2,6,32,128]{3,2,1,0:T(8,128)(2,1)S(1)} %get-tuple-element.60), channel_id=1, source_target_pairs={{0,8},{1,11},{2,10},{3,9},{4,12},{5,15},{6,14},{7,13},{8,0},{9,3},... | collective-permute-start | bytes 294920 | tf_op jit(solution)/shard_map/ppermute | solution.py:252
  22.4 1.0 %collective-permute-start.8 = (bf16[2,6,32,128]{3,2,1,0:T(8,128)(2,1)S(1)}, bf16[2,6,32,128]{3,2,1,0:T(8,128)(2,1)S(1)}, u32[]{:S(2)}, u32[]{:S(2)}) collective-permute-start(bf16[2,6,32,128]{3,2,1,0:T(8,128)(2,1)S(1)} %get-tuple-element.57), channel_id=1, source_target_pairs={{0,12},{1,15},{2,14},{3,13},{4,8},{5,11},{6,10},{7,9},{8,4},{9,7},... | collective-permute-start | bytes 294920 | tf_op jit(solution)/shard_map/ppermute | solution.py:252
  23.3 2.3 %blank.1.blank_ref = f32[2,768,768]{2,1,0:T(8,128)} custom-call(s32[8,128]{1,0:T(8,128)S(1)} %get-tuple-element.63._.info_ref), custom_call_target="tpu_custom_call" | custom-call | tf_op jit(solution)/shard_map/blank/pallas_call | solution.py:326
  25.6 0.0 collective-permute-done.11.refs_5_
  25.7 4.5 %collective-permute-done.10.refs_6_ = bf16[2,6,32,128]{3,2,1,0:T(8,128)(2,1)S(1)} collective-permute-done((bf16[2,6,32,128]{3,2,1,0:T(8,128)(2,1)S(1)}, bf16[2,6,32,128]{3,2,1,0:T(8,128)(2,1)S(1)}, u32[]{:S(2)}, u32[]{:S(2)}) %collective-permute-start.10) | collective-permute-done | bytes 98336 | tf_op jit(solution)/shard_map/ppermute | solution.py:252
  30.2 0.0 collective-permute-done.8.refs_7_
  30.2 0.1 collective-permute-start.13
  30.3 1.6 %collective-permute-done.13.refs_8_ = bf16[41,32,128]{2,1,0:T(8,128)(2,1)S(1)} collective-permute-done((bf16[41,32,128]{2,1,0:T(8,128)(2,1)S(1)}, bf16[41,32,128]{2,1,0:T(8,128)(2,1)S(1)}, u32[]{:S(2)}, u32[]{:S(2)}) %collective-permute-start.13) | collective-permute-done | bytes 335904 | tf_op jit(solution)/shard_map/ppermute | solution.py:245
  31.9 2.0 %exchange.1 = f32[2,768,768]{2,1,0:T(8,128)} custom-call(f32[2,768,768]{2,1,0:T(8,128)} %blank.1.blank_ref, s32[8,128]{1,0:T(8,128)S(1)} %get-tuple-element.63._.info_ref, bf16[256,256]{1,0:T(8,128)(2,1)S(1)} %factor.1.factor_ref, bf16[12,32,128]{2,1,0:T(8,128)(2,1)S(1)} %get-tuple-element.66.self_ref, ...), custom_call_target="tpu_custom_call", output_to_operand_aliasing={{}: (0, {})} | custom-call | tf_op jit(solution)/shard_map/exchange/pallas_call | solution.py:348
  (13 shorter events, 0.1 us)
Async XLA Ops:
  0.0 2.0 %copy-start.1 = (s32[2]{0:T(128)S(1)}, s32[2]{0:T(128)}, u32[]{:S(2)}) copy-start(s32[2]{0:T(128)} %param.7) | copy-start | bytes 28
  0.0 2.1 %copy-start.2 = (s32[32]{0:T(128)S(1)}, s32[32]{0:T(128)}, u32[]{:S(2)}) copy-start(s32[32]{0:T(128)} %param.6) | copy-start | bytes 388
  0.0 2.0 %collective-permute-start = (s32[2]{0:T(128)}, s32[2]{0:T(128)S(1)}, u32[]{:S(2)}, u32[]{:S(2)}) collective-permute-start(s32[2]{0:T(128)} %param.7), channel_id=1, source_target_pairs={{0,1},{1,0},{2,3},{3,2},{4,5},{5,4},{6,7},{7,6},{8,9},{9,8},{10,11... | collective-permute-start | bytes 32 | tf_op jit(solution)/shard_map/ppermute | solution.py:245
  0.5 9.3 %copy-start = (bf16[16,16]{1,0:T(8,128)(2,1)S(1)}, bf16[16,16]{1,0:T(8,128)(2,1)}, u32[]{:S(2)}) copy-start(bf16[16,16]{1,0:T(8,128)(2,1)} %metric_ref.1) | copy-start | bytes 1540
  2.3 7.8 %collective-permute-start.6 = (bf16[32,5,32,128]{3,2,1,0:T(8,128)(2,1)S(1)}, bf16[32,5,32,128]{3,2,1,0:T(8,128)(2,1)S(1)}, u32[]{:S(2)}, u32[]{:S(2)}) collective-permute-start(bf16[32,5,32,128]{3,2,1,0:T(8,128)(2,1)S(1)} %slice.4.raw_ref.own_raw), channel_id=1, source_target_pairs={{0,1},{1,0},{2,3},{3,2},{4,5},{5,4},{6,7},{7,6},{8,9},{9,8},{10,11... | collective-permute-start | bytes 3932168 | tf_op jit(solution)/shard_map/ppermute | solution.py:245
  2.4 13.1 %collective-permute-start.1 = (bf16[9,32,128]{2,1,0:T(8,128)(2,1)S(1)}, bf16[9,32,128]{2,1,0:T(8,128)(2,1)S(1)}, u32[]{:S(2)}, u32[]{:S(2)}) collective-permute-start(bf16[9,32,128]{2,1,0:T(8,128)(2,1)S(1)} %get-tuple-element.45), channel_id=1, source_target_pairs={{0,12},{1,15},{2,14},{3,13},{4,8},{5,11},{6,10},{7,9},{8,4},{9,7},... | collective-permute-start | bytes 221192 | tf_op jit(solution)/shard_map/ppermute | solution.py:252
  7.5 8.1 %collective-permute-start.2 = (bf16[9,32,128]{2,1,0:T(8,128)(2,1)S(1)}, bf16[9,32,128]{2,1,0:T(8,128)(2,1)S(1)}, u32[]{:S(2)}, u32[]{:S(2)}) collective-permute-start(bf16[9,32,128]{2,1,0:T(8,128)(2,1)S(1)} %get-tuple-element.46), channel_id=1, source_target_pairs={{0,8},{1,11},{2,10},{3,9},{4,12},{5,15},{6,14},{7,13},{8,0},{9,3},... | collective-permute-start | bytes 221192 | tf_op jit(solution)/shard_map/ppermute | solution.py:252
  7.5 8.1 %collective-permute-start.3 = (bf16[9,32,128]{2,1,0:T(8,128)(2,1)S(1)}, bf16[9,32,128]{2,1,0:T(8,128)(2,1)S(1)}, u32[]{:S(2)}, u32[]{:S(2)}) collective-permute-start(bf16[9,32,128]{2,1,0:T(8,128)(2,1)S(1)} %get-tuple-element.47), channel_id=1, source_target_pairs={{0,4},{1,7},{2,6},{3,5},{4,0},{5,3},{6,2},{7,1},{8,12},{9,15},{10,... | collective-permute-start | bytes 221192 | tf_op jit(solution)/shard_map/ppermute | solution.py:252
  8.1 4.4 %collective-permute-start.4 = (bf16[1,32,128]{2,1,0:T(8,128)(2,1)S(1)}, bf16[1,32,128]{2,1,0:T(8,128)(2,1)S(1)}, u32[]{:S(2)}, u32[]{:S(2)}) collective-permute-start(bf16[1,32,128]{2,1,0:T(8,128)(2,1)S(1)} %get-tuple-element.48), channel_id=1, source_target_pairs={{0,2},{1,3},{2,0},{3,1},{4,6},{5,7},{6,4},{7,5},{8,10},{9,11},{10,... | collective-permute-start | bytes 24584 | tf_op jit(solution)/shard_map/ppermute | solution.py:252
  10.3 8.7 %collective-permute-start.7 = (bf16[8,32,128]{2,1,0:T(8,128)(2,1)S(1)}, bf16[8,32,128]{2,1,0:T(8,128)(2,1)S(1)}, u32[]{:S(2)}, u32[]{:S(2)}) collective-permute-start(bf16[8,32,128]{2,1,0:T(8,128)(2,1)S(1)} %get-tuple-element.56), channel_id=1, source_target_pairs={{0,8},{1,11},{2,10},{3,9},{4,12},{5,15},{6,14},{7,13},{8,0},{9,3},... | collective-permute-start | bytes 196616 | tf_op jit(solution)/shard_map/ppermute | solution.py:252
  12.5 6.7 %collective-permute-start.9 = (bf16[8,32,128]{2,1,0:T(8,128)(2,1)S(1)}, bf16[8,32,128]{2,1,0:T(8,128)(2,1)S(1)}, u32[]{:S(2)}, u32[]{:S(2)}) collective-permute-start(bf16[8,32,128]{2,1,0:T(8,128)(2,1)S(1)} %get-tuple-element.59), channel_id=1, source_target_pairs={{0,12},{1,15},{2,14},{3,13},{4,8},{5,11},{6,10},{7,9},{8,4},{9,7},... | collective-permute-start | bytes 196616 | tf_op jit(solution)/shard_map/ppermute | solution.py:252
  15.6 1.2 %collective-permute-start.5 = (s32[4,128]{1,0:T(4,128)S(1)}, s32[4,128]{1,0:T(4,128)S(1)}, u32[]{:S(2)}, u32[]{:S(2)}) collective-permute-start(s32[4,128]{1,0:T(4,128)S(1)} %counts.1.counts_ref), channel_id=1, source_target_pairs={{0,1},{1,0},{2,3},{3,2},{4,5},{5,4},{6,7},{7,6},{8,9},{9,8},{10,11... | collective-permute-start | bytes 6152 | tf_op jit(solution)/shard_map/ppermute | solution.py:245
  17.3 8.3 %collective-permute-start.11 = (bf16[2,9,32,128]{3,2,1,0:T(8,128)(2,1)S(1)}, bf16[2,9,32,128]{3,2,1,0:T(8,128)(2,1)S(1)}, u32[]{:S(2)}, u32[]{:S(2)}) collective-permute-start(bf16[2,9,32,128]{3,2,1,0:T(8,128)(2,1)S(1)} %get-tuple-element.61), channel_id=1, source_target_pairs={{0,4},{1,7},{2,6},{3,5},{4,0},{5,3},{6,2},{7,1},{8,12},{9,15},{10,... | collective-permute-start | bytes 442376 | tf_op jit(solution)/shard_map/ppermute | solution.py:252
  17.5 8.2 %collective-permute-start.12 = (bf16[12,32,128]{2,1,0:T(8,128)(2,1)S(1)}, bf16[12,32,128]{2,1,0:T(8,128)(2,1)S(1)}, u32[]{:S(2)}, u32[]{:S(2)}) collective-permute-start(bf16[12,32,128]{2,1,0:T(8,128)(2,1)S(1)} %get-tuple-element.62), channel_id=1, source_target_pairs={{0,2},{1,3},{2,0},{3,1},{4,6},{5,7},{6,4},{7,5},{8,10},{9,11},{10,... | collective-permute-start | bytes 294920 | tf_op jit(solution)/shard_map/ppermute | solution.py:252
  19.2 11.0 %collective-permute-start.10 = (bf16[2,6,32,128]{3,2,1,0:T(8,128)(2,1)S(1)}, bf16[2,6,32,128]{3,2,1,0:T(8,128)(2,1)S(1)}, u32[]{:S(2)}, u32[]{:S(2)}) collective-permute-start(bf16[2,6,32,128]{3,2,1,0:T(8,128)(2,1)S(1)} %get-tuple-element.60), channel_id=1, source_target_pairs={{0,8},{1,11},{2,10},{3,9},{4,12},{5,15},{6,14},{7,13},{8,0},{9,3},... | collective-permute-start | bytes 294920 | tf_op jit(solution)/shard_map/ppermute | solution.py:252
  22.4 7.8 %collective-permute-start.8 = (bf16[2,6,32,128]{3,2,1,0:T(8,128)(2,1)S(1)}, bf16[2,6,32,128]{3,2,1,0:T(8,128)(2,1)S(1)}, u32[]{:S(2)}, u32[]{:S(2)}) collective-permute-start(bf16[2,6,32,128]{3,2,1,0:T(8,128)(2,1)S(1)} %get-tuple-element.57), channel_id=1, source_target_pairs={{0,12},{1,15},{2,14},{3,13},{4,8},{5,11},{6,10},{7,9},{8,4},{9,7},... | collective-permute-start | bytes 294920 | tf_op jit(solution)/shard_map/ppermute | solution.py:252
  30.2 1.7 %collective-permute-start.13 = (bf16[41,32,128]{2,1,0:T(8,128)(2,1)S(1)}, bf16[41,32,128]{2,1,0:T(8,128)(2,1)S(1)}, u32[]{:S(2)}, u32[]{:S(2)}) collective-permute-start(bf16[41,32,128]{2,1,0:T(8,128)(2,1)S(1)} %cross.1), channel_id=1, source_target_pairs={{0,1},{1,0},{2,3},{3,2},{4,5},{5,4},{6,7},{7,6},{8,9},{9,8},{10,11... | collective-permute-start | bytes 1007624 | tf_op jit(solution)/shard_map/ppermute | solution.py:245
